TPU v7x, 128 devices: a whole 4x4x4 slice. The times are simulated.
128 devices in a mesh: dp: 16 (over x, z_hi, core), tensor: 8 (over y, z_lo).
Axes of the slice: x: 4, y: 4, z: 4 (z_hi: 2, z_lo: 2; z = z_hi * 2 + z_lo), core: 2. Of those that a mesh axis runs over, the one named last changes fastest.
Arguments:
- tokens: bfloat16 [32768, 1024], P(('dp', 'tensor')), may hold values from -6 to 6
- cotangent: bfloat16 [32768, 1024], P(('dp', 'tensor')), may hold values from -6 to 6
- destination: int32 [32768], P(('dp', 'tensor')), may hold values from 0 to 32767, as said below
- variate_ids: int32 [32768], P(('dp', 'tensor')), may hold values from 0 to 7
- time_ids: int32 [32768], P(('dp', 'tensor')), may hold values from 0 to 511
- seq_lengths: int32 [16, 4], P('dp'), may hold values from 1 to 2048, as said below
- qkv_weight: bfloat16 [3, 1024, 1024], P(None, 'dp', 'tensor'), may hold values from -0.1875 to 0.1875
- out_weight: bfloat16 [1024, 1024], P('tensor', 'dp'), may hold values from -4 to 4
- gate_up_weight: bfloat16 [2, 1024, 4096], P(None, 'dp', 'tensor'), may hold values from -0.1875 to 0.1875
- down_weight: bfloat16 [4096, 1024], P('tensor', 'dp'), may hold values from -0.09375 to 0.09375
- norm_gains: bfloat16 [2, 1024], P(None, 'dp'), may hold values from 0.5 to 1.5
- qk_gains: float32 [2, 64], replicated, may hold values from 0.5 to 1.5
- variate_bias: float32 [2, 16], P(None, 'tensor'), may hold values from -3 to 3
Outputs:
- mixed: bfloat16 [32768, 1024], P(('dp', 'tensor'))
- input_grad: bfloat16 [32768, 1024], P(('dp', 'tensor'))
- qkv_grad: float32 [3, 1024, 1024], P(None, 'dp', 'tensor')
- out_grad: float32 [1024, 1024], P('tensor', 'dp')
- gate_up_grad: float32 [2, 1024, 4096], P(None, 'dp', 'tensor')
- down_grad: float32 [4096, 1024], P('tensor', 'dp')
- gains_grad: float32 [2, 1024], P(None, 'dp')
- qk_gains_grad: float32 [2, 64], replicated
- bias_grad: float32 [2, 16], P(None, 'tensor')
Inputs may be any that keep to these rules, and one draw needn't show every extreme that they name: `destination`: a permutation of the 32768 rows; among the 256 input rows of each device exactly 2 go to each aligned block of 256 rows of the group order. `seq_lengths`: each row sums to 2048; in each group one sequence, at a place drawn from the seed, holds more than 1792 tokens.
All inputs are finite; a program needn't handle non-finite values.
Results may differ from a plain program's by a relative error of at most 0.028.
Values may be sent and summed in bfloat16 or wider, within the bound.
No kernel may reach another device: no remote copies, remote signals or barrier semaphores. Data moves between devices by JAX's collectives and lax.ppermute only.
A program may use at most 128 MiB of HBM per device.

v0:
```python
import jax
import jax.numpy as jnp
from jax import lax
from jax.sharding import PartitionSpec as P

HEADS = 16
HEAD_DIM = 64
QBLOCK = 512


EPS = 1e-06
THETA = 10000.0
MASKED = -1e30


def root_stats(values):
    return lax.rsqrt(jnp.mean(values * values, axis=-1, keepdims=True) + EPS)


def norm_back(grad_in, normed, scale_inv):
    return scale_inv * (grad_in - normed * jnp.mean(grad_in * normed, axis=-1, keepdims=True))


def rotary(time_rows):
    half_dim = HEAD_DIM // 2
    steps_up = jnp.arange(half_dim).astype(jnp.float32)
    inverse = THETA ** (-2.0 * steps_up / HEAD_DIM)
    angles = time_rows.astype(jnp.float32)[:, None] * inverse[None, :]
    return (jnp.cos(angles)[:, None, :], jnp.sin(angles)[:, None, :])


def turn(values, cosine, sine):
    half_dim = values.shape[-1] // 2
    first_half = values[..., :half_dim]
    second_half = values[..., half_dim:]
    return jnp.concatenate(
        [first_half * cosine - second_half * sine, first_half * sine + second_half * cosine],
        axis=-1,
    )


def turn_back(grads, cosine, sine):
    half_dim = grads.shape[-1] // 2
    upper_half = grads[..., :half_dim]
    lower_half = grads[..., half_dim:]
    return jnp.concatenate(
        [upper_half * cosine + lower_half * sine, lower_half * cosine - upper_half * sine], axis=-1
    )


def block_scores(query_rows, seg_rows, var_rows, key_rows, segments, variates, bias_pair):
    raw_scores = jnp.einsum(
        "bhd,khd->hbk", query_rows, key_rows, preferred_element_type=jnp.float32
    )
    same_var = var_rows[:, None] == variates[None, :]
    scores = raw_scores + jnp.where(
        same_var[None], bias_pair[0][:, None, None], bias_pair[1][:, None, None]
    )
    inside = (seg_rows[:, None] == segments[None, :])[None]
    return (jnp.where(inside, scores, MASKED), same_var)


def body(
    tokens,
    cotangent,
    destination,
    variate_ids,
    time_ids,
    seq_lengths,
    qkv_weight,
    out_weight,
    gate_up_weight,
    down_weight,
    norm_gains,
    qk_gains,
    variate_bias,
):
    local_rows = tokens.shape[0]
    groups_count = lax.axis_size("dp")
    width_count = lax.axis_size("tensor")
    device_count = groups_count * width_count
    group_rows = local_rows * width_count
    each_rows = local_rows // device_count
    per_group = local_rows // groups_count
    tensor_place = lax.axis_index("tensor")
    sort_order = jnp.argsort(destination, stable=True)

    def spread(values):
        picked = values[sort_order].reshape(groups_count, 1, per_group)
        return jnp.broadcast_to(picked, (groups_count, width_count, per_group)).reshape(-1)

    got_dest, got_variate, got_time = (
        lax.all_to_all(
            spread(destination), ("dp", "tensor"), split_axis=0, concat_axis=0, tiled=True
        ),
        lax.all_to_all(
            spread(variate_ids), ("dp", "tensor"), split_axis=0, concat_axis=0, tiled=True
        ),
        lax.all_to_all(spread(time_ids), ("dp", "tensor"), split_axis=0, concat_axis=0, tiled=True),
    )
    arrived, arrived_grad = (
        lax.all_to_all(
            tokens[sort_order], ("dp", "tensor"), split_axis=0, concat_axis=0, tiled=True
        ),
        lax.all_to_all(
            cotangent[sort_order], ("dp", "tensor"), split_axis=0, concat_axis=0, tiled=True
        ),
    )
    group_order = jnp.argsort(got_dest % group_rows)
    variates = got_variate[group_order]
    time_rows = got_time[group_order]
    mine_dest = lax.dynamic_index_in_dim(
        got_dest.reshape(device_count, width_count, each_rows), tensor_place, axis=1, keepdims=False
    ).reshape(-1)
    mine_slot = mine_dest % local_rows
    mine_order = jnp.argsort(mine_slot)
    inputs = arrived[mine_order].astype(jnp.float32)
    out_grad_rows = arrived_grad[mine_order]
    ends = jnp.cumsum(seq_lengths[0])
    positions = jnp.arange(group_rows)
    segments = jnp.sum((positions[:, None] >= ends[None, :]).astype(jnp.int32), axis=1)
    w_qkv, w_out, w_gate_up, w_down, gathered_gains = (
        lax.all_gather(qkv_weight, "dp", axis=1, tiled=True),
        lax.all_gather(out_weight, "dp", axis=1, tiled=True),
        lax.all_gather(gate_up_weight, "dp", axis=1, tiled=True),
        lax.all_gather(down_weight, "dp", axis=1, tiled=True),
        lax.all_gather(norm_gains, "dp", axis=1, tiled=True),
    )
    gain_one = gathered_gains[0].astype(jnp.float32)
    gain_two = gathered_gains[1].astype(jnp.float32)
    head_count = w_qkv.shape[2] // HEAD_DIM
    scale_one = root_stats(inputs)
    normed_one = inputs * scale_one
    attn_in, grad_all = (
        lax.all_gather((normed_one * gain_one).astype(jnp.bfloat16), "tensor", axis=0, tiled=True),
        lax.all_gather(out_grad_rows, "tensor", axis=0, tiled=True),
    )
    projected = jnp.einsum("gd,kde->kge", attn_in, w_qkv, preferred_element_type=jnp.float32)
    query_raw = projected[0].reshape(group_rows, head_count, HEAD_DIM)
    key_raw = projected[1].reshape(group_rows, head_count, HEAD_DIM)
    query_inv = root_stats(query_raw)
    query_unit = query_raw * query_inv
    key_inv = root_stats(key_raw)
    key_unit = key_raw * key_inv
    cosine, sine = rotary(time_rows)
    query_rot = (turn(query_unit * qk_gains[0], cosine, sine) * HEAD_DIM ** (-0.5)).astype(
        jnp.bfloat16
    )
    key_rot = turn(key_unit * qk_gains[1], cosine, sine).astype(jnp.bfloat16)
    value_rot = projected[2].astype(jnp.bfloat16).reshape(group_rows, head_count, HEAD_DIM)
    block_count = group_rows // QBLOCK
    offsets = jnp.arange(block_count) * QBLOCK

    def forward_block(offset):
        query_rows = lax.dynamic_slice_in_dim(query_rot, offset, QBLOCK, 0)
        seg_rows = lax.dynamic_slice_in_dim(segments, offset, QBLOCK, 0)
        var_rows = lax.dynamic_slice_in_dim(variates, offset, QBLOCK, 0)
        scores, same_var = block_scores(
            query_rows, seg_rows, var_rows, key_rot, segments, variates, variate_bias
        )
        row_top = jnp.max(scores, axis=-1, keepdims=True)
        exp_scores = jnp.exp(scores - row_top)
        row_total = jnp.sum(exp_scores, axis=-1, keepdims=True)
        probs = (exp_scores / row_total).astype(jnp.bfloat16)
        attended = jnp.einsum("hbk,khd->bhd", probs, value_rot, preferred_element_type=jnp.float32)
        return (attended, (row_top + jnp.log(row_total))[..., 0])

    attended, log_totals = lax.map(forward_block, offsets)
    attn_rows = attended.reshape(group_rows, head_count * HEAD_DIM).astype(jnp.bfloat16)
    hidden_one = inputs + lax.psum_scatter(
        jnp.dot(attn_rows, w_out, preferred_element_type=jnp.float32).astype(jnp.bfloat16),
        "tensor",
        scatter_dimension=0,
        tiled=True,
    ).astype(jnp.float32)
    scale_two = root_stats(hidden_one)
    normed_two = hidden_one * scale_two
    ffn_in = lax.all_gather(
        (normed_two * gain_two).astype(jnp.bfloat16), "tensor", axis=0, tiled=True
    )
    gate_up = jnp.einsum("gd,kdf->kgf", ffn_in, w_gate_up, preferred_element_type=jnp.float32)
    gate_rows = gate_up[0]
    up_rows = gate_up[1]
    hidden = (jax.nn.silu(gate_rows) * up_rows).astype(jnp.bfloat16)
    mixed = hidden_one + lax.psum_scatter(
        jnp.dot(hidden, w_down, preferred_element_type=jnp.float32).astype(jnp.bfloat16),
        "tensor",
        scatter_dimension=0,
        tiled=True,
    ).astype(jnp.float32)
    grad_hidden = jnp.einsum("gd,fd->gf", grad_all, w_down, preferred_element_type=jnp.float32)
    down_grad = jnp.einsum("gf,gd->fd", hidden, grad_all, preferred_element_type=jnp.float32)
    sigmoid_gate = jax.nn.sigmoid(gate_rows)
    grad_gate = (
        grad_hidden * up_rows * (sigmoid_gate * (1.0 + gate_rows * (1.0 - sigmoid_gate)))
    ).astype(jnp.bfloat16)
    grad_up = (grad_hidden * jax.nn.silu(gate_rows)).astype(jnp.bfloat16)
    grad_pair = jnp.stack([grad_gate, grad_up])
    gate_up_grad = jnp.einsum("gd,kgf->kdf", ffn_in, grad_pair, preferred_element_type=jnp.float32)
    gate_up_part, down_part = (gate_up_grad, down_grad)
    rows_now = grad_pair
    grad_normed_two = lax.psum_scatter(
        jnp.einsum("kgf,kdf->gd", rows_now, w_gate_up, preferred_element_type=jnp.float32).astype(
            jnp.bfloat16
        ),
        "tensor",
        scatter_dimension=0,
        tiled=True,
    ).astype(jnp.float32)
    gain_two_grad = jnp.sum(grad_normed_two * normed_two, axis=0)
    grad_one = out_grad_rows.astype(jnp.float32) + norm_back(
        grad_normed_two * gain_two, normed_two, scale_two
    )
    grad_one_all = lax.all_gather(grad_one.astype(jnp.bfloat16), "tensor", axis=0, tiled=True)
    grad_attn = (
        jnp.einsum("gd,ed->ge", grad_one_all, w_out, preferred_element_type=jnp.float32)
        .astype(jnp.bfloat16)
        .reshape(group_rows, head_count, HEAD_DIM)
    )
    out_grad = jnp.einsum("ge,gd->ed", attn_rows, grad_one_all, preferred_element_type=jnp.float32)
    zero_keys = jnp.zeros((group_rows, head_count, HEAD_DIM), jnp.float32)

    def backward_block(running, block_in):
        key_acc, value_acc, bias_acc = running
        offset, log_total = block_in
        query_rows = lax.dynamic_slice_in_dim(query_rot, offset, QBLOCK, 0)
        seg_rows = lax.dynamic_slice_in_dim(segments, offset, QBLOCK, 0)
        var_rows = lax.dynamic_slice_in_dim(variates, offset, QBLOCK, 0)
        grad_block = lax.dynamic_slice_in_dim(grad_attn, offset, QBLOCK, 0)
        scores, same_var = block_scores(
            query_rows, seg_rows, var_rows, key_rot, segments, variates, variate_bias
        )
        probs = jnp.exp(scores - log_total[..., None])
        grad_probs = jnp.einsum(
            "bhd,khd->hbk", grad_block, value_rot, preferred_element_type=jnp.float32
        )
        value_acc = value_acc + jnp.einsum(
            "hbk,bhd->khd",
            probs.astype(jnp.bfloat16),
            grad_block,
            preferred_element_type=jnp.float32,
        )
        grad_scores = probs * (grad_probs - jnp.sum(probs * grad_probs, axis=-1, keepdims=True))
        low_scores = grad_scores.astype(jnp.bfloat16)
        grad_query = jnp.einsum(
            "hbk,khd->bhd", low_scores, key_rot, preferred_element_type=jnp.float32
        )
        key_acc = key_acc + jnp.einsum(
            "hbk,bhd->khd", low_scores, query_rows, preferred_element_type=jnp.float32
        )
        same_sum = jnp.sum(jnp.where(same_var[None], grad_scores, 0.0), axis=(1, 2))
        other_sum = jnp.sum(jnp.where(same_var[None], 0.0, grad_scores), axis=(1, 2))
        bias_acc = bias_acc + jnp.stack([same_sum, other_sum])
        return ((key_acc, value_acc, bias_acc), grad_query)

    (grad_key, grad_value, bias_part), grad_query = lax.scan(
        backward_block,
        (zero_keys, zero_keys, jnp.zeros((2, head_count), jnp.float32)),
        (offsets, log_totals),
    )
    grad_query = grad_query.reshape(group_rows, head_count, HEAD_DIM)
    grad_q_unit = turn_back(grad_query * HEAD_DIM ** (-0.5), cosine, sine)
    grad_k_unit = turn_back(grad_key, cosine, sine)
    query_gain_grad = jnp.sum(grad_q_unit * query_unit, axis=(0, 1))
    key_gain_grad = jnp.sum(grad_k_unit * key_unit, axis=(0, 1))
    grad_q_raw = norm_back(grad_q_unit * qk_gains[0], query_unit, query_inv)
    grad_k_raw = norm_back(grad_k_unit * qk_gains[1], key_unit, key_inv)
    grad_proj = jnp.stack(
        [
            grad_q_raw.reshape(group_rows, -1),
            grad_k_raw.reshape(group_rows, -1),
            grad_value.reshape(group_rows, -1),
        ]
    ).astype(jnp.bfloat16)
    qkv_grad = jnp.einsum("gd,kge->kde", attn_in, grad_proj, preferred_element_type=jnp.float32)
    rows_now = grad_proj
    grad_normed_one = lax.psum_scatter(
        jnp.einsum("kge,kde->gd", rows_now, w_qkv, preferred_element_type=jnp.float32).astype(
            jnp.bfloat16
        ),
        "tensor",
        scatter_dimension=0,
        tiled=True,
    ).astype(jnp.float32)
    gain_one_grad = jnp.sum(grad_normed_one * normed_one, axis=0)
    input_grad = grad_one + norm_back(grad_normed_one * gain_one, normed_one, scale_one)
    qkv_part, out_part, gate_up_part, down_part = (
        lax.psum_scatter(
            qkv_grad.astype(jnp.bfloat16), "dp", scatter_dimension=1, tiled=True
        ).astype(jnp.float32),
        lax.psum_scatter(
            out_grad.astype(jnp.bfloat16), "dp", scatter_dimension=1, tiled=True
        ).astype(jnp.float32),
        lax.psum_scatter(
            gate_up_part.astype(jnp.bfloat16), "dp", scatter_dimension=1, tiled=True
        ).astype(jnp.float32),
        lax.psum_scatter(
            down_part.astype(jnp.bfloat16), "dp", scatter_dimension=1, tiled=True
        ).astype(jnp.float32),
    )
    bias_full = lax.dynamic_update_slice(
        jnp.zeros((2, HEADS), jnp.float32), bias_part, (jnp.int32(0), tensor_place * head_count)
    )
    gain_sums, qk_sums, bias_sums = lax.psum(
        (
            jnp.stack([gain_one_grad, gain_two_grad]),
            jnp.stack([query_gain_grad, key_gain_grad]),
            bias_full,
        ),
        ("dp", "tensor"),
    )
    shard_width = norm_gains.shape[1]
    gains_grad = lax.dynamic_slice_in_dim(
        gain_sums, lax.axis_index("dp") * shard_width, shard_width, 1
    )
    bias_grad = lax.dynamic_slice_in_dim(bias_sums, tensor_place * head_count, head_count, 1)
    back_rows, back_grads = (
        lax.all_to_all(
            mixed.astype(jnp.bfloat16)[mine_slot],
            ("dp", "tensor"),
            split_axis=0,
            concat_axis=0,
            tiled=True,
        ),
        lax.all_to_all(
            input_grad.astype(jnp.bfloat16)[mine_slot],
            ("dp", "tensor"),
            split_axis=0,
            concat_axis=0,
            tiled=True,
        ),
    )
    undo_order = jnp.argsort(sort_order)
    return (
        back_rows[undo_order],
        back_grads[undo_order],
        qkv_part,
        out_part,
        gate_up_part,
        down_part,
        gains_grad,
        qk_sums,
        bias_grad,
    )


def solution(mesh):
    in_specs = (
        P(("dp", "tensor"), None),
        P(("dp", "tensor"), None),
        P(("dp", "tensor")),
        P(("dp", "tensor")),
        P(("dp", "tensor")),
        P("dp", None),
        P(None, "dp", "tensor"),
        P("tensor", "dp"),
        P(None, "dp", "tensor"),
        P("tensor", "dp"),
        P(None, "dp"),
        P(),
        P(None, "tensor"),
    )
    out_specs = (
        P(("dp", "tensor"), None),
        P(("dp", "tensor"), None),
        P(None, "dp", "tensor"),
        P("tensor", "dp"),
        P(None, "dp", "tensor"),
        P("tensor", "dp"),
        P(None, "dp"),
        P(),
        P(None, "tensor"),
    )
    return jax.shard_map(body, mesh=mesh, in_specs=in_specs, out_specs=out_specs, check_vma=False)
```

profile of v0, /device:TPU:0, one launch (start us, length us, event | category | flops | bytes accessed | tf_op | source)
XLA Modules:
  0.0 1357.1 jit_solution(11727827310148908205)
XLA Ops:
  15.2 11.1 all-to-all-start.1
  26.3 24.0 %all-gather.1 = bf16[16,64,2]{1,2,0:T(2,128)(2,1)S(1)} all-gather(bf16[1,64,2]{1,2,0:T(2,128)(2,1)} %bitcast.291), channel_id=1, replica_groups=mesh['dp'=16,'tensor'=8] {'dp'}, dimensions={0}, use_global_device_ids=true | all-gather | bytes 4352 | tf_op jit(solution)/shard_map/all_gather | solution.py:127
  52.6 5.3 all-to-all-start
  61.6 9.9 all-to-all-done
  76.9 4.7 all-to-all-start.3
  81.8 26.4 %all_gather.30 = bf16[128,1024]{0,1:T(8,128)(2,1)S(1)} all-gather(bf16[128,64]{0,1:T(8,128)(2,1)S(1)} %copy-done.43), channel_id=1, replica_groups=mesh['dp'=16,'tensor'=8] {'dp'}, dimensions={1}, use_global_device_ids=true | all-gather | bytes 278528 | tf_op jit(solution)/shard_map/all_gather | solution.py:124
  108.4 36.1 %all_gather.29 = bf16[3,1024,128]{2,1,0:T(8,128)(2,1)} all-gather(bf16[3,64,128]{2,1,0:T(8,128)(2,1)S(1)} %copy-done.41), channel_id=1, replica_groups=mesh['dp'=16,'tensor'=8] {'dp'}, dimensions={1}, use_global_device_ids=true | all-gather | bytes 835584 | tf_op jit(solution)/shard_map/all_gather | solution.py:123
  147.1 10.4 all-to-all-start.2
  159.2 7.6 all-to-all-done.2
  168.6 5.0 sort.67
  173.6 11.8 gather_fusion.6
  185.4 11.8 gather_fusion.4
  198.2 4.4 fusion.44
  205.1 56.6 %while.31 = (s32[]{:T(128)}, bf16[4,512,2,64]{1,3,2,0:T(8,128)(2,1)S(1)}, f32[4,2,512]{2,1,0:T(2,128)S(1)}, s32[4]{0:T(128)S(1)}, s32[2048]{0:T(1024)S(1)}, /*in...) while((s32[]{:T(128)}, ...), condition=%wide.region_11.12_spmd.clone, body=%wide.region_8.11_spmd.sunk.clone | while | flops 570424320 | bytes 35059932 | solution.py:168
  267.0 93.6 %reduce-scatter.7.cloned.1.call-done = bf16[256,1024]{1,0:T(8,128)(2,1)} async-done(((bf16[2048,1024]{1,0:T(8,128)(2,1)}), bf16[256,1024]{1,0:T(8,128)(2,1)}) %reduce-scatter.7.cloned.1.call-update) | async-done | bytes 524304 | tf_op jit(solution)/shard_map/reduce_scatter | solution.py:170
  366.0 23.4 %all_to_all.84 = bf16[128,2,1024]{2,1,0:T(2,128)(2,1)S(1)} all-to-all(bf16[128,2,1024]{2,1,0:T(2,128)(2,1)S(1)} %all_to_all.71), channel_id=1, replica_groups=mesh['dp'=16,'tensor'=8] {'dp','tensor'}, dimensions={0} | all-to-all | bytes 1048576 | tf_op jit(solution)/shard_map/all_to_all | solution.py:105
  392.1 68.3 %all-gather.11.cloned.1.call-done = bf16[2048,1024]{1,0:T(8,128)(2,1)} async-done(((bf16[256,1024]{1,0:T(8,128)(2,1)}), bf16[2048,1024]{1,0:T(8,128)(2,1)}) %all-gather.11.cloned.1.call-update) | async-done | bytes 4194320 | tf_op jit(solution)/shard_map/all_gather | solution.py:178
  460.4 10.6 convolution_bitcast_fusion.1
  471.1 39.1 %all-gather.15.cloned.1.call-done = bf16[512,1024]{0,1:T(8,128)(2,1)} async-done(((bf16[512,64]{0,1:T(8,128)(2,1)}), bf16[512,1024]{0,1:T(8,128)(2,1)}) %all-gather.15.cloned.1.call-update) | async-done | bytes 1048592 | tf_op jit(solution)/shard_map/all_gather | solution.py:126
  510.2 90.0 %all-gather.19.cloned.1.call-done = bf16[2048,1024]{1,0:T(8,128)(2,1)} async-done(((bf16[256,1024]{1,0:T(8,128)(2,1)}), bf16[2048,1024]{1,0:T(8,128)(2,1)}) %all-gather.19.cloned.1.call-update) | async-done | bytes 4194320 | tf_op jit(solution)/shard_map/all_gather | solution.py:136
  600.2 10.3 fusion.48
  612.5 6.3 bitcast_convert_fusion.1
  618.9 92.1 %reduce-scatter.11.cloned.1.call-done = bf16[256,1024]{1,0:T(8,128)(2,1)} async-done(((bf16[2048,1024]{1,0:T(8,128)(2,1)}), bf16[256,1024]{1,0:T(8,128)(2,1)}) %reduce-scatter.11.cloned.1.call-update) | async-done | bytes 524304 | tf_op jit(solution)/shard_map/reduce_scatter | solution.py:202
  715.8 90.5 %all-gather.17.cloned.1.call-done = bf16[2048,1024]{1,0:T(8,128)(2,1)} async-done(((bf16[256,1024]{1,0:T(8,128)(2,1)}), bf16[2048,1024]{1,0:T(8,128)(2,1)}) %all-gather.17.cloned.1.call-update) | async-done | bytes 4194320 | tf_op jit(solution)/shard_map/all_gather | solution.py:214
  806.3 4.5 convolution_convert_fusion.2
  810.8 90.6 %while.32 = (s32[]{:T(128)}, f32[2048,2,64]{0,2,1:T(8,128)S(1)}, f32[2048,2,64]{0,2,1:T(8,128)S(1)}, f32[2,2]{1,0:T(2,128)S(1)}, f32[4,512,2,64]{1,3,2,0:T(8,128...) while((s32[]{:T(128)}, f32[2048,2,64]{0,2,1:T(8,128)S(1)}, ...), condition=%wide.region_22.23_spmd.clone.clone, body=%wide.region_18.22_spmd.clone.sunk.clone | while | flops 1374682112 | bytes 76857704 | solution.py:256
  817.3 5.2 multiply_reduce_fusion.8
  822.4 5.0 select_reduce_fusion.4
  839.9 5.2 multiply_reduce_fusion.8
  845.0 5.0 select_reduce_fusion.4
  862.5 5.2 multiply_reduce_fusion.8
  867.6 5.0 select_reduce_fusion.4
  885.0 5.1 multiply_reduce_fusion.8
  890.2 5.0 select_reduce_fusion.4
  906.9 4.4 bitcast_convert_fusion
  912.6 5.9 convolution_convert_fusion
  920.1 5.8 convolution_convert_fusion.3
  926.4 8.1 convert_bitcast_fusion
  934.5 4.1 copy.69
  938.6 4.7 convolution_convert_fusion.4
  943.5 4.9 fusion.58
  951.1 54.9 %reduce-scatter.13.cloned.1.call-done = bf16[256,1024]{1,0:T(8,128)(2,1)} async-done(((bf16[2048,1024]{1,0:T(8,128)(2,1)}), bf16[256,1024]{1,0:T(8,128)(2,1)}) %reduce-scatter.13.cloned.1.call-update) | async-done | bytes 524304 | tf_op jit(solution)/shard_map/reduce_scatter | solution.py:277
  1007.5 102.9 %reduce-scatter.9.cloned.1.call-done = bf16[256,1024]{1,0:T(8,128)(2,1)} async-done(((bf16[2048,1024]{1,0:T(8,128)(2,1)}), bf16[256,1024]{1,0:T(8,128)(2,1)}) %reduce-scatter.9.cloned.1.call-update) | async-done | bytes 524304 | tf_op jit(solution)/shard_map/reduce_scatter | solution.py:185
  1114.6 19.7 %all-to-all-start.6 = ((bf16[128,2,1024]{2,1,0:T(2,128)(2,1)}), bf16[128,2,1024]{2,1,0:T(2,128)(2,1)S(1)}, u32[]{:S(2)}, u32[]{:S(2)}) async-start(bf16[128,2,1024]{2,1,0:T(2,128)(2,1)} %all_to_all.74), calls=%async_computation.10 | async-start | bytes 1048576 | tf_op jit(solution)/shard_map/all_to_all | solution.py:325
  1138.7 55.3 %reduce-scatter.17.cloned.1.call-done = bf16[512,64]{0,1:T(8,128)(2,1)} async-done(((bf16[512,1024]{0,1:T(8,128)(2,1)}), bf16[512,64]{0,1:T(8,128)(2,1)}) %reduce-scatter.17.cloned.1.call-update) | async-done | bytes 65552 | tf_op jit(solution)/shard_map/reduce_scatter | solution.py:297
  1196.0 66.2 %reduce-scatter.15.cloned.1.call-done = bf16[128,64]{0,1:T(8,128)(2,1)} async-done(((bf16[128,1024]{0,1:T(8,128)(2,1)}), bf16[128,64]{0,1:T(8,128)(2,1)}) %reduce-scatter.15.cloned.1.call-update) | async-done | bytes 16400 | tf_op jit(solution)/shard_map/reduce_scatter | solution.py:291
  1265.7 7.7 all-to-all-start.4
  1276.7 67.1 %all-reduce.2 = (f32[2,1024]{1,0:T(2,128)S(1)}, f32[2,64]{1,0:T(2,128)}, f32[2,16]{1,0:T(2,128)S(1)}) all-reduce(f32[2,1024]{1,0:T(2,128)S(1)} %pad_maximum_fusion.11, f32[2,64]{1,0:T(2,128)S(1)} %pad_maximum_fusion.12, f32[2,16]{1,0:T(2,128)S(1)} %dynamic_update_slice.14), channel_id=1, replica_groups=mesh['dp'=16,'tensor'=8] {'dp','tensor'}, use_global_device_ids=true, to_apply=%region_33.34 | all-reduce | flops 2208 | bytes 17664 | tf_op jit(solution)/shard_map/psum | solution.py:304
  (366 shorter events, 173.3 us)
Async XLA Ops:
  8.0 42.5 %copy-start = (bf16[256,1024]{1,0:T(8,128)(2,1)S(1)}, bf16[256,1024]{1,0:T(8,128)(2,1)}, u32[]{:S(2)}) copy-start(bf16[256,1024]{1,0:T(8,128)(2,1)} %param.17) | copy-start | bytes 1572868
  15.2 37.5 %all-to-all-start.1 = ((s32[128,16,1]{1,2,0:T(1,128)}), s32[128,16,1]{1,2,0:T(1,128)S(1)}, u32[]{:S(2)}, u32[]{:S(2)}) async-start(s32[128,16,1]{1,2,0:T(1,128)} %bitcast.8), calls=%async_computation.1 | async-start | bytes 131072 | tf_op jit(solution)/shard_map/all_to_all | solution.py:93
  50.5 22.7 %copy-start.39 = (f32[1,1024]{1,0:T(1,128)}, f32[1,1024]{1,0:T(1,128)S(1)}, u32[]{:S(2)}) copy-start(f32[1,1024]{1,0:T(1,128)S(1)} %get-tuple-element.343) | copy-start | bytes 12292
  52.6 18.9 %all-to-all-start = ((bf16[128,2,1024]{2,1,0:T(2,128)(2,1)}), bf16[128,2,1024]{2,1,0:T(2,128)(2,1)S(1)}, u32[]{:S(2)}, u32[]{:S(2)}) async-start(bf16[128,2,1024]{2,1,0:T(2,128)(2,1)} %all_to_all.56), calls=%async_computation | async-start | bytes 1048576 | tf_op jit(solution)/shard_map/all_to_all | solution.py:102
  58.0 16.2 %copy-start.2 = (s32[256]{0:T(256)S(1)}, s32[256]{0:T(256)}, u32[]{:S(2)}) copy-start(s32[256]{0:T(256)} %param.20) | copy-start | bytes 3076
  58.0 140.3 %all-gather.9.cloned.1.call-start = ((), (), s32[]{:S(2)}) async-start(), calls=%async_computation.13 | async-start | bytes 4718592 | tf_op jit(solution)/shard_map/all_gather | solution.py:135
  71.7 9.8 copy-start.55
  71.7 10.1 copy-start.43
  71.7 36.6 %copy-start.52 = (f32[2,64]{1,0:T(2,128)S(1)}, f32[2,64]{1,0:T(2,128)}, u32[]{:S(2)}) copy-start(f32[2,64]{1,0:T(2,128)} %param.28) | copy-start | bytes 1540
  71.8 36.6 %copy-start.41 = (bf16[3,64,128]{2,1,0:T(8,128)(2,1)S(1)}, bf16[3,64,128]{2,1,0:T(8,128)(2,1)}, u32[]{:S(2)}) copy-start(bf16[3,64,128]{2,1,0:T(8,128)(2,1)} %param.23) | copy-start | bytes 147460
  71.8 72.7 %copy-start.3 = (s32[256]{0:T(256)S(1)}, s32[256]{0:T(256)}, u32[]{:S(2)}) copy-start(s32[256]{0:T(256)} %param.21) | copy-start | bytes 3076
  73.1 112.3 %copy-start.44 = (f32[256]{0:T(256)}, f32[256]{0:T(256)S(1)}, u32[]{:S(2)}) copy-start(f32[256]{0:T(256)S(1)} %add_rsqrt_fusion.3) | copy-start | bytes 3076
  76.9 69.6 %all-to-all-start.3 = ((s32[128,16,1]{1,2,0:T(1,128)}), s32[128,16,1]{1,2,0:T(1,128)S(1)}, u32[]{:S(2)}, u32[]{:S(2)}) async-start(s32[128,16,1]{1,2,0:T(1,128)} %bitcast.23), calls=%async_computation.3 | async-start | bytes 131072 | tf_op jit(solution)/shard_map/all_to_all | solution.py:96
  108.4 94.8 %copy-start.46 = (f32[64]{0:T(128)}, f32[64]{0:T(128)S(1)}, u32[]{:S(2)}) copy-start(f32[64]{0:T(128)S(1)} %get-tuple-element.344) | copy-start | bytes 772
  108.4 96.0 %copy-start.48 = (f32[64]{0:T(128)}, f32[64]{0:T(128)S(1)}, u32[]{:S(2)}) copy-start(f32[64]{0:T(128)S(1)} %get-tuple-element.345) | copy-start | bytes 772
  147.1 19.6 %all-to-all-start.2 = ((s32[128,16,1]{1,2,0:T(1,128)}), s32[128,16,1]{1,2,0:T(1,128)S(1)}, u32[]{:S(2)}, u32[]{:S(2)}) async-start(s32[128,16,1]{1,2,0:T(1,128)} %bitcast.20), calls=%async_computation.2 | async-start | bytes 131072 | tf_op jit(solution)/shard_map/all_to_all | solution.py:99
  157.5 203.1 %reduce-scatter.7.cloned.1.call-start = ((), (), s32[]{:S(2)}) async-start(), calls=%async_computation.14 | async-start | bytes 4718592 | tf_op jit(solution)/shard_map/reduce_scatter | solution.py:170
  198.2 6.4 copy-start.21
  198.2 6.4 copy-start.23
  266.3 98.3 %copy-start.4 = (bf16[256,1024]{1,0:T(8,128)(2,1)S(1)}, bf16[256,1024]{1,0:T(8,128)(2,1)}, u32[]{:S(2)}) copy-start(bf16[256,1024]{1,0:T(8,128)(2,1)} %param.18) | copy-start | bytes 1572868
  266.3 125.8 %all-gather.13.cloned.1.call-start = ((), (), s32[]{:S(2)}) async-start(), calls=%async_computation.16 | async-start | bytes 2228224 | tf_op jit(solution)/shard_map/all_gather | solution.py:125
  266.9 193.5 %all-gather.11.cloned.1.call-start = ((), (), s32[]{:S(2)}) async-start(), calls=%async_computation.15 | async-start | bytes 4718592 | tf_op jit(solution)/shard_map/all_gather | solution.py:178
  364.0 146.2 %all-gather.15.cloned.1.call-start = ((), (), s32[]{:S(2)}) async-start(), calls=%async_computation.17 | async-start | bytes 1114112 | tf_op jit(solution)/shard_map/all_gather | solution.py:126
  364.6 235.6 %all-gather.19.cloned.1.call-start = ((), (), s32[]{:S(2)}) async-start(), calls=%async_computation.24 | async-start | bytes 4718592 | tf_op jit(solution)/shard_map/all_gather | solution.py:136
  391.6 319.4 %reduce-scatter.11.cloned.1.call-start = ((), (), s32[]{:S(2)}) async-start(), calls=%async_computation.19 | async-start | bytes 4718592 | tf_op jit(solution)/shard_map/reduce_scatter | solution.py:202
  471.0 141.5 %copy-start.53 = (bf16[2,1024,512]{2,1,0:T(8,128)(2,1)S(1)}, bf16[2,1024,512]{2,1,0:T(8,128)(2,1)}, u32[]{:S(2)}) copy-start(bf16[2,1024,512]{2,1,0:T(8,128)(2,1)} %all-gather.13.cloned.1.call-done) | copy-start | bytes 6291460
  618.9 92.2 %copy-start.11 = (bf16[256,1024]{1,0:T(8,128)(2,1)S(1)}, bf16[256,1024]{1,0:T(8,128)(2,1)}, u32[]{:S(2)}) copy-start(bf16[256,1024]{1,0:T(8,128)(2,1)} %reduce-scatter.7.cloned.1.call-done) | copy-start | bytes 1572868
  618.9 94.4 %copy-start.13 = (bf16[256,1024]{1,0:T(8,128)(2,1)S(1)}, bf16[256,1024]{1,0:T(8,128)(2,1)}, u32[]{:S(2)}) copy-start(bf16[256,1024]{1,0:T(8,128)(2,1)} %gather_fusion.10) | copy-start | bytes 1572868
  618.9 96.8 %copy-start.47 = (f32[64]{0:T(128)S(1)}, f32[64]{0:T(128)}, u32[]{:S(2)}) copy-start(f32[64]{0:T(128)} %copy-done.46) | copy-start | bytes 772
  618.9 96.9 %copy-start.49 = (f32[64]{0:T(128)S(1)}, f32[64]{0:T(128)}, u32[]{:S(2)}) copy-start(f32[64]{0:T(128)} %copy-done.48) | copy-start | bytes 772
  618.9 187.4 %all-gather.17.cloned.1.call-start = ((), (), s32[]{:S(2)}) async-start(), calls=%async_computation.20 | async-start | bytes 4718592 | tf_op jit(solution)/shard_map/all_gather | solution.py:214
  715.5 290.4 %reduce-scatter.13.cloned.1.call-start = ((), (), s32[]{:S(2)}) async-start(), calls=%async_computation.21 | async-start | bytes 4718592 | tf_op jit(solution)/shard_map/reduce_scatter | solution.py:277
  911.4 199.0 %reduce-scatter.9.cloned.1.call-start = ((), (), s32[]{:S(2)}) async-start(), calls=%async_computation.18 | async-start | bytes 4718592 | tf_op jit(solution)/shard_map/reduce_scatter | solution.py:185
  918.5 275.5 %reduce-scatter.17.cloned.1.call-start = ((), (), s32[]{:S(2)}) async-start(), calls=%async_computation.23 | async-start | bytes 1114112 | tf_op jit(solution)/shard_map/reduce_scatter | solution.py:297
  926.0 336.2 %reduce-scatter.15.cloned.1.call-start = ((), (), s32[]{:S(2)}) async-start(), calls=%async_computation.22 | async-start | bytes 278528 | tf_op jit(solution)/shard_map/reduce_scatter | solution.py:291
  938.6 4.8 copy-start.31
  938.6 4.9 copy-start.33
  943.4 330.0 %all-reduce.6.cloned.1.call-start = ((), (), s32[]{:S(2)}) async-start(), calls=%async_computation.25 | async-start | bytes 6291456
  948.4 57.6 %copy-start.40 = (f32[1,1024]{1,0:T(1,128)S(1)}, f32[1,1024]{1,0:T(1,128)}, u32[]{:S(2)}) copy-start(f32[1,1024]{1,0:T(1,128)} %copy-done.39) | copy-start | bytes 12292
  948.4 57.6 %copy-start.45 = (f32[256]{0:T(256)S(1)}, f32[256]{0:T(256)}, u32[]{:S(2)}) copy-start(f32[256]{0:T(256)} %copy-done.44) | copy-start | bytes 3076
  948.4 162.0 %copy-start.12 = (bf16[256,1024]{1,0:T(8,128)(2,1)S(1)}, bf16[256,1024]{1,0:T(8,128)(2,1)}, u32[]{:S(2)}) copy-start(bf16[256,1024]{1,0:T(8,128)(2,1)} %reduce-scatter.7.cloned.1.call-done) | copy-start | bytes 1572868
  948.4 162.0 %copy-start.14 = (bf16[256,1024]{1,0:T(8,128)(2,1)S(1)}, bf16[256,1024]{1,0:T(8,128)(2,1)}, u32[]{:S(2)}) copy-start(bf16[256,1024]{1,0:T(8,128)(2,1)} %gather_fusion.10) | copy-start | bytes 1572868
  948.4 162.0 %copy-start.19 = (bf16[256,1024]{1,0:T(8,128)(2,1)S(1)}, bf16[256,1024]{1,0:T(8,128)(2,1)}, u32[]{:S(2)}) copy-start(bf16[256,1024]{1,0:T(8,128)(2,1)} %reduce-scatter.11.cloned.1.call-done) | copy-start | bytes 1572868
  1112.4 21.9 %copy-start.51 = (s32[256]{0:T(256)S(1)}, s32[256]{0:T(256)}, u32[]{:S(2)}) copy-start(s32[256]{0:T(256)} %copy-done.50) | copy-start | bytes 3076
  1112.4 25.1 %copy-start.56 = (u32[128]{0:T(128)S(1)}, u32[128]{0:T(128)}, u32[]{:S(2)}) copy-start(u32[128]{0:T(128)} %constant.136) | copy-start | bytes 1540
  1114.6 151.1 %all-to-all-start.6 = ((bf16[128,2,1024]{2,1,0:T(2,128)(2,1)}), bf16[128,2,1024]{2,1,0:T(2,128)(2,1)S(1)}, u32[]{:S(2)}, u32[]{:S(2)}) async-start(bf16[128,2,1024]{2,1,0:T(2,128)(2,1)} %all_to_all.74), calls=%async_computation.10 | async-start | bytes 1048576 | tf_op jit(solution)/shard_map/all_to_all | solution.py:325
  1138.7 137.9 %copy-start.42 = (f32[1024]{0:T(1024)S(1)}, f32[1024]{0:T(1024)}, u32[]{:S(2)}) copy-start(f32[1024]{0:T(1024)} %get-tuple-element.245) | copy-start | bytes 12292
  1265.7 81.6 %all-to-all-start.4 = ((bf16[128,2,1024]{2,1,0:T(2,128)(2,1)}), bf16[128,2,1024]{2,1,0:T(2,128)(2,1)S(1)}, u32[]{:S(2)}, u32[]{:S(2)}) async-start(bf16[128,2,1024]{2,1,0:T(2,128)(2,1)} %all_to_all.68), calls=%async_computation.6 | async-start | bytes 1048576 | tf_op jit(solution)/shard_map/all_to_all | solution.py:318
  (34 other events, 70.0 us)
Sparse Core Ops, SparseCore 0:
  74.3 97.2 all-gather.8
  266.5 94.0 reduce-scatter.6
  619.0 91.9 reduce-scatter.10
  911.5 94.4 reduce-scatter.12
  1008.2 102.1 reduce-scatter.8
  1114.1 79.9 reduce-scatter.16
  1198.8 63.2 reduce-scatter.14
Sparse Core Ops, SparseCore 1:
  269.3 66.1 all-gather.12
  364.1 96.3 all-gather.10
  462.7 47.4 all-gather.14
  511.8 88.3 all-gather.18
  715.6 90.6 all-gather.16
  951.0 248.3 all-reduce.5
where the time goes:
time: 1370 us; the launch traced here: 1360 us
  waiting for transfers between devices  772 us (56%)
  blocking collectives  177 us (13%)
  matrix products  153 us (11%)
  other arithmetic  86 us (6%)
  local copies, waits for them, and re-layouts  74.8 us (5%)
  starting transfers between devices  60.4 us (4%)
  between operations  17.6 us (1%)
  loops' own time  16.1 us (1%)
    reduce_scatter x1, waiting for transfers between devices, body(): lax.psum_scatter(jnp.dot(hidden, w_down, preferred_element_type=jnp.float...  103 us
    reduce_scatter x1, waiting for transfers between devices, body(): lax.psum_scatter(jnp.dot(attn_rows, w_out, preferred_element_type=jnp.flo...  93.6 us
    reduce_scatter x1, waiting for transfers between devices, body(): lax.psum_scatter(jnp.einsum('kgf,kdf->gd', rows_now, w_gate_up, preferred...  92.1 us
    all_gather x1, waiting for transfers between devices, body(): lax.all_gather(grad_one.astype(jnp.bfloat16), 'tensor', axis=0, tiled=True)  90.5 us
    all_gather x1, waiting for transfers between devices, body(): lax.all_gather(out_grad_rows, 'tensor', axis=0, tiled=True)  90 us
    all_gather x1, waiting for transfers between devices, body(): lax.all_gather((normed_two * gain_two).astype(jnp.bfloat16), 'tensor', ax...  68.3 us
    psum x1, blocking collectives, body(): lax.psum((jnp.stack([gain_one_grad, gain_two_grad]), jnp.stack([query_gai...  67.1 us
    reduce_scatter x1, waiting for transfers between devices, body(): lax.psum_scatter(out_grad.astype(jnp.bfloat16), 'dp', scatter_dimension=1...  66.2 us
  transfers between devices with their start and end apart: 19, of which 12 were waited for; matrix products, arithmetic and copies ran while one was open for 9% of the time, Pallas kernels for 0%

commit v1 on v0

v1 whole, which is shorter than its diff:
```python
import functools

import jax
import jax.numpy as jnp
from jax import lax
from jax.experimental import pallas as pl
from jax.experimental.pallas import tpu as pltpu
from jax.sharding import Mesh
from jax.sharding import PartitionSpec as P

HEADS = 16
HEAD_DIM = 64
HALF = HEAD_DIM // 2
D = 1024
FF = 4096
ROWS = 256
RING = 4
PLANE = ROWS * RING
GROUP = 2 * PLANE
DEVICES = 128
VARIATES = 8
SEQS = 4
WIDE = 128
EPS = 1e-06
THETA = 10000.0
LOG2E = 1.4426950408889634
FAR = -16384.0
F32 = jnp.float32
BF16 = jnp.bfloat16

ALL = ("x", "zh", "core", "y", "zl")
FLAT = ("x", "zh", "zl")
NT = (((1,), (1,)), ((), ()))
TN = (((0,), (0,)), ((), ()))


def mm(left, right, dims=(((1,), (0,)), ((), ()))):
    return lax.dot_general(left, right, dims, preferred_element_type=F32)


def root_stats(values):
    return lax.rsqrt(jnp.mean(values * values, axis=-1, keepdims=True) + EPS)


def norm_back(grad_in, normed, scale_inv):
    return scale_inv * (grad_in - normed * jnp.mean(grad_in * normed, axis=-1, keepdims=True))


def pieces(values, count):
    out = []
    for _ in range(count):
        part = lax.reduce_precision(values, 8, 7)
        out.append(part.astype(BF16))
        values = values - part
    return out


def ring(values, step):
    return lax.ppermute(values, "y", [(i, (i + step) % RING) for i in range(RING)])


def swap_core(values):
    return lax.ppermute(values, "core", [(0, 1), (1, 0)])


def gather_ring(values):
    ahead = ring(values, -1)
    behind = ring(values, 1)
    half = values.shape[0] // 2
    far_top = ring(ahead[:half], -1)
    far_low = ring(behind[half:], 1)
    return [values, ahead, jnp.concatenate([far_top, far_low], 0), behind]


def reduce_ring(parts):
    far = ring(parts[2], 2)
    near = ring(parts[1], 1)
    back = ring(parts[3], -1)
    return (
        parts[0].astype(F32) + near.astype(F32) + back.astype(F32) + far.astype(F32)
    )


def flat_gather(shard):
    many = jnp.broadcast_to(shard[None], (16,) + shard.shape)
    mine = lax.all_to_all(many, FLAT, 0, 0, tiled=True)
    other = swap_core(mine)
    low = lax.axis_index("core") == 0
    both = jnp.stack([jnp.where(low, mine, other), jnp.where(low, other, mine)])
    return both.reshape((2, 4, 2, 2) + shard.shape)


def weights_of(shard):
    kinds, depth, width = shard.shape
    full = flat_gather(shard)
    return full.transpose(4, 1, 2, 0, 5, 3, 6).reshape(kinds, 16 * depth, 2 * width)


def grads_home(full, kinds, depth, width):
    core = lax.axis_index("core")
    split = full.reshape(kinds, 4, 2, 2, depth, 2, width)
    keep = lax.dynamic_index_in_dim(split, core, 3, keepdims=False)
    send = lax.dynamic_index_in_dim(split, 1 - core, 3, keepdims=False)
    got = swap_core(send)
    total = (keep.astype(F32) + got.astype(F32)).astype(BF16)
    total = total.transpose(1, 2, 4, 0, 3, 5).reshape(16, kinds, depth, width)
    arrived = lax.all_to_all(total, FLAT, 0, 0, tiled=True)
    return jnp.sum(arrived.astype(F32), axis=0)


def attend_kernel(q_ref, k_ref, v_ref, o_ref, *, chunks):
    size = k_ref.shape[1] // chunks
    query = q_ref[0]
    total = None
    for c in range(chunks):
        rows = pl.ds(c * size, size)
        score = mm(query, k_ref[0, rows, :], NT)
        prob = jnp.exp2(score).astype(BF16)
        part = mm(prob, v_ref[0, rows, :])
        total = part if total is None else total + part
    row_sum = total[:, HEAD_DIM : HEAD_DIM + 1]
    lane = lax.broadcasted_iota(jnp.int32, total.shape, 1)
    o_ref[0] = jnp.where(lane < HEAD_DIM, total / row_sum, jnp.log2(row_sum))


def attend(q_aug, k_aug, v_aug):
    heads, rows, wide = q_aug.shape
    block = 512
    return pl.pallas_call(
        functools.partial(attend_kernel, chunks=4),
        grid=(heads, rows // block),
        in_specs=[
            pl.BlockSpec((1, block, wide), lambda h, i: (h, i, 0)),
            pl.BlockSpec((1, rows, wide), lambda h, i: (h, 0, 0)),
            pl.BlockSpec((1, rows, wide), lambda h, i: (h, 0, 0)),
        ],
        out_specs=pl.BlockSpec((1, block, wide), lambda h, i: (h, i, 0)),
        out_shape=jax.ShapeDtypeStruct((heads, rows, wide), F32),
        compiler_params=pltpu.CompilerParams(vmem_limit_bytes=48 * 2**20),
        cost_estimate=pl.CostEstimate(
            flops=heads * rows * rows * wide * 8, bytes_accessed=heads * rows * wide * 10,
            transcendentals=heads * rows * rows,
        ),
    )(q_aug, k_aug, v_aug)


def attend_back_kernel(q_ref, k_ref, v_ref, g_ref, dq_ref, dk_ref, dv_ref, *, chunks):
    size = k_ref.shape[1] // chunks
    query = q_ref[0]
    grad = g_ref[0]

    @pl.when(pl.program_id(1) == 0)
    def _():
        dk_ref[...] = jnp.zeros_like(dk_ref)
        dv_ref[...] = jnp.zeros_like(dv_ref)

    total = None
    for c in range(chunks):
        rows = pl.ds(c * size, size)
        keys = k_ref[0, rows, :]
        prob = jnp.exp2(mm(keys, query, NT))
        slope = mm(v_ref[0, rows, :], grad, NT)
        d_score = (prob * slope).astype(BF16)
        dv_ref[0, rows, :] += mm(prob.astype(BF16), grad)
        dk_ref[0, rows, :] += mm(d_score, query)
        part = mm(d_score, keys, TN)
        total = part if total is None else total + part
    dq_ref[0] = total


def attend_back(q_aug, k_aug, v_aug, g_aug):
    heads, rows, wide = q_aug.shape
    block = 512
    moving = pl.BlockSpec((1, block, wide), lambda h, i: (h, i, 0))
    fixed = pl.BlockSpec((1, rows, wide), lambda h, i: (h, 0, 0))
    shape = jax.ShapeDtypeStruct((heads, rows, wide), F32)
    return pl.pallas_call(
        functools.partial(attend_back_kernel, chunks=4),
        grid=(heads, rows // block),
        in_specs=[moving, fixed, fixed, moving],
        out_specs=[moving, fixed, fixed],
        out_shape=[shape] * 3,
        compiler_params=pltpu.CompilerParams(vmem_limit_bytes=48 * 2**20),
        cost_estimate=pl.CostEstimate(
            flops=heads * rows * rows * wide * 20, bytes_accessed=heads * rows * wide * 20,
            transcendentals=heads * rows * rows,
        ),
    )(q_aug, k_aug, v_aug, g_aug)


def feed_kernel(b_ref, g_ref, w_ref, y_ref, db_ref, hid_ref, dg_ref, du_ref, y_sum, db_sum):
    step = pl.program_id(0)
    rows = b_ref[...]
    gate_w, up_w, down_w = w_ref[0], w_ref[1], w_ref[2]
    gate = mm(rows, gate_w)
    up = mm(rows, up_w)
    d_hidden = mm(g_ref[...], down_w)
    sig = 1.0 / (1.0 + jnp.exp(-gate))
    silu = gate * sig
    hidden = (silu * up).astype(BF16)
    d_gate = (d_hidden * up * (sig * (1.0 + gate * (1.0 - sig)))).astype(BF16)
    d_up = (d_hidden * silu).astype(BF16)
    hid_ref[...] = hidden
    dg_ref[...] = d_gate
    du_ref[...] = d_up
    y_part = mm(hidden, down_w, NT)
    db_part = mm(d_gate, gate_w, NT) + mm(d_up, up_w, NT)

    @pl.when(step == 0)
    def _():
        y_sum[...] = y_part
        db_sum[...] = db_part

    @pl.when(step > 0)
    def _():
        y_sum[...] += y_part
        db_sum[...] += db_part

    @pl.when(step == pl.num_programs(0) - 1)
    def _():
        y_ref[...] = y_sum[...].astype(BF16)
        db_ref[...] = db_sum[...].astype(BF16)


def feed(rows_b, rows_g, weights):
    rows = rows_b.shape[0]
    width = weights.shape[2]
    block = 256
    whole = pl.BlockSpec((rows, D), lambda f: (0, 0))
    part = pl.BlockSpec((rows, block), lambda f: (0, f))
    low_d = jax.ShapeDtypeStruct((rows, D), BF16)
    low_f = jax.ShapeDtypeStruct((rows, width), BF16)
    return pl.pallas_call(
        feed_kernel,
        grid=(width // block,),
        in_specs=[whole, whole, pl.BlockSpec((3, D, block), lambda f: (0, 0, f))],
        out_specs=[whole, whole, part, part, part],
        out_shape=[low_d, low_d, low_f, low_f, low_f],
        scratch_shapes=[pltpu.VMEM((rows, D), F32)] * 2,
        compiler_params=pltpu.CompilerParams(vmem_limit_bytes=48 * 2**20),
        cost_estimate=pl.CostEstimate(
            flops=12 * rows * D * width, bytes_accessed=6 * D * width + rows * D * 8 + rows * width * 6,
            transcendentals=rows * width,
        ),
    )(rows_b, rows_g, weights)


def turn(values, cosine, sine):
    first, second = values[..., :HALF], values[..., HALF:]
    return jnp.concatenate(
        [first * cosine - second * sine, first * sine + second * cosine], axis=-1
    )


def turn_back(grads, cosine, sine):
    upper, lower = grads[..., :HALF], grads[..., HALF:]
    return jnp.concatenate(
        [upper * cosine + lower * sine, lower * cosine - upper * sine], axis=-1
    )


def body(
    tokens,
    cotangent,
    destination,
    variate_ids,
    time_ids,
    seq_lengths,
    qkv_weight,
    out_weight,
    gate_up_weight,
    down_weight,
    norm_gains,
    qk_gains,
    variate_bias,
):
    core = lax.axis_index("core")
    low_core = core == 0
    y_at = lax.axis_index("y")
    zl_at = lax.axis_index("zl")

    def mine_other(pair):
        return (
            jnp.where(low_core, pair[..., :WIDE], pair[..., WIDE:]),
            jnp.where(low_core, pair[..., WIDE:], pair[..., :WIDE]),
        )

    def side_by_side(mine, other):
        return jnp.concatenate(
            [jnp.where(low_core, mine, other), jnp.where(low_core, other, mine)], axis=-1
        )

    slot = destination % ROWS
    group_at = destination // GROUP
    block_at = (destination % GROUP) // ROWS
    device_at = ((group_at // 2) * 2 + block_at // 4) * 8 + (block_at % 4) * 2 + group_at % 2
    key = device_at * ROWS + slot
    rank = jnp.sum((key[None, :] < key[:, None]).astype(jnp.int32), axis=1)
    deal = (jnp.arange(ROWS)[:, None] == rank[None, :]).astype(BF16)
    facts = jnp.stack([slot, variate_ids, time_ids // 32, time_ids % 32], axis=1).astype(BF16)
    facts = jnp.concatenate([facts, jnp.zeros((ROWS, WIDE - 4), BF16)], axis=1)
    gains_row = jnp.broadcast_to(norm_gains.reshape(1, WIDE), (ROWS, WIDE))
    outgoing = jnp.concatenate([tokens, cotangent, facts, gains_row], axis=1)
    span = outgoing.shape[1]
    outgoing = mm(deal, outgoing).astype(BF16).reshape(DEVICES, 2, span)
    arrived = lax.all_to_all(outgoing, ALL, 0, 0, tiled=True)

    attn_shard = jnp.concatenate([qkv_weight, out_weight.T[None]], 0)
    feed_shard = jnp.concatenate([gate_up_weight, down_weight.T[None]], 0)
    attn_shard, arrived = lax.optimization_barrier((attn_shard, arrived))
    attn_w = weights_of(attn_shard)
    feed_shard, attn_w = lax.optimization_barrier((feed_shard, attn_w))
    feed_w = weights_of(feed_shard)

    lengths_other = swap_core(seq_lengths)
    lengths = jnp.where(zl_at == core, seq_lengths, lengths_other)[0]
    bias_other = lax.ppermute(variate_bias, "zl", [(0, 1), (1, 0)])
    bias_pair = jnp.where(zl_at == core, variate_bias, bias_other)

    all_gains = arrived[:, 0, span - WIDE :].reshape(16, 8, 2, 64)[:, 0]
    all_gains = all_gains.transpose(1, 0, 2).reshape(2, D).astype(F32)
    gain_one, gain_two = all_gains[0], all_gains[1]
    slots = arrived[:, :, 2 * D].reshape(2 * DEVICES)
    place = (jnp.arange(ROWS).astype(BF16)[:, None] == slots[None, :]).astype(BF16)
    placed = mm(place, arrived.reshape(2 * DEVICES, span))
    inputs = placed[:, :D]
    grad_rows = placed[:, D : 2 * D].astype(BF16)
    facts_here = placed[:, 2 * D : 2 * D + WIDE].astype(BF16)

    scale_one = root_stats(inputs)
    normed_one = inputs * scale_one
    attn_in = (normed_one * gain_one).astype(BF16)
    attn_all = gather_ring(jnp.concatenate([attn_in, facts_here], axis=1))
    attn_all = jnp.concatenate(attn_all, 0)
    facts_all = attn_all[:, D:].astype(F32)
    attn_all = attn_all[:, :D]
    grad_all = gather_ring(grad_rows)

    variates_own = facts_all[:, 1].astype(jnp.int32)
    times = facts_all[:, 2] * 32.0 + facts_all[:, 3]
    variates = jnp.concatenate([variates_own, swap_core(variates_own)])
    blocks_y = (y_at + jnp.arange(RING)) % RING
    blocks = jnp.concatenate([core * RING + blocks_y, (1 - core) * RING + blocks_y])
    positions = (blocks[:, None] * ROWS + jnp.arange(ROWS)[None, :]).reshape(GROUP)
    segments = jnp.sum((positions[:, None] >= jnp.cumsum(lengths)[None, :]).astype(jnp.int32), 1)

    projected = jnp.einsum("gd,kde->kge", attn_all, attn_w[:3], preferred_element_type=F32)
    heads_here = 4
    query_raw = projected[0].reshape(PLANE, heads_here, HEAD_DIM)
    key_raw = projected[1].reshape(PLANE, heads_here, HEAD_DIM)
    query_inv = root_stats(query_raw)
    query_unit = query_raw * query_inv
    key_inv = root_stats(key_raw)
    key_unit = key_raw * key_inv
    inverse = THETA ** (-2.0 * jnp.arange(HALF).astype(F32) / HEAD_DIM)
    angles = times[:, None] * inverse[None, :]
    cosine, sine = jnp.cos(angles)[:, None, :], jnp.sin(angles)[:, None, :]
    query_rot = turn(query_unit * qk_gains[0], cosine, sine) * (HEAD_DIM ** (-0.5) * LOG2E)
    key_rot = turn(key_unit * qk_gains[1], cosine, sine)
    qkv_low = jnp.stack(
        [
            query_rot.reshape(PLANE, 2 * WIDE).astype(BF16),
            key_rot.reshape(PLANE, 2 * WIDE).astype(BF16),
            projected[2].astype(BF16),
        ]
    )
    qkv_mine, qkv_send = mine_other(qkv_low)
    qkv_got = swap_core(qkv_send)
    qkv_mine = jnp.concatenate([qkv_mine, qkv_got], axis=1)
    qkv_mine = qkv_mine.reshape(3, GROUP, 2, HEAD_DIM).transpose(0, 2, 1, 3)

    var_hot = (variates[:, None] == jnp.arange(VARIATES)[None, :]).astype(F32)
    seg_hot = (segments[:, None] == jnp.arange(SEQS)[None, :]).astype(F32)
    bias_parts = pieces(bias_pair * LOG2E, 3)
    query_tail = jnp.concatenate([var_hot] * 3 + [seg_hot], axis=1).astype(BF16)
    key_bias = [
        jnp.where(
            (var_hot > 0)[None], part[0][:, None, None].astype(F32), part[1][:, None, None].astype(F32)
        )
        for part in bias_parts
    ]
    seg_far = jnp.broadcast_to(((1.0 - seg_hot) * FAR)[None], (2, GROUP, SEQS))
    key_tail = jnp.concatenate(key_bias + [seg_far, jnp.ones((2, GROUP, 3), F32)], axis=2).astype(BF16)
    tail = 3 * VARIATES + SEQS
    spare = WIDE - HEAD_DIM
    query_tail = jnp.broadcast_to(query_tail[None], (2, GROUP, tail))
    zeros = jnp.zeros((2, GROUP, spare), BF16)
    query_aug = jnp.concatenate([qkv_mine[0], query_tail, zeros[..., tail:]], axis=2)
    key_aug = jnp.concatenate([qkv_mine[1], key_tail, zeros[..., tail + 3 :]], axis=2)
    value_aug = jnp.concatenate(
        [qkv_mine[2], jnp.ones((2, GROUP, 3), BF16), zeros[..., 3:]], axis=2
    )
    attended = attend(query_aug, key_aug, value_aug)
    log_total = attended[:, :, HEAD_DIM : HEAD_DIM + 1]
    attended = attended[:, :, :HEAD_DIM]
    att_low = attended.transpose(1, 0, 2).reshape(GROUP, WIDE).astype(BF16)
    att_plane = side_by_side(att_low[:PLANE], swap_core(att_low[PLANE:]))
    out_part = mm(att_plane, attn_w[3], NT).astype(BF16).reshape(RING, ROWS, D)
    hidden_one = inputs + reduce_ring([out_part[r] for r in range(RING)])

    scale_two = root_stats(hidden_one)
    normed_two = hidden_one * scale_two
    feed_in = (normed_two * gain_two).astype(BF16)
    feed_all = gather_ring(feed_in)
    fed = [feed(feed_all[r], grad_all[r], feed_w) for r in range(RING)]
    grad_normed_two = reduce_ring([f[1] for f in fed])
    mixed = (hidden_one + reduce_ring([f[0] for f in fed])).astype(BF16)

    feed_rows = jnp.concatenate(feed_all, 0)
    hidden_all = jnp.concatenate([f[2] for f in fed], 0)
    d_pair = jnp.stack(
        [jnp.concatenate([f[3] for f in fed], 0), jnp.concatenate([f[4] for f in fed], 0)]
    )
    grad_cat = jnp.concatenate(grad_all, 0)
    gate_up_full = jnp.einsum("gd,kgf->kdf", feed_rows, d_pair, preferred_element_type=F32).astype(BF16)
    down_full = mm(grad_cat, hidden_all, TN).astype(BF16)
    feed_grad = grads_home(jnp.concatenate([gate_up_full, down_full[None]], 0), 3, 64, 512)

    gain_two_grad = jnp.sum(grad_normed_two * normed_two, axis=0)
    grad_one = grad_rows.astype(F32) + norm_back(grad_normed_two * gain_two, normed_two, scale_two)

    grad_one_all = jnp.concatenate(gather_ring(grad_one.astype(BF16)), 0)
    grad_att = mm(grad_one_all, attn_w[3]).astype(BF16)
    grad_mine, grad_send = mine_other(grad_att)
    grad_mine = jnp.concatenate([grad_mine, swap_core(grad_send)], 0)
    grad_mine = grad_mine.reshape(GROUP, 2, HEAD_DIM).transpose(1, 0, 2)
    dots = jnp.sum(grad_mine.astype(F32) * attended, axis=-1, keepdims=True)
    grad_aug = jnp.concatenate([grad_mine] + pieces(-dots, 3) + [zeros[..., 3:]], axis=2)
    query_back = jnp.concatenate(
        [qkv_mine[0], query_tail] + pieces(-log_total, 3) + [zeros[..., tail + 3 :]], axis=2
    )
    d_query, d_key, d_value = attend_back(query_back, key_aug, value_aug, grad_aug)
    by_variate = jnp.sum(d_key[:, :, HEAD_DIM : HEAD_DIM + VARIATES] * var_hot[None], axis=(1, 2))
    by_all = jnp.sum(d_key[:, :, HEAD_DIM : HEAD_DIM + VARIATES], axis=(1, 2))
    bias_part = jnp.stack([by_variate, by_all - by_variate])
    d_all = jnp.stack([d_query, d_key * (1.0 / LOG2E), d_value])[..., :HEAD_DIM].astype(BF16)
    d_all = d_all.transpose(0, 2, 1, 3).reshape(3, GROUP, WIDE)
    d_plane = side_by_side(d_all[:, :PLANE], swap_core(d_all[:, PLANE:]))
    d_query_rows = d_plane[0].astype(F32).reshape(PLANE, heads_here, HEAD_DIM)
    d_key_rows = d_plane[1].astype(F32).reshape(PLANE, heads_here, HEAD_DIM)
    grad_q_unit = turn_back(d_query_rows * HEAD_DIM ** (-0.5), cosine, sine)
    grad_k_unit = turn_back(d_key_rows, cosine, sine)
    query_gain_grad = jnp.sum(grad_q_unit * query_unit, axis=(0, 1))
    key_gain_grad = jnp.sum(grad_k_unit * key_unit, axis=(0, 1))
    grad_q_raw = norm_back(grad_q_unit * qk_gains[0], query_unit, query_inv)
    grad_k_raw = norm_back(grad_k_unit * qk_gains[1], key_unit, key_inv)
    grad_proj = jnp.stack(
        [
            grad_q_raw.reshape(PLANE, 2 * WIDE).astype(BF16),
            grad_k_raw.reshape(PLANE, 2 * WIDE).astype(BF16),
            d_plane[2],
        ]
    )
    in_part = jnp.einsum("kge,kde->gd", grad_proj, attn_w[:3], preferred_element_type=F32)
    in_part = in_part.astype(BF16).reshape(RING, ROWS, D)
    grad_normed_one = reduce_ring([in_part[r] for r in range(RING)])
    qkv_full = jnp.einsum("gd,kge->kde", attn_all, grad_proj, preferred_element_type=F32).astype(BF16)
    out_full = mm(grad_one_all, att_plane, TN).astype(BF16)
    attn_grad = grads_home(jnp.concatenate([qkv_full, out_full[None]], 0), 4, 64, 128)

    gain_one_grad = jnp.sum(grad_normed_one * normed_one, axis=0)
    input_grad = grad_one + norm_back(grad_normed_one * gain_one, normed_one, scale_one)

    back_mixed = mm(place, mixed, TN).astype(BF16).reshape(DEVICES, 2, D)
    home_mixed = lax.all_to_all(back_mixed, ALL, 0, 0, tiled=True)
    new_tokens = mm(deal, home_mixed.reshape(ROWS, D), TN).astype(BF16)

    gain_sums = jnp.stack([gain_one_grad, gain_two_grad]).reshape(2, 16, 64).transpose(1, 0, 2)
    gain_sums = jnp.broadcast_to(gain_sums.reshape(16, 1, WIDE), (16, 8, WIDE))
    qk_row = jnp.concatenate([query_gain_grad, key_gain_grad])
    qk_row = jnp.broadcast_to(qk_row[None, None], (16, 8, WIDE))
    here = (jnp.arange(8) == y_at * 2 + core)[None, :, None]
    bias_row = jnp.where(here, bias_part.reshape(1, 1, 4), 0.0)
    bias_row = jnp.broadcast_to(bias_row, (16, 8, 4))
    smalls = jnp.concatenate([gain_sums, qk_row, bias_row, jnp.zeros((16, 8, WIDE - 4), F32)], axis=2)
    smalls = jnp.stack(pieces(smalls.reshape(DEVICES, 3 * WIDE), 2), axis=1)
    back_grads = mm(place, input_grad.astype(BF16), TN).astype(BF16).reshape(DEVICES, 2, D)
    home = lax.all_to_all(jnp.concatenate([back_grads, smalls], axis=2), ALL, 0, 0, tiled=True)
    token_grads = mm(deal, home[:, :, :D].reshape(ROWS, D), TN).astype(BF16)
    sums = jnp.sum(home[:, :, D:].astype(F32), axis=(0, 1))
    gains_grad = sums[:WIDE].reshape(2, 64)
    qk_grad = sums[WIDE : 2 * WIDE].reshape(2, 64)
    bias_grad = sums[2 * WIDE : 2 * WIDE + 4].reshape(2, 2)

    return (
        new_tokens,
        token_grads,
        attn_grad[:3],
        attn_grad[3].T,
        feed_grad[:2],
        feed_grad[2].T,
        gains_grad,
        qk_grad,
        bias_grad,
    )


def solution(mesh):
    fine = Mesh(mesh.devices.reshape(4, 2, 2, 4, 2), ALL)
    dp = ("x", "zh", "core")
    tensor = ("y", "zl")
    in_specs = (
        P(ALL, None),
        P(ALL, None),
        P(ALL),
        P(ALL),
        P(ALL),
        P(dp, None),
        P(None, dp, tensor),
        P(tensor, dp),
        P(None, dp, tensor),
        P(tensor, dp),
        P(None, dp),
        P(),
        P(None, tensor),
    )
    out_specs = (
        P(ALL, None),
        P(ALL, None),
        P(None, dp, tensor),
        P(tensor, dp),
        P(None, dp, tensor),
        P(tensor, dp),
        P(None, dp),
        P(),
        P(None, tensor),
    )
    return jax.shard_map(body, mesh=fine, in_specs=in_specs, out_specs=out_specs, check_vma=False)
```

time: 1370 us -> 618 us (0.45)
  waiting for transfers between devices: 772 us -> 150 us
  blocking collectives: 177 us -> 0 us
  local copies, waits for them, and re-layouts: 74.8 us -> 198 us
  matrix products: 153 us -> 39.2 us
  Pallas kernels: 0 us -> 68.6 us
  starting transfers between devices: 60.4 us -> 86.9 us
  other arithmetic: 86 us -> 61 us
  loops' own time: 16.1 us -> 0 us
  between operations: 17.6 us -> 2.55 us
    reduce_scatter x6 -> x0, waiting for transfers between devices: 465 us -> none  [the longest x1 103 us: body(): lax.psum_scatter(jnp.dot(hidden, w_down, preferred_element_type=jnp.float...]
    all_gather x6 -> x0, waiting for transfers between devices: 288 us -> none  [the longest x1 90.5 us: body(): lax.all_gather(grad_one.astype(jnp.bfloat16), 'tensor', axis=0, tiled=True)]
    dot_general x40 -> x14, matrix products: 153 us -> 39.2 us  [the longest x10 23.9 us: mm(): return lax.dot_general(left, right, dims, preferred_element_type=F32)]
    all_gather x3 -> x0, blocking collectives: 86.5 us -> none  [the longest x1 36.1 us: body(): lax.all_gather(qkv_weight, 'dp', axis=1, tiled=True)]
    ppermute x0 -> x39, waiting for transfers between devices: none -> 86.1 us  [the longest x28 84.9 us: ring(): lax.ppermute(values, 'y', [(i, (i + step) % RING) for i in range(RING)])]
    pallas_call x0 -> x6, Pallas kernels: none -> 68.6 us  [the longest x4 29.3 us: feed(): pl.pallas_call(feed_kernel, grid=(width // block,), in_specs=[whole, whol...]
    psum x1 -> x0, blocking collectives: 67.1 us -> none  [body(): lax.psum((jnp.stack([gain_one_grad, gain_two_grad]), jnp.stack([query_gai...]
    concatenate x0 -> x18, local copies, waits for them, and re-layouts: none -> 51.2 us  [the longest x3 16.8 us: body(): jnp.concatenate([gate_up_full, down_full[None]], 0)]
  transfers between devices with their start and end apart: 19 -> 46, of which waited for: 12 -> 18; matrix products, arithmetic and copies ran while one was open for 9% -> 40% of each run, Pallas kernels for 0% -> 9%
where the time goes in v1:
time: 618 us; the launch traced here: 607 us
  local copies, waits for them, and re-layouts  198 us (32%)
  waiting for transfers between devices  150 us (24%)
  starting transfers between devices  86.9 us (14%)
  Pallas kernels  68.6 us (11%)
  other arithmetic  61 us (10%)
  matrix products  39.2 us (6%)
    ppermute x28, waiting for transfers between devices, ring(): lax.ppermute(values, 'y', [(i, (i + step) % RING) for i in range(RING)])  84.9 us
    unnamed x179, local copies, waits for them, and re-layouts  41.3 us
    ppermute x28, starting transfers between devices, ring(): lax.ppermute(values, 'y', [(i, (i + step) % RING) for i in range(RING)])  34.7 us
    all_to_all x2, waiting for transfers between devices, grads_home(): arrived = lax.all_to_all(total, FLAT, 0, 0, tiled=True)  30.6 us
    pallas_call x4, Pallas kernels, feed(): pl.pallas_call(feed_kernel, grid=(width // block,), in_specs=[whole, whol...  29.3 us
    pallas_call x1, Pallas kernels, attend_back(): pl.pallas_call(functools.partial(attend_back_kernel, chunks=4), grid=(hea...  25.5 us
    dot_general x10, matrix products, mm(): return lax.dot_general(left, right, dims, preferred_element_type=F32)  23.9 us
    all_to_all x1, waiting for transfers between devices, body(): arrived = lax.all_to_all(outgoing, ALL, 0, 0, tiled=True)  19.8 us
  transfers between devices with their start and end apart: 46, of which 18 were waited for; matrix products, arithmetic and copies ran while one was open for 40% of the time, Pallas kernels for 9%

profile of v1, /device:TPU:0, one launch (start us, length us, event | category | flops | bytes accessed | tf_op | source)
XLA Modules:
  0.0 606.7 jit_solution(4682743753507683055)
XLA Ops:
  9.8 10.6 %all-to-all-start = ((bf16[128,2,2304]{2,1,0:T(2,128)(2,1)}), bf16[128,2,2304]{2,1,0:T(2,128)(2,1)S(1)}, u32[]{:S(2)}, u32[]{:S(2)}) async-start(bf16[128,2,2304]{2,1,0:T(2,128)(2,1)} %reshape.763), calls=%async_computation | async-start | bytes 2359296 | tf_op jit(solution)/shard_map/all_to_all | solution.py:306
  21.2 19.8 %all-to-all-done = bf16[128,2,2304]{2,1,0:T(2,128)(2,1)S(1)} async-done(((bf16[128,2,2304]{2,1,0:T(2,128)(2,1)}), bf16[128,2,2304]{2,1,0:T(2,128)(2,1)S(1)}, u32[]{:S(2)}, u32[]{:S(2)}) %all-to-all-start) | async-done | bytes 1179680 | tf_op jit(solution)/shard_map/all_to_all | solution.py:306
  48.2 3.7 all-to-all-start.1
  51.9 7.5 %collective-permute-done.1 = bf16[256,1152]{1,0:T(8,128)(2,1)S(1)} collective-permute-done((bf16[256,1152]{1,0:T(8,128)(2,1)S(1)}, bf16[256,1152]{1,0:T(8,128)(2,1)S(1)}, u32[]{:S(2)}, u32[]{:S(2)}) %collective-permute-start.1) | collective-permute-done | bytes 589856 | tf_op jit(solution)/shard_map/ppermute | solution.py:59
  64.2 3.7 collective-permute-done.2
  68.5 3.5 collective-permute-done.4
  77.3 3.5 copy.160
  83.9 4.2 convolution_bitcast_fusion
  97.9 4.7 all-to-all-start.2
  111.7 7.8 %concatenate.147.k_ref = bf16[2,2048,128]{2,1,0:T(8,128)(2,1)} concatenate(bf16[2,2048,64]{2,1,0:T(8,128)(2,1)} %get-tuple-element.89, bf16[2,2048,8]{2,1,0:T(8,128)(2,1)} %get-tuple-element.133, bf16[2,2048,8]{2,1,0:T(8,128)(2,1)} %get-tuple-element.132, bf16[2,2048,8]{2,1,0:T(8,128)(2,1)} %get-tuple-element.131, bf16[2,2048,4]{2,1,0:T(8,128)(2,1)} %broadcast_in_dim.183, ...), dimensions={2} | concatenate | bytes 2097152 | tf_op jit(solution)/shard_map/concatenate | solution.py:389
  121.5 13.8 %shard_map.196 = f32[2,2048,128]{2,1,0:T(8,128)S(1)} custom-call(bf16[2,2048,128]{2,1,0:T(8,128)(2,1)S(1)} %maximum_maximum_fusion.q_ref, bf16[2,2048,128]{2,1,0:T(8,128)(2,1)S(1)} %copy-done.6, bf16[2,2048,128]{2,1,0:T(8,128)(2,1)S(1)} %pad_maximum_fusion.4.v_ref), custom_call_target="tpu_custom_call" | custom-call | flops 8589934592 | bytes 5242880 | tf_op jit(solution)/shard_map/pallas_call | solution.py:129
  141.1 3.4 convolution_convert_fusion.1
  155.0 21.2 %collective-permute-done.10 = bf16[256,1024]{1,0:T(8,128)(2,1)} collective-permute-done((bf16[256,1024]{1,0:T(8,128)(2,1)S(1)}, bf16[256,1024]{1,0:T(8,128)(2,1)}, u32[]{:S(2)}, u32[]{:S(2)}) %collective-permute-start.10) | collective-permute-done | bytes 524320 | tf_op jit(solution)/shard_map/ppermute | solution.py:59
  183.5 3.8 collective-permute-done.18.g_ref
  193.5 10.4 %collective-permute-done.23 = bf16[128,1024]{1,0:T(8,128)(2,1)} collective-permute-done((bf16[128,1024]{1,0:T(8,128)(2,1)}, bf16[128,1024]{1,0:T(8,128)(2,1)}, u32[]{:S(2)}, u32[]{:S(2)}) %collective-permute-start.23) | collective-permute-done | bytes 262176 | tf_op jit(solution)/shard_map/ppermute | solution.py:59
  209.7 4.0 copy.161
  223.0 7.3 %concatenate.152.q_ref = bf16[2,2048,128]{2,1,0:T(8,128)(2,1)} concatenate(bf16[2,2048,64]{2,1,0:T(8,128)(2,1)} %get-tuple-element.90, bf16[2,2048,28]{2,1,0:T(8,128)(2,1)} %copy-done.34, bf16[2,2048,1]{2,1,0:T(8,128)(2,1)} %get-tuple-element.100, bf16[2,2048,1]{2,1,0:T(8,128)(2,1)} %get-tuple-element.99, bf16[2,2048,1]{2,1,0:T(8,128)(2,1)} %get-tuple-element.98, ...), dimensions={2} | concatenate | bytes 2097152 | tf_op jit(solution)/shard_map/concatenate | solution.py:429
  236.4 3.3 broadcast_select_fusion.1
  240.2 6.0 copy.171
  246.2 11.0 %reshape.769.w_ref = bf16[3,1024,1024]{2,1,0:T(8,128)(2,1)} reshape(bf16[3,4,2,2,64,2,512]{6,5,4,3,2,1,0:T(2,128)(2,1)} %copy.171) | data formatting | bytes 12582912 | tf_op jit(solution)/shard_map/reshape | solution.py:96
  257.2 7.3 %shard_map.197 = (bf16[256,1024]{1,0:T(8,128)(2,1)S(1)}, bf16[256,1024]{1,0:T(8,128)(2,1)S(1)}, bf16[256,1024]{1,0:T(8,128)(2,1)S(1)}, bf16[256,1024]{1,0:T(8,128)(2,1)S(1)}, bf16[256,1024]{1,0:T(8,128)(2,1)S(1)}) custom-call(bf16[256,1024]{1,0:T(8,128)(2,1)} %get-tuple-element.74.b_ref, bf16[256,1024]{1,0:T(8,128)(2,1)} %slice.399.g_ref, ...), custom_call_target="tpu_custom_call" | custom-call | flops 3221225472 | bytes 9961472 | tf_op jit(solution)/shard_map/pallas_call | solution.py:233
  266.1 7.8 %shard_map.200 = (bf16[256,1024]{1,0:T(8,128)(2,1)}, bf16[256,1024]{1,0:T(8,128)(2,1)}, bf16[256,1024]{1,0:T(8,128)(2,1)S(1)}, bf16[256,1024]{1,0:T(8,128)(2,1)S(1)}, bf16[256,1024]{1,0:T(8,128)(2,1)S(1)}) custom-call(bf16[256,1024]{1,0:T(8,128)(2,1)S(1)} %copy-done.9, bf16[256,1024]{1,0:T(8,128)(2,1)S(1)} %copy-done.8, bf16[3,1024,1024]{2,1,0:T(8,128)(2,1)} %reshape.769.w_ref), custom_call_target="tpu_custom_call" | custom-call | flops 3221225472 | bytes 9961472 | tf_op jit(solution)/shard_map/pallas_call | solution.py:233
  274.8 3.7 collective-permute-start.27
  278.5 7.1 %shard_map.199 = (bf16[256,1024]{1,0:T(8,128)(2,1)S(1)}, bf16[256,1024]{1,0:T(8,128)(2,1)S(1)}, bf16[256,1024]{1,0:T(8,128)(2,1)S(1)}, bf16[256,1024]{1,0:T(8,128)(2,1)S(1)}, bf16[256,1024]{1,0:T(8,128)(2,1)S(1)}) custom-call(bf16[256,1024]{1,0:T(8,128)(2,1)} %collective-permute-done.17.b_ref, bf16[256,1024]{1,0:T(8,128)(2,1)S(1)} %collective-permute-done.18.g_ref, ...), custom_call_target="tpu_custom_call" | custom-call | flops 3221225472 | bytes 9961472 | tf_op jit(solution)/shard_map/pallas_call | solution.py:233
  288.0 7.1 %shard_map.198 = (bf16[256,1024]{1,0:T(8,128)(2,1)S(1)}, bf16[256,1024]{1,0:T(8,128)(2,1)S(1)}, bf16[256,1024]{1,0:T(8,128)(2,1)S(1)}, bf16[256,1024]{1,0:T(8,128)(2,1)S(1)}, bf16[256,1024]{1,0:T(8,128)(2,1)S(1)}) custom-call(bf16[256,1024]{1,0:T(8,128)(2,1)} %collective-permute-done.14.b_ref, bf16[256,1024]{1,0:T(8,128)(2,1)S(1)} %copy-done.1, ...), custom_call_target="tpu_custom_call" | custom-call | flops 3221225472 | bytes 9961472 | tf_op jit(solution)/shard_map/pallas_call | solution.py:233
  297.9 6.2 %convert_bitcast_fusion = bf16[2,1024,1024]{1,2,0:T(8,128)(2,1)} fusion(bf16[1,1024,1024]{2,1,0:T(8,128)(2,1)S(1)} %maximum_bitcast_fusion.3, bf16[1,1024,1024]{2,1,0:T(8,128)(2,1)S(1)} %maximum_bitcast_fusion.2, bf16[1024,1024]{1,0:T(8,128)(2,1)S(1)} %copy-done.69), kind=kOutput, calls=%fused_computation.9 | convolution fusion | flops 4299161600 | bytes 10485760 | tf_op jit(solution)/shard_map/gd,kgf->kdf/dot_general | solution.py:415
  304.1 6.2 %copy.187 = bf16[2,1024,1024]{2,1,0:T(8,128)(2,1)} copy(bf16[2,1024,1024]{1,2,0:T(8,128)(2,1)} %convert_bitcast_fusion) | data formatting | bytes 8388608 | tf_op jit(solution)/shard_map/convert_element_type | solution.py:415
  310.3 7.8 %concatenate.170 = bf16[2,4,2,2,64,2,512]{6,5,4,3,2,1,0:T(2,128)(2,1)} reshape(bf16[2,1024,1024]{2,1,0:T(8,128)(2,1)} %copy.187) | data formatting | bytes 8388608 | tf_op jit(solution)/shard_map/concatenate | solution.py:417
  320.4 9.2 %constant_dynamic-update-slice_fusion.23 = bf16[3,4,2,2,64,2,512]{6,5,4,3,2,1,0:T(2,128)(2,1)} fusion(bf16[2,4,2,2,64,2,512]{6,5,4,3,2,1,0:T(2,128)(2,1)} %concatenate.170), kind=kLoop, calls=%fused_computation.227 | loop fusion | bytes 8388608
  331.4 9.3 %collective-permute-done.26 = bf16[256,1024]{1,0:T(8,128)(2,1)S(1)} collective-permute-done((bf16[256,1024]{1,0:T(8,128)(2,1)}, bf16[256,1024]{1,0:T(8,128)(2,1)S(1)}, u32[]{:S(2)}, u32[]{:S(2)}) %collective-permute-start.26) | collective-permute-done | bytes 524320 | tf_op jit(solution)/shard_map/ppermute | solution.py:59
  342.3 3.2 constant_dynamic-update-slice_fusion.9
  345.8 3.2 collective-permute-start.28
  353.7 11.5 %all-to-all-start.3 = ((bf16[128,2,1024]{2,1,0:T(2,128)(2,1)}), bf16[128,2,1024]{2,1,0:T(2,128)(2,1)}, u32[]{:S(2)}, u32[]{:S(2)}) async-start(bf16[128,2,1024]{2,1,0:T(2,128)(2,1)} %reshape.770), calls=%async_computation.3 | async-start | bytes 1048576 | tf_op jit(solution)/shard_map/all_to_all | solution.py:465
  370.4 5.3 fusion.25
  375.7 4.5 concatenate.173
  380.2 4.5 constant_dynamic-update-slice_fusion.22
  390.0 6.9 %dynamic-slice_bitcast_fusion = bf16[3,4,2,64,2,512]{5,4,3,2,1,0:T(2,128)(2,1)} fusion(bf16[3,4,2,2,64,2,512]{6,5,4,3,2,1,0:T(2,128)(2,1)} %constant_dynamic-update-slice_fusion.22, s32[]{:T(128)S(6)} %select_n.195), kind=kLoop, calls=%fused_computation.18 | loop fusion | bytes 6291460 | tf_op jit(solution)/shard_map/jit(dynamic_index_in_dim)/squeeze | solution.py:103
  417.6 3.4 fusion.14
  421.0 6.4 %concatenate.155.g_ref = bf16[2,2048,128]{2,1,0:T(8,128)(2,1)S(1)} concatenate(bf16[2,2048,64]{2,1,0:T(8,128)(2,1)} %bitcast.212, bf16[2,2048,1]{2,1,0:T(8,128)(2,1)} %copy.176, bf16[2,2048,1]{2,1,0:T(8,128)(2,1)} %get-tuple-element.87, bf16[2,2048,1]{2,1,0:T(8,128)(2,1)} %get-tuple-element.86, bf16[2,2048,61]{2,1,0:T(8,128)(2,1)} %copy-done.37), dimensions={2} | concatenate | bytes 2097152 | tf_op jit(solution)/shard_map/concatenate | solution.py:428
  428.6 25.5 %shard_map.201 = (f32[2,2048,128]{2,1,0:T(8,128)}, f32[2,2048,128]{2,1,0:T(8,128)}, f32[2,2048,128]{2,1,0:T(8,128)}) custom-call(bf16[2,2048,128]{2,1,0:T(8,128)(2,1)S(1)} %copy-done.3, bf16[2,2048,128]{2,1,0:T(8,128)(2,1)S(1)} %copy-done.7, bf16[2,2048,128]{2,1,0:T(8,128)(2,1)S(1)} %copy-done.5, bf16[2,2048,128]{2,1,0:T(8,128)(2,1)S(1)} %concatenate.155.g_ref), custom_call_target="tpu_custom_call" | custom-call | flops 21474836480 | bytes 10485760 | tf_op jit(solution)/shard_map/pallas_call | solution.py:177
  486.3 18.5 %collective-permute-done.34 = bf16[256,1024]{1,0:T(8,128)(2,1)S(1)} collective-permute-done((bf16[256,1024]{1,0:T(8,128)(2,1)S(1)}, bf16[256,1024]{1,0:T(8,128)(2,1)S(1)}, u32[]{:S(2)}, u32[]{:S(2)}) %collective-permute-start.34) | collective-permute-done | bytes 524320 | tf_op jit(solution)/shard_map/ppermute | solution.py:59
  513.8 9.1 %all-to-all-start.4 = ((bf16[128,2,1408]{2,1,0:T(2,128)(2,1)}), bf16[128,2,1408]{2,1,0:T(2,128)(2,1)S(1)}, u32[]{:S(2)}, u32[]{:S(2)}) async-start(bf16[128,2,1408]{2,1,0:T(2,128)(2,1)} %pad_maximum_fusion.7), calls=%async_computation.4 | async-start | bytes 1441792 | tf_op jit(solution)/shard_map/all_to_all | solution.py:478
  526.8 11.8 %all-to-all-done.4 = bf16[128,2,1408]{2,1,0:T(2,128)(2,1)S(1)} async-done(((bf16[128,2,1408]{2,1,0:T(2,128)(2,1)}), bf16[128,2,1408]{2,1,0:T(2,128)(2,1)S(1)}, u32[]{:S(2)}, u32[]{:S(2)}) %all-to-all-start.4) | async-done | bytes 720928 | tf_op jit(solution)/shard_map/all_to_all | solution.py:478
  538.5 3.7 all-to-all-start.5
  542.2 7.9 %fusion.5 = bf16[4,2,2,3,64,512]{5,2,4,1,0,3:T(2,128)(2,1)S(1)} fusion(bf16[3,4,2,64,2,512]{5,4,3,2,1,0:T(2,128)(2,1)} %collective-permute-done.38, bf16[3,4,2,2,64,2,512]{6,5,4,3,2,1,0:T(2,128)(2,1)} %constant_dynamic-update-slice_fusion.22, s32[]{:T(128)S(6)} %select_n.194), kind=kLoop, calls=%fused_computation.11 | loop fusion | flops 6291456 | bytes 9437188 | tf_op jit(solution)/shard_map/transpose | solution.py:106
  552.5 7.3 %all-to-all-done.5 = bf16[16,4,64,128]{3,2,1,0:T(8,128)(2,1)S(1)} async-done(((bf16[16,4,64,128]{3,2,1,0:T(8,128)(2,1)}), bf16[16,4,64,128]{3,2,1,0:T(8,128)(2,1)S(1)}, u32[]{:S(2)}, u32[]{:S(2)}) %all-to-all-start.5) | async-done | bytes 1048608 | tf_op jit(solution)/shard_map/all_to_all | solution.py:107
  560.8 4.0 all-to-all-start.6
  581.3 23.3 %all-to-all-done.6 = bf16[16,3,64,512]{3,2,1,0:T(8,128)(2,1)S(1)} async-done(((bf16[16,3,64,512]{3,2,1,0:T(8,128)(2,1)}), bf16[16,3,64,512]{3,2,1,0:T(8,128)(2,1)S(1)}, u32[]{:S(2)}, u32[]{:S(2)}) %all-to-all-start.6) | async-done | bytes 3145760 | tf_op jit(solution)/shard_map/all_to_all | solution.py:107
  (458 shorter events, 219.5 us)
Async XLA Ops:
  0.6 20.2 %collective-permute-start.7 = (s32[1,4]{1,0:T(1,128)}, s32[1,4]{1,0:T(1,128)S(1)}, u32[]{:S(2)}, u32[]{:S(2)}) collective-permute-start(s32[1,4]{1,0:T(1,128)} %param.18), channel_id=1, source_target_pairs={{0,8},{8,0},{1,9},{9,1},{2,10},{10,2},{3,11},{11,3},{4,12},{12,4},... | collective-permute-start | bytes 56 | tf_op jit(solution)/shard_map/ppermute | solution.py:63
  0.7 44.3 %collective-permute-start.8 = (f32[2,2]{1,0:T(2,128)}, f32[2,2]{1,0:T(2,128)S(1)}, u32[]{:S(2)}, u32[]{:S(2)}) collective-permute-start(f32[2,2]{1,0:T(2,128)} %param.25), channel_id=1, source_target_pairs={{0,1},{1,0},{2,3},{3,2},{4,5},{5,4},{6,7},{7,6},{8,9},{9,8},{10,11... | collective-permute-start | bytes 56 | tf_op jit(solution)/shard_map/ppermute | solution.py:317
  9.8 31.2 %all-to-all-start = ((bf16[128,2,2304]{2,1,0:T(2,128)(2,1)}), bf16[128,2,2304]{2,1,0:T(2,128)(2,1)S(1)}, u32[]{:S(2)}, u32[]{:S(2)}) async-start(bf16[128,2,2304]{2,1,0:T(2,128)(2,1)} %reshape.763), calls=%async_computation | async-start | bytes 2359296 | tf_op jit(solution)/shard_map/all_to_all | solution.py:306
  44.8 14.6 %collective-permute-start.1 = (bf16[256,1152]{1,0:T(8,128)(2,1)S(1)}, bf16[256,1152]{1,0:T(8,128)(2,1)S(1)}, u32[]{:S(2)}, u32[]{:S(2)}) collective-permute-start(bf16[256,1152]{1,0:T(8,128)(2,1)S(1)} %get-tuple-element.123), channel_id=1, source_target_pairs={{0,6},{2,0},{4,2},{6,4},{1,7},{3,1},{5,3},{7,5},{8,14},{10,8},{12,... | collective-permute-start | bytes 1769480 | tf_op jit(solution)/shard_map/ppermute | solution.py:59
  45.0 18.1 %collective-permute-start.3 = (bf16[256,1152]{1,0:T(8,128)(2,1)S(1)}, bf16[256,1152]{1,0:T(8,128)(2,1)S(1)}, u32[]{:S(2)}, u32[]{:S(2)}) collective-permute-start(bf16[256,1152]{1,0:T(8,128)(2,1)S(1)} %get-tuple-element.123), channel_id=1, source_target_pairs={{0,2},{2,4},{4,6},{6,0},{1,3},{3,5},{5,7},{7,1},{8,10},{10,12},{12... | collective-permute-start | bytes 1769480 | tf_op jit(solution)/shard_map/ppermute | solution.py:59
  48.2 24.6 %all-to-all-start.1 = ((bf16[16,4,64,128]{3,2,1,0:T(8,128)(2,1)}), bf16[16,4,64,128]{3,2,1,0:T(8,128)(2,1)S(1)}, u32[]{:S(2)}, u32[]{:S(2)}) async-start(bf16[16,4,64,128]{3,2,1,0:T(8,128)(2,1)} %broadcast_in_dim.174), calls=%async_computation.1 | async-start | bytes 2097152 | tf_op jit(solution)/shard_map/all_to_all | solution.py:86
  60.1 7.7 %collective-permute-start.2 = (bf16[128,1152]{1,0:T(8,128)(2,1)}, bf16[128,1152]{1,0:T(8,128)(2,1)S(1)}, u32[]{:S(2)}, u32[]{:S(2)}) collective-permute-start(bf16[128,1152]{1,0:T(8,128)(2,1)} %slice.372), channel_id=1, source_target_pairs={{0,6},{2,0},{4,2},{6,4},{1,7},{3,1},{5,3},{7,5},{8,14},{10,8},{12,... | collective-permute-start | bytes 884744 | tf_op jit(solution)/shard_map/ppermute | solution.py:59
  63.2 8.9 %collective-permute-start.4 = (bf16[128,1152]{1,0:T(8,128)(2,1)S(1)}, bf16[128,1152]{1,0:T(8,128)(2,1)S(1)}, u32[]{:S(2)}, u32[]{:S(2)}) collective-permute-start(bf16[128,1152]{1,0:T(8,128)(2,1)S(1)} %slice.373), channel_id=1, source_target_pairs={{0,2},{2,4},{4,6},{6,0},{1,3},{3,5},{5,7},{7,1},{8,10},{10,12},{12... | collective-permute-start | bytes 884744 | tf_op jit(solution)/shard_map/ppermute | solution.py:59
  72.8 4.1 collective-permute-start
  75.1 1.8 collective-permute-start.6
  92.1 10.5 %collective-permute-start.5 = (bf16[3,1024,128]{1,2,0:T(8,128)(2,1)S(1)}, bf16[3,1024,128]{1,2,0:T(8,128)(2,1)S(1)}, u32[]{:S(2)}, u32[]{:S(2)}) collective-permute-start(bf16[3,1024,128]{1,2,0:T(8,128)(2,1)S(1)} %get-tuple-element.107), channel_id=1, source_target_pairs={{0,8},{8,0},{1,9},{9,1},{2,10},{10,2},{3,11},{11,3},{4,12},{12,4},... | collective-permute-start | bytes 2359304 | tf_op jit(solution)/shard_map/ppermute | solution.py:63
  97.9 48.6 %all-to-all-start.2 = ((bf16[16,3,64,512]{3,2,1,0:T(8,128)(2,1)}), bf16[16,3,64,512]{3,2,1,0:T(8,128)(2,1)}, u32[]{:S(2)}, u32[]{:S(2)}) async-start(bf16[16,3,64,512]{3,2,1,0:T(8,128)(2,1)} %broadcast_in_dim.185), calls=%async_computation.2 | async-start | bytes 6291456 | tf_op jit(solution)/shard_map/all_to_all | solution.py:86
  138.2 1.9 collective-permute-start.9
  146.5 89.9 %collective-permute-start.13 = (bf16[16,3,64,512]{3,2,1,0:T(8,128)(2,1)}, bf16[16,3,64,512]{3,2,1,0:T(8,128)(2,1)}, u32[]{:S(2)}, u32[]{:S(2)}) collective-permute-start(bf16[16,3,64,512]{3,2,1,0:T(8,128)(2,1)} %all-to-all-done.2), channel_id=1, source_target_pairs={{0,8},{8,0},{1,9},{9,1},{2,10},{10,2},{3,11},{11,3},{4,12},{12,4},... | collective-permute-start | bytes 9437192 | tf_op jit(solution)/shard_map/ppermute | solution.py:63
  148.9 27.3 %collective-permute-start.10 = (bf16[256,1024]{1,0:T(8,128)(2,1)S(1)}, bf16[256,1024]{1,0:T(8,128)(2,1)}, u32[]{:S(2)}, u32[]{:S(2)}) collective-permute-start(bf16[256,1024]{1,0:T(8,128)(2,1)S(1)} %get-tuple-element.101), channel_id=1, source_target_pairs={{0,2},{2,4},{4,6},{6,0},{1,3},{3,5},{5,7},{7,1},{8,10},{10,12},{12... | collective-permute-start | bytes 1572872 | tf_op jit(solution)/shard_map/ppermute | solution.py:59
  148.9 27.3 %collective-permute-start.12 = (bf16[256,1024]{1,0:T(8,128)(2,1)}, bf16[256,1024]{1,0:T(8,128)(2,1)}, u32[]{:S(2)}, u32[]{:S(2)}) collective-permute-start(bf16[256,1024]{1,0:T(8,128)(2,1)} %get-tuple-element.102), channel_id=1, source_target_pairs={{0,4},{2,6},{4,0},{6,2},{1,5},{3,7},{5,1},{7,3},{8,12},{10,14},{12... | collective-permute-start | bytes 1572872 | tf_op jit(solution)/shard_map/ppermute | solution.py:59
  150.4 26.2 %collective-permute-start.11 = (bf16[256,1024]{1,0:T(8,128)(2,1)}, bf16[256,1024]{1,0:T(8,128)(2,1)}, u32[]{:S(2)}, u32[]{:S(2)}) collective-permute-start(bf16[256,1024]{1,0:T(8,128)(2,1)} %get-tuple-element.103), channel_id=1, source_target_pairs={{0,6},{2,0},{4,2},{6,4},{1,7},{3,1},{5,3},{7,5},{8,14},{10,8},{12,... | collective-permute-start | bytes 1572872 | tf_op jit(solution)/shard_map/ppermute | solution.py:59
  154.1 33.2 %collective-permute-start.18 = (bf16[256,1024]{1,0:T(8,128)(2,1)}, bf16[256,1024]{1,0:T(8,128)(2,1)S(1)}, u32[]{:S(2)}, u32[]{:S(2)}) collective-permute-start(bf16[256,1024]{1,0:T(8,128)(2,1)} %slice.399.g_ref), channel_id=1, source_target_pairs={{0,2},{2,4},{4,6},{6,0},{1,3},{3,5},{5,7},{7,1},{8,10},{10,12},{12... | collective-permute-start | bytes 1572872 | tf_op jit(solution)/shard_map/ppermute | solution.py:59
  176.2 15.1 %collective-permute-start.15 = (bf16[256,1024]{1,0:T(8,128)(2,1)}, bf16[256,1024]{1,0:T(8,128)(2,1)S(1)}, u32[]{:S(2)}, u32[]{:S(2)}) collective-permute-start(bf16[256,1024]{1,0:T(8,128)(2,1)} %slice.399.g_ref), channel_id=1, source_target_pairs={{0,6},{2,0},{4,2},{6,4},{1,7},{3,1},{5,3},{7,5},{8,14},{10,8},{12,... | collective-permute-start | bytes 1572872 | tf_op jit(solution)/shard_map/ppermute | solution.py:59
  180.3 33.4 %collective-permute-start.17 = (bf16[256,1024]{1,0:T(8,128)(2,1)}, bf16[256,1024]{1,0:T(8,128)(2,1)}, u32[]{:S(2)}, u32[]{:S(2)}) collective-permute-start(bf16[256,1024]{1,0:T(8,128)(2,1)} %get-tuple-element.74.b_ref), channel_id=1, source_target_pairs={{0,2},{2,4},{4,6},{6,0},{1,3},{3,5},{5,7},{7,1},{8,10},{10,12},{12... | collective-permute-start | bytes 1572872 | tf_op jit(solution)/shard_map/ppermute | solution.py:59
  181.9 33.9 %collective-permute-start.14 = (bf16[256,1024]{1,0:T(8,128)(2,1)}, bf16[256,1024]{1,0:T(8,128)(2,1)}, u32[]{:S(2)}, u32[]{:S(2)}) collective-permute-start(bf16[256,1024]{1,0:T(8,128)(2,1)} %get-tuple-element.74.b_ref), channel_id=1, source_target_pairs={{0,6},{2,0},{4,2},{6,4},{1,7},{3,1},{5,3},{7,5},{8,14},{10,8},{12,... | collective-permute-start | bytes 1572872 | tf_op jit(solution)/shard_map/ppermute | solution.py:59
  188.0 15.9 %collective-permute-start.23 = (bf16[128,1024]{1,0:T(8,128)(2,1)}, bf16[128,1024]{1,0:T(8,128)(2,1)}, u32[]{:S(2)}, u32[]{:S(2)}) collective-permute-start(bf16[128,1024]{1,0:T(8,128)(2,1)} %slice.403), channel_id=1, source_target_pairs={{0,2},{2,4},{4,6},{6,0},{1,3},{3,5},{5,7},{7,1},{8,10},{10,12},{12... | collective-permute-start | bytes 786440 | tf_op jit(solution)/shard_map/ppermute | solution.py:59
  191.3 22.4 %copy-start = (bf16[256,1024]{1,0:T(8,128)(2,1)}, bf16[256,1024]{1,0:T(8,128)(2,1)S(1)}, u32[]{:S(2)}) copy-start(bf16[256,1024]{1,0:T(8,128)(2,1)S(1)} %collective-permute-done.15.g_ref) | copy-start | bytes 1572868
  192.0 14.5 %collective-permute-start.22 = (bf16[128,1024]{1,0:T(8,128)(2,1)}, bf16[128,1024]{1,0:T(8,128)(2,1)}, u32[]{:S(2)}, u32[]{:S(2)}) collective-permute-start(bf16[128,1024]{1,0:T(8,128)(2,1)} %slice.402), channel_id=1, source_target_pairs={{0,6},{2,0},{4,2},{6,4},{1,7},{3,1},{5,3},{7,5},{8,14},{10,8},{12,... | collective-permute-start | bytes 786440 | tf_op jit(solution)/shard_map/ppermute | solution.py:59
  215.4 17.6 %collective-permute-start.21 = (bf16[128,1024]{1,0:T(8,128)(2,1)}, bf16[128,1024]{1,0:T(8,128)(2,1)S(1)}, u32[]{:S(2)}, u32[]{:S(2)}) collective-permute-start(bf16[128,1024]{1,0:T(8,128)(2,1)} %slice.401), channel_id=1, source_target_pairs={{0,2},{2,4},{4,6},{6,0},{1,3},{3,5},{5,7},{7,1},{8,10},{10,12},{12... | collective-permute-start | bytes 786440 | tf_op jit(solution)/shard_map/ppermute | solution.py:59
  217.5 14.7 %collective-permute-start.20 = (bf16[128,1024]{1,0:T(8,128)(2,1)}, bf16[128,1024]{1,0:T(8,128)(2,1)S(1)}, u32[]{:S(2)}, u32[]{:S(2)}) collective-permute-start(bf16[128,1024]{1,0:T(8,128)(2,1)} %slice.400), channel_id=1, source_target_pairs={{0,6},{2,0},{4,2},{6,4},{1,7},{3,1},{5,3},{7,5},{8,14},{10,8},{12,... | collective-permute-start | bytes 786440 | tf_op jit(solution)/shard_map/ppermute | solution.py:59
  274.8 74.2 %collective-permute-start.24 = (bf16[256,1024]{1,0:T(8,128)(2,1)}, bf16[256,1024]{1,0:T(8,128)(2,1)}, u32[]{:S(2)}, u32[]{:S(2)}) collective-permute-start(bf16[256,1024]{1,0:T(8,128)(2,1)} %get-tuple-element.43), channel_id=1, source_target_pairs={{0,4},{2,6},{4,0},{6,2},{1,5},{3,7},{5,1},{7,3},{8,12},{10,14},{12... | collective-permute-start | bytes 1572872 | tf_op jit(solution)/shard_map/ppermute | solution.py:59
  274.8 54.8 %collective-permute-start.27 = (bf16[256,1024]{1,0:T(8,128)(2,1)}, bf16[256,1024]{1,0:T(8,128)(2,1)}, u32[]{:S(2)}, u32[]{:S(2)}) collective-permute-start(bf16[256,1024]{1,0:T(8,128)(2,1)} %get-tuple-element.47), channel_id=1, source_target_pairs={{0,4},{2,6},{4,0},{6,2},{1,5},{3,7},{5,1},{7,3},{8,12},{10,14},{12... | collective-permute-start | bytes 1572872 | tf_op jit(solution)/shard_map/ppermute | solution.py:59
  318.1 30.9 %collective-permute-start.19 = (bf16[256,1024]{1,0:T(8,128)(2,1)}, bf16[256,1024]{1,0:T(8,128)(2,1)}, u32[]{:S(2)}, u32[]{:S(2)}) collective-permute-start(bf16[256,1024]{1,0:T(8,128)(2,1)} %copy-done.12), channel_id=1, source_target_pairs={{0,6},{2,0},{4,2},{6,4},{1,7},{3,1},{5,3},{7,5},{8,14},{10,8},{12,... | collective-permute-start | bytes 1572872 | tf_op jit(solution)/shard_map/ppermute | solution.py:59
  318.4 22.3 %collective-permute-start.26 = (bf16[256,1024]{1,0:T(8,128)(2,1)}, bf16[256,1024]{1,0:T(8,128)(2,1)S(1)}, u32[]{:S(2)}, u32[]{:S(2)}) collective-permute-start(bf16[256,1024]{1,0:T(8,128)(2,1)} %copy-done.15), channel_id=1, source_target_pairs={{0,6},{2,0},{4,2},{6,4},{1,7},{3,1},{5,3},{7,5},{8,14},{10,8},{12,... | collective-permute-start | bytes 1572872 | tf_op jit(solution)/shard_map/ppermute | solution.py:59
  318.7 22.0 %collective-permute-start.25 = (bf16[256,1024]{1,0:T(8,128)(2,1)}, bf16[256,1024]{1,0:T(8,128)(2,1)S(1)}, u32[]{:S(2)}, u32[]{:S(2)}) collective-permute-start(bf16[256,1024]{1,0:T(8,128)(2,1)} %copy-done.16), channel_id=1, source_target_pairs={{0,2},{2,4},{4,6},{6,0},{1,3},{3,5},{5,7},{7,1},{8,10},{10,12},{12... | collective-permute-start | bytes 1572872 | tf_op jit(solution)/shard_map/ppermute | solution.py:59
  329.6 19.4 %collective-permute-start.16 = (bf16[256,1024]{1,0:T(8,128)(2,1)S(1)}, bf16[256,1024]{1,0:T(8,128)(2,1)S(1)}, u32[]{:S(2)}, u32[]{:S(2)}) collective-permute-start(bf16[256,1024]{1,0:T(8,128)(2,1)S(1)} %copy-done.14), channel_id=1, source_target_pairs={{0,2},{2,4},{4,6},{6,0},{1,3},{3,5},{5,7},{7,1},{8,10},{10,12},{12... | collective-permute-start | bytes 1572872 | tf_op jit(solution)/shard_map/ppermute | solution.py:59
  345.6 39.1 %collective-permute-start.30 = (bf16[256,1024]{1,0:T(8,128)(2,1)}, bf16[256,1024]{1,0:T(8,128)(2,1)}, u32[]{:S(2)}, u32[]{:S(2)}) collective-permute-start(bf16[256,1024]{1,0:T(8,128)(2,1)} %get-tuple-element.76), channel_id=1, source_target_pairs={{0,2},{2,4},{4,6},{6,0},{1,3},{3,5},{5,7},{7,1},{8,10},{10,12},{12... | collective-permute-start | bytes 1572872 | tf_op jit(solution)/shard_map/ppermute | solution.py:59
  345.8 40.8 %collective-permute-start.28 = (bf16[256,1024]{1,0:T(8,128)(2,1)}, bf16[256,1024]{1,0:T(8,128)(2,1)}, u32[]{:S(2)}, u32[]{:S(2)}) collective-permute-start(bf16[256,1024]{1,0:T(8,128)(2,1)} %get-tuple-element.76), channel_id=1, source_target_pairs={{0,6},{2,0},{4,2},{6,4},{1,7},{3,1},{5,3},{7,5},{8,14},{10,8},{12,... | collective-permute-start | bytes 1572872 | tf_op jit(solution)/shard_map/ppermute | solution.py:59
  353.7 160.1 %all-to-all-start.3 = ((bf16[128,2,1024]{2,1,0:T(2,128)(2,1)}), bf16[128,2,1024]{2,1,0:T(2,128)(2,1)}, u32[]{:S(2)}, u32[]{:S(2)}) async-start(bf16[128,2,1024]{2,1,0:T(2,128)(2,1)} %reshape.770), calls=%async_computation.3 | async-start | bytes 1048576 | tf_op jit(solution)/shard_map/all_to_all | solution.py:465
  385.7 14.0 %collective-permute-start.31 = (bf16[128,1024]{1,0:T(8,128)(2,1)S(1)}, bf16[128,1024]{1,0:T(8,128)(2,1)S(1)}, u32[]{:S(2)}, u32[]{:S(2)}) collective-permute-start(bf16[128,1024]{1,0:T(8,128)(2,1)S(1)} %slice.406), channel_id=1, source_target_pairs={{0,2},{2,4},{4,6},{6,0},{1,3},{3,5},{5,7},{7,1},{8,10},{10,12},{12... | collective-permute-start | bytes 786440 | tf_op jit(solution)/shard_map/ppermute | solution.py:59
  387.6 11.3 %collective-permute-start.29 = (bf16[128,1024]{1,0:T(8,128)(2,1)S(1)}, bf16[128,1024]{1,0:T(8,128)(2,1)S(1)}, u32[]{:S(2)}, u32[]{:S(2)}) collective-permute-start(bf16[128,1024]{1,0:T(8,128)(2,1)S(1)} %slice.405), channel_id=1, source_target_pairs={{0,6},{2,0},{4,2},{6,4},{1,7},{3,1},{5,3},{7,5},{8,14},{10,8},{12,... | collective-permute-start | bytes 786440 | tf_op jit(solution)/shard_map/ppermute | solution.py:59
  397.0 145.2 %collective-permute-start.38 = (bf16[3,4,2,64,2,512]{5,4,3,2,1,0:T(2,128)(2,1)}, bf16[3,4,2,64,2,512]{5,4,3,2,1,0:T(2,128)(2,1)}, u32[]{:S(2)}, u32[]{:S(2)}) collective-permute-start(bf16[3,4,2,64,2,512]{5,4,3,2,1,0:T(2,128)(2,1)} %dynamic-slice_bitcast_fusion), channel_id=1, source_target_pairs={{0,8},{8,0},{1,9},{9,1},{2,10},{10,2},{3,11},{11,3},{4,12},{12,4},... | collective-permute-start | bytes 9437192 | tf_op jit(solution)/shard_map/ppermute | solution.py:63
  404.8 4.5 collective-permute-start.32
  461.9 2.8 collective-permute-start.33
  478.1 26.8 %collective-permute-start.34 = (bf16[256,1024]{1,0:T(8,128)(2,1)S(1)}, bf16[256,1024]{1,0:T(8,128)(2,1)S(1)}, u32[]{:S(2)}, u32[]{:S(2)}) collective-permute-start(bf16[256,1024]{1,0:T(8,128)(2,1)S(1)} %get-tuple-element.95), channel_id=1, source_target_pairs={{0,2},{2,4},{4,6},{6,0},{1,3},{3,5},{5,7},{7,1},{8,10},{10,12},{12... | collective-permute-start | bytes 1572872 | tf_op jit(solution)/shard_map/ppermute | solution.py:59
  478.1 26.7 %collective-permute-start.36 = (bf16[256,1024]{1,0:T(8,128)(2,1)S(1)}, bf16[256,1024]{1,0:T(8,128)(2,1)S(1)}, u32[]{:S(2)}, u32[]{:S(2)}) collective-permute-start(bf16[256,1024]{1,0:T(8,128)(2,1)S(1)} %get-tuple-element.96), channel_id=1, source_target_pairs={{0,4},{2,6},{4,0},{6,2},{1,5},{3,7},{5,1},{7,3},{8,12},{10,14},{12... | collective-permute-start | bytes 1572872 | tf_op jit(solution)/shard_map/ppermute | solution.py:59
  480.5 25.0 %collective-permute-start.35 = (bf16[256,1024]{1,0:T(8,128)(2,1)S(1)}, bf16[256,1024]{1,0:T(8,128)(2,1)S(1)}, u32[]{:S(2)}, u32[]{:S(2)}) collective-permute-start(bf16[256,1024]{1,0:T(8,128)(2,1)S(1)} %get-tuple-element.97), channel_id=1, source_target_pairs={{0,6},{2,0},{4,2},{6,4},{1,7},{3,1},{5,3},{7,5},{8,14},{10,8},{12,... | collective-permute-start | bytes 1572872 | tf_op jit(solution)/shard_map/ppermute | solution.py:59
  483.8 23.7 %copy-start.43 = (bf16[4,4,2,2,64,2,128]{6,5,4,3,2,1,0:T(2,128)(2,1)}, bf16[4,4,2,2,64,2,128]{6,5,4,3,2,1,0:T(2,128)(2,1)S(1)}, u32[]{:S(2)}) copy-start(bf16[4,4,2,2,64,2,128]{6,5,4,3,2,1,0:T(2,128)(2,1)S(1)} %constant_dynamic-update-slice_fusion.10) | copy-start | bytes 6291460
  486.1 36.8 %collective-permute-start.37 = (bf16[4,4,2,64,2,128]{5,4,3,2,1,0:T(2,128)(2,1)}, bf16[4,4,2,64,2,128]{5,4,3,2,1,0:T(2,128)(2,1)}, u32[]{:S(2)}, u32[]{:S(2)}) collective-permute-start(bf16[4,4,2,64,2,128]{5,4,3,2,1,0:T(2,128)(2,1)} %dynamic-slice_bitcast_fusion.1), channel_id=1, source_target_pairs={{0,8},{8,0},{1,9},{9,1},{2,10},{10,2},{3,11},{11,3},{4,12},{12,4},... | collective-permute-start | bytes 3145736 | tf_op jit(solution)/shard_map/ppermute | solution.py:63
  513.8 24.7 %all-to-all-start.4 = ((bf16[128,2,1408]{2,1,0:T(2,128)(2,1)}), bf16[128,2,1408]{2,1,0:T(2,128)(2,1)S(1)}, u32[]{:S(2)}, u32[]{:S(2)}) async-start(bf16[128,2,1408]{2,1,0:T(2,128)(2,1)} %pad_maximum_fusion.7), calls=%async_computation.4 | async-start | bytes 1441792 | tf_op jit(solution)/shard_map/all_to_all | solution.py:478
  538.5 21.2 %all-to-all-start.5 = ((bf16[16,4,64,128]{3,2,1,0:T(8,128)(2,1)}), bf16[16,4,64,128]{3,2,1,0:T(8,128)(2,1)S(1)}, u32[]{:S(2)}, u32[]{:S(2)}) async-start(bf16[16,4,64,128]{3,2,1,0:T(8,128)(2,1)} %bitcast.64), calls=%async_computation.5 | async-start | bytes 2097152 | tf_op jit(solution)/shard_map/all_to_all | solution.py:107
  560.8 43.8 %all-to-all-start.6 = ((bf16[16,3,64,512]{3,2,1,0:T(8,128)(2,1)}), bf16[16,3,64,512]{3,2,1,0:T(8,128)(2,1)S(1)}, u32[]{:S(2)}, u32[]{:S(2)}) async-start(bf16[16,3,64,512]{3,2,1,0:T(8,128)(2,1)} %bitcast.74), calls=%async_computation.6 | async-start | bytes 6291456 | tf_op jit(solution)/shard_map/all_to_all | solution.py:107
  (80 other events, 469.4 us)

commit v2 on v1

v2 whole, which is shorter than its diff:
```python
import functools

import jax
import jax.numpy as jnp
from jax import lax
from jax.experimental import pallas as pl
from jax.experimental.pallas import tpu as pltpu
from jax.sharding import Mesh
from jax.sharding import PartitionSpec as P

HEADS = 16
HEAD_DIM = 64
HALF = HEAD_DIM // 2
D = 1024
FF = 4096
ROWS = 256
RING = 4
PLANE = ROWS * RING
GROUP = 2 * PLANE
DEVICES = 128
VARIATES = 8
SEQS = 4
WIDE = 128
EPS = 1e-06
THETA = 10000.0
LOG2E = 1.4426950408889634
FAR = -16384.0
F32 = jnp.float32
BF16 = jnp.bfloat16

ALL = ("x", "zh", "core", "y", "zl")
FLAT = ("x", "zh", "zl")
NT = (((1,), (1,)), ((), ()))
TN = (((0,), (0,)), ((), ()))


def mm(left, right, dims=(((1,), (0,)), ((), ()))):
    return lax.dot_general(left, right, dims, preferred_element_type=F32)


def root_stats(values):
    return lax.rsqrt(jnp.mean(values * values, axis=-1, keepdims=True) + EPS)


def norm_back(grad_in, normed, scale_inv):
    return scale_inv * (grad_in - normed * jnp.mean(grad_in * normed, axis=-1, keepdims=True))


def pieces(values, count):
    out = []
    for _ in range(count):
        part = lax.reduce_precision(values, 8, 7)
        out.append(part.astype(BF16))
        values = values - part
    return out


def ring(values, step):
    return lax.ppermute(values, "y", [(i, (i + step) % RING) for i in range(RING)])


def swap_core(values):
    return lax.ppermute(values, "core", [(0, 1), (1, 0)])


def gather_ring(values):
    ahead = ring(values, -1)
    behind = ring(values, 1)
    half = values.shape[0] // 2
    far_top = ring(ahead[:half], -1)
    far_low = ring(behind[half:], 1)
    return [values, ahead, jnp.concatenate([far_top, far_low], 0), behind]


def reduce_ring(parts):
    far = ring(parts[2], 2)
    near = ring(parts[1], 1)
    back = ring(parts[3], -1)
    return (
        parts[0].astype(F32) + near.astype(F32) + back.astype(F32) + far.astype(F32)
    )


def flat_gather(shard):
    many = jnp.broadcast_to(shard[None], (16,) + shard.shape)
    mine = lax.all_to_all(many, FLAT, 0, 0, tiled=True)
    return mine, swap_core(mine)


def assemble_kernel(core_ref, mine_ref, other_ref, out_ref, sems, *, depth, width):
    core = core_ref[0]
    copies = []
    for side, ref in enumerate((mine_ref, other_ref)):
        at = core if side == 0 else 1 - core
        for i in range(16):
            rows = pl.multiple_of((i // 2) * 2 * depth + at * depth, depth)
            target = out_ref.at[:, pl.ds(rows, depth), pl.ds((i % 2) * width, width)]
            copies.append(pltpu.make_async_copy(ref.at[i], target, sems.at[side, i]))
    for copy in copies:
        copy.start()
    for copy in copies:
        copy.wait()


def assemble(core, mine, other):
    _, kinds, depth, width = mine.shape
    anywhere = pl.BlockSpec(memory_space=pl.ANY)
    return pl.pallas_call(
        functools.partial(assemble_kernel, depth=depth, width=width),
        in_specs=[pl.BlockSpec(memory_space=pltpu.SMEM), anywhere, anywhere],
        out_specs=anywhere,
        out_shape=jax.ShapeDtypeStruct((kinds, 16 * depth, 2 * width), BF16),
        scratch_shapes=[pltpu.SemaphoreType.DMA((2, 16))],
        cost_estimate=pl.CostEstimate(
            flops=0, bytes_accessed=kinds * 128 * depth * width, transcendentals=0
        ),
    )(core, mine, other)


def grads_home(split):
    total = (split[0].astype(F32) + swap_core(split[1]).astype(F32)).astype(BF16)
    arrived = lax.all_to_all(total, FLAT, 0, 0, tiled=True)
    return jnp.sum(arrived.astype(F32), axis=0)


def weight_grad_kernel(core_ref, *refs, parts, switch):
    lefts, others, rights = refs[:parts], refs[parts : 2 * parts], refs[2 * parts : 3 * parts]
    out_ref = refs[3 * parts]
    core = core_ref[0]
    kind = pl.program_id(0)

    def work(sides):
        total = None
        for side, right in zip(sides, rights):
            part = mm(side[...], right[0], TN)
            total = part if total is None else total + part
        total = total.astype(BF16)
        depth = total.shape[0] // 16
        for p in range(8):
            for c in range(2):
                at = (2 * p + c) * depth
                out_ref[jnp.bitwise_xor(core, c), p, 0, 0] = total[at : at + depth]

    @pl.when(kind < switch)
    def _():
        work(lefts)

    @pl.when(kind >= switch)
    def _():
        work(others)


def weight_grads(core, lefts, others, rights, switch):
    parts = len(lefts)
    kinds, _, width = rights[0].shape
    half = width // 2
    sides = [pl.BlockSpec((v.shape[0], D), lambda k, z: (0, 0)) for v in list(lefts) + list(others)]
    moving = [pl.BlockSpec((1, v.shape[1], half), lambda k, z: (k, 0, z)) for v in rights]
    rows = sum(v.shape[1] for v in rights)
    out = pl.pallas_call(
        functools.partial(weight_grad_kernel, parts=parts, switch=switch),
        grid=(kinds, 2),
        in_specs=[pl.BlockSpec(memory_space=pltpu.SMEM)] + sides + moving,
        out_specs=pl.BlockSpec((2, 8, 1, 1, 64, half), lambda k, z: (0, 0, z, k, 0, 0)),
        out_shape=jax.ShapeDtypeStruct((2, 8, 2, kinds, 64, half), BF16),
        compiler_params=pltpu.CompilerParams(vmem_limit_bytes=48 * 2**20),
        cost_estimate=pl.CostEstimate(
            flops=2 * kinds * rows * D * width,
            bytes_accessed=2 * kinds * D * width + 4 * rows * D + 2 * kinds * rows * width,
            transcendentals=0,
        ),
    )(core, *lefts, *others, *rights)
    return out.reshape(2, 16, kinds, 64, half)


def lanes_of(shape):
    return lax.broadcasted_iota(jnp.int32, shape, 1)


def head_sums(values):
    wide = values.shape[1]
    row = lax.broadcasted_iota(jnp.int32, (wide, wide), 0) // HEAD_DIM
    same = (row == lanes_of((wide, wide)) // HEAD_DIM).astype(BF16)
    high = values.astype(BF16)
    low = (values - high.astype(F32)).astype(BF16)
    return mm(high, same) + mm(low, same)


def partner(values):
    wide = values.shape[1]
    first = lanes_of(values.shape) % HEAD_DIM < HALF
    return jnp.where(first, pltpu.roll(values, wide - HALF, 1), pltpu.roll(values, HALF, 1))


def angles_of(facts, freq_ref):
    facts = facts.astype(F32)
    times = facts[:, 2:3] * 32.0 + facts[:, 3:4]
    angle = times * freq_ref[0:1, :WIDE]
    first = lanes_of(angle.shape) % HEAD_DIM < HALF
    cosine = jnp.cos(angle)
    sine = jnp.sin(angle)
    sine = jnp.where(first, -sine, sine)
    return jnp.concatenate([cosine, cosine], 1), jnp.concatenate([sine, sine], 1)


def project_kernel(core_ref, a_ref, w_ref, freq_ref, mine_ref, send_ref, raw_ref):
    low = core_ref[0] == 0
    rows = a_ref[:, :D]
    cosine, sine = angles_of(a_ref[:, D:], freq_ref)

    def emit(kind, value):
        left, right = value[:, :WIDE], value[:, WIDE:]
        mine_ref[kind] = jnp.where(low, left, right).astype(BF16)
        send_ref[kind] = jnp.where(low, right, left).astype(BF16)

    for kind in range(2):
        raw = mm(rows, w_ref[kind])
        raw_ref[kind] = raw
        unit = raw * lax.rsqrt(head_sums(raw * raw) * (1.0 / HEAD_DIM) + EPS)
        value = unit * freq_ref[1 + kind : 2 + kind, :]
        value = value * cosine + partner(value) * sine
        if kind == 0:
            value = value * (HEAD_DIM ** (-0.5) * LOG2E)
        emit(kind, value)
    emit(2, mm(rows, w_ref[2]))


def project(core, rows_all, attn_w, freq):
    block = 512
    both = pl.BlockSpec((3, block, WIDE), lambda i: (0, i, 0))
    low = jax.ShapeDtypeStruct((3, PLANE, WIDE), BF16)
    return pl.pallas_call(
        project_kernel,
        grid=(PLANE // block,),
        in_specs=[
            pl.BlockSpec(memory_space=pltpu.SMEM),
            pl.BlockSpec((block, D + WIDE), lambda i: (i, 0)),
            pl.BlockSpec((3, D, 2 * WIDE), lambda i: (0, 0, 0)),
            pl.BlockSpec((8, 2 * WIDE), lambda i: (0, 0)),
        ],
        out_specs=[both, both, pl.BlockSpec((2, block, 2 * WIDE), lambda i: (0, i, 0))],
        out_shape=[low, low, jax.ShapeDtypeStruct((2, PLANE, 2 * WIDE), F32)],
        compiler_params=pltpu.CompilerParams(vmem_limit_bytes=48 * 2**20),
        cost_estimate=pl.CostEstimate(
            flops=8 * PLANE * D * 2 * WIDE, bytes_accessed=PLANE * D * 8, transcendentals=PLANE * 1024
        ),
    )(core, rows_all, attn_w, freq)


def unproject_kernel(
    core_ref, mine_ref, got_ref, raw_ref, facts_ref, w_ref, freq_ref, dp_ref, part_ref, gain_ref
):
    low = core_ref[0] == 0
    cosine, sine = angles_of(facts_ref[...], freq_ref)

    @pl.when(pl.program_id(0) == 0)
    def _():
        gain_ref[...] = jnp.zeros_like(gain_ref)

    total = None
    for kind in range(3):
        mine, got = mine_ref[kind], got_ref[kind]
        grad = jnp.concatenate([jnp.where(low, mine, got), jnp.where(low, got, mine)], 1)
        if kind < 2:
            grad = grad.astype(F32)
            if kind == 0:
                grad = grad * (HEAD_DIM ** (-0.5))
            raw = raw_ref[kind]
            inv = lax.rsqrt(head_sums(raw * raw) * (1.0 / HEAD_DIM) + EPS)
            unit = raw * inv
            grad = grad * cosine - partner(grad) * sine
            gain_ref[kind : kind + 1, :] += jnp.sum(grad * unit, axis=0, keepdims=True)
            scaled = grad * freq_ref[1 + kind : 2 + kind, :]
            mean = head_sums(scaled * unit) * (1.0 / HEAD_DIM)
            grad = (inv * (scaled - unit * mean)).astype(BF16)
        dp_ref[kind] = grad
        part = mm(grad, w_ref[kind], NT)
        total = part if total is None else total + part
    part_ref[...] = total.astype(BF16)


def unproject(core, mine, got, raw, rows_all, attn_w, freq):
    block = 512
    both = pl.BlockSpec((3, block, WIDE), lambda i: (0, i, 0))
    return pl.pallas_call(
        unproject_kernel,
        grid=(PLANE // block,),
        in_specs=[
            pl.BlockSpec(memory_space=pltpu.SMEM),
            both,
            both,
            pl.BlockSpec((2, block, 2 * WIDE), lambda i: (0, i, 0)),
            pl.BlockSpec((block, WIDE), lambda i: (i, D // WIDE)),
            pl.BlockSpec((3, D, 2 * WIDE), lambda i: (0, 0, 0)),
            pl.BlockSpec((8, 2 * WIDE), lambda i: (0, 0)),
        ],
        out_specs=[
            pl.BlockSpec((3, block, 2 * WIDE), lambda i: (0, i, 0)),
            pl.BlockSpec((block, D), lambda i: (i, 0)),
            pl.BlockSpec((8, 2 * WIDE), lambda i: (0, 0)),
        ],
        out_shape=[
            jax.ShapeDtypeStruct((3, PLANE, 2 * WIDE), BF16),
            jax.ShapeDtypeStruct((PLANE, D), BF16),
            jax.ShapeDtypeStruct((8, 2 * WIDE), F32),
        ],
        compiler_params=pltpu.CompilerParams(vmem_limit_bytes=48 * 2**20),
        cost_estimate=pl.CostEstimate(
            flops=8 * PLANE * D * 2 * WIDE, bytes_accessed=PLANE * D * 8, transcendentals=PLANE * 1024
        ),
    )(core, mine, got, raw, rows_all, attn_w, freq)


LOG_LANE = 3 * VARIATES + SEQS


def with_pieces(base, values, first_lane, lanes):
    for i in range(3):
        part = values.astype(BF16).astype(F32)
        base = jnp.where(lanes == first_lane + i, part, base)
        values = values - part
    return base


def attend_kernel(qkv_ref, all_ref, qt_ref, kt_ref, vt_ref, att_ref, low_ref, tail_ref, *, chunks):
    size = all_ref.shape[1] // chunks
    query = jnp.concatenate([qkv_ref[0], qt_ref[...]], 1)
    zero = jnp.zeros_like(query)
    head_of = (lanes_of(query.shape) // HEAD_DIM) % 2
    lanes = lanes_of((query.shape[0], WIDE))
    out = None
    tail = qt_ref[...].astype(F32)
    for head in range(2):
        masked = jnp.where(head_of == head, query, zero)
        total = None
        for c in range(chunks):
            rows = pl.ds(c * size, size)
            keys = jnp.concatenate([all_ref[1, rows, :], kt_ref[rows, :]], 1)
            values = jnp.concatenate([all_ref[2, rows, :], vt_ref[rows, :]], 1)
            prob = jnp.exp2(mm(masked, keys, NT)).astype(BF16)
            part = mm(prob, values)
            total = part if total is None else total + part
        row_sum = total[:, WIDE : WIDE + 1]
        here = total[:, :WIDE] / row_sum
        out = here if head == 0 else jnp.where(lanes < HEAD_DIM, out, here)
        tail = with_pieces(tail, -jnp.log2(row_sum), head * HEAD_DIM + LOG_LANE, lanes)
    att_ref[...] = out
    low_ref[...] = out.astype(BF16)
    tail_ref[...] = tail.astype(BF16)


def attend(qkv, query_tail, key_tail, value_tail):
    block = 512
    rows = qkv.shape[1]
    moving = pl.BlockSpec((block, WIDE), lambda i: (i, 0))
    fixed = pl.BlockSpec((rows, WIDE), lambda i: (0, 0))
    low = jax.ShapeDtypeStruct((rows, WIDE), BF16)
    return pl.pallas_call(
        functools.partial(attend_kernel, chunks=4),
        grid=(rows // block,),
        in_specs=[
            pl.BlockSpec((1, block, WIDE), lambda i: (0, i, 0)),
            pl.BlockSpec((3, rows, WIDE), lambda i: (0, 0, 0)),
            moving,
            fixed,
            fixed,
        ],
        out_specs=[moving, moving, moving],
        out_shape=[jax.ShapeDtypeStruct((rows, WIDE), F32), low, low],
        compiler_params=pltpu.CompilerParams(vmem_limit_bytes=48 * 2**20),
        cost_estimate=pl.CostEstimate(
            flops=16 * rows * rows * WIDE, bytes_accessed=rows * WIDE * 24, transcendentals=2 * rows * rows
        ),
    )(qkv, qkv, query_tail, key_tail, value_tail)


def attend_back_kernel(
    qkv_ref, all_ref, qt_ref, kt_ref, vt_ref, hot_ref, grad_ref, att_ref,
    dq_ref, dk_ref, dv_ref, bias_ref, dk_sum, dv_sum, *, chunks
):
    size = all_ref.shape[1] // chunks
    step = pl.program_id(0)
    query = jnp.concatenate([qkv_ref[0], qt_ref[...]], 1)
    grad = grad_ref[...]
    zero = jnp.zeros_like(query)
    head_of = (lanes_of(query.shape) // HEAD_DIM) % 2
    lanes = lanes_of((query.shape[0], WIDE))
    overlap = grad.astype(F32) * att_ref[...]

    @pl.when(step == 0)
    def _():
        dk_sum[...] = jnp.zeros_like(dk_sum)
        dv_sum[...] = jnp.zeros_like(dv_sum)

    out = None
    for head in range(2):
        mine = head_of[:, :WIDE] == head
        masked = jnp.where(head_of == head, query, zero)
        grad_here = jnp.where(mine, grad, zero[:, :WIDE])
        dots = jnp.sum(jnp.where(mine, overlap, 0.0), axis=1, keepdims=True)
        extra = with_pieces(jnp.zeros(lanes.shape, F32), -dots, 0, lanes).astype(BF16)
        grad_wide = jnp.concatenate([grad_here, extra], 1)
        total = None
        for c in range(chunks):
            rows = pl.ds(c * size, size)
            keys = all_ref[1, rows, :]
            prob = jnp.exp2(mm(jnp.concatenate([keys, kt_ref[rows, :]], 1), masked, NT))
            slope = mm(jnp.concatenate([all_ref[2, rows, :], vt_ref[rows, :]], 1), grad_wide, NT)
            d_score = (prob * slope).astype(BF16)
            dv_sum[rows, :] += mm(prob.astype(BF16), grad_here)
            dk_sum[rows, :] += mm(d_score, masked)
            part = mm(d_score, keys, TN)
            total = part if total is None else total + part
        out = total if head == 0 else jnp.where(lanes < HEAD_DIM, out, total)
    dq_ref[...] = out.astype(BF16)

    @pl.when(step == pl.num_programs(0) - 1)
    def _():
        dk_ref[...] = (dk_sum[:, :WIDE] * (1.0 / LOG2E)).astype(BF16)
        dv_ref[...] = dv_sum[...].astype(BF16)
        counts = dk_sum[:, WIDE:]
        bias_ref[...] = jnp.zeros_like(bias_ref)
        bias_ref[0:1, :] = jnp.sum(counts * hot_ref[...].astype(F32), axis=0, keepdims=True)
        bias_ref[1:2, :] = jnp.sum(counts, axis=0, keepdims=True)


def attend_back(qkv, query_tail, key_tail, value_tail, query_hot, grad, attended):
    block = 512
    rows = qkv.shape[1]
    moving = pl.BlockSpec((block, WIDE), lambda i: (i, 0))
    fixed = pl.BlockSpec((rows, WIDE), lambda i: (0, 0))
    low = jax.ShapeDtypeStruct((rows, WIDE), BF16)
    return pl.pallas_call(
        functools.partial(attend_back_kernel, chunks=4),
        grid=(rows // block,),
        in_specs=[
            pl.BlockSpec((1, block, WIDE), lambda i: (0, i, 0)),
            pl.BlockSpec((3, rows, WIDE), lambda i: (0, 0, 0)),
            moving,
            fixed,
            fixed,
            fixed,
            moving,
            moving,
        ],
        out_specs=[moving, fixed, fixed, pl.BlockSpec((8, WIDE), lambda i: (0, 0))],
        out_shape=[low, low, low, jax.ShapeDtypeStruct((8, WIDE), F32)],
        scratch_shapes=[pltpu.VMEM((rows, 2 * WIDE), F32), pltpu.VMEM((rows, WIDE), F32)],
        compiler_params=pltpu.CompilerParams(vmem_limit_bytes=48 * 2**20),
        cost_estimate=pl.CostEstimate(
            flops=40 * rows * rows * WIDE, bytes_accessed=rows * WIDE * 24, transcendentals=2 * rows * rows
        ),
    )(qkv, qkv, query_tail, key_tail, value_tail, query_hot, grad, attended)


def feed_kernel(b_ref, g_ref, w_ref, y_ref, db_ref, act_ref, y_sum, db_sum):
    step = pl.program_id(0)
    rows = b_ref[...]
    gate_w, up_w, down_w = w_ref[0], w_ref[1], w_ref[2]
    gate = mm(rows, gate_w)
    up = mm(rows, up_w)
    d_hidden = mm(g_ref[...], down_w)
    sig = 1.0 / (1.0 + jnp.exp(-gate))
    silu = gate * sig
    hidden = (silu * up).astype(BF16)
    d_gate = (d_hidden * up * (sig * (1.0 + gate * (1.0 - sig)))).astype(BF16)
    d_up = (d_hidden * silu).astype(BF16)
    act_ref[0] = d_gate
    act_ref[1] = d_up
    act_ref[2] = hidden
    y_part = mm(hidden, down_w, NT)
    db_part = mm(d_gate, gate_w, NT) + mm(d_up, up_w, NT)

    @pl.when(step == 0)
    def _():
        y_sum[...] = y_part
        db_sum[...] = db_part

    @pl.when(step > 0)
    def _():
        y_sum[...] += y_part
        db_sum[...] += db_part

    @pl.when(step == pl.num_programs(0) - 1)
    def _():
        y_ref[...] = y_sum[...].astype(BF16)
        db_ref[...] = db_sum[...].astype(BF16)


def feed(rows_b, rows_g, weights):
    rows = rows_b.shape[0]
    width = weights.shape[2]
    block = 256
    whole = pl.BlockSpec((rows, D), lambda f: (0, 0))
    part = pl.BlockSpec((3, rows, block), lambda f: (0, 0, f))
    low_d = jax.ShapeDtypeStruct((rows, D), BF16)
    low_f = jax.ShapeDtypeStruct((3, rows, width), BF16)
    return pl.pallas_call(
        feed_kernel,
        grid=(width // block,),
        in_specs=[whole, whole, pl.BlockSpec((3, D, block), lambda f: (0, 0, f))],
        out_specs=[whole, whole, part],
        out_shape=[low_d, low_d, low_f],
        scratch_shapes=[pltpu.VMEM((rows, D), F32)] * 2,
        compiler_params=pltpu.CompilerParams(vmem_limit_bytes=48 * 2**20),
        cost_estimate=pl.CostEstimate(
            flops=12 * rows * D * width, bytes_accessed=6 * D * width + rows * D * 8 + rows * width * 6,
            transcendentals=rows * width,
        ),
    )(rows_b, rows_g, weights)


def body(
    tokens,
    cotangent,
    destination,
    variate_ids,
    time_ids,
    seq_lengths,
    qkv_weight,
    out_weight,
    gate_up_weight,
    down_weight,
    norm_gains,
    qk_gains,
    variate_bias,
):
    core = lax.axis_index("core")
    low_core = core == 0
    y_at = lax.axis_index("y")
    zl_at = lax.axis_index("zl")

    core_scalar = core.reshape(1).astype(jnp.int32)

    def side_by_side(mine, other):
        return jnp.concatenate(
            [jnp.where(low_core, mine, other), jnp.where(low_core, other, mine)], axis=-1
        )

    slot = destination % ROWS
    group_at = destination // GROUP
    block_at = (destination % GROUP) // ROWS
    device_at = ((group_at // 2) * 2 + block_at // 4) * 8 + (block_at % 4) * 2 + group_at % 2
    key = device_at * ROWS + slot
    rank = jnp.sum((key[None, :] < key[:, None]).astype(jnp.int32), axis=1)
    deal = (jnp.arange(ROWS)[:, None] == rank[None, :]).astype(BF16)
    facts = jnp.stack([slot, variate_ids, time_ids // 32, time_ids % 32], axis=1).astype(BF16)
    facts = jnp.concatenate([facts, jnp.zeros((ROWS, WIDE - 4), BF16)], axis=1)
    gains_row = jnp.broadcast_to(norm_gains.reshape(1, WIDE), (ROWS, WIDE))
    outgoing = jnp.concatenate([tokens, cotangent, facts, gains_row], axis=1)
    span = outgoing.shape[1]
    outgoing = mm(deal, outgoing).astype(BF16).reshape(DEVICES, 2, span)
    arrived = lax.all_to_all(outgoing, ALL, 0, 0, tiled=True)

    attn_shard = jnp.concatenate([qkv_weight, out_weight.T[None]], 0)
    feed_shard = jnp.concatenate([gate_up_weight, down_weight.T[None]], 0)
    attn_shard, arrived = lax.optimization_barrier((attn_shard, arrived))
    attn_mine, attn_other = flat_gather(attn_shard)
    attn_w = assemble(core_scalar, attn_mine, attn_other)
    feed_shard, attn_other = lax.optimization_barrier((feed_shard, attn_other))
    feed_mine, feed_other = flat_gather(feed_shard)
    feed_w = assemble(core_scalar, feed_mine, feed_other)

    lengths_other = swap_core(seq_lengths)
    lengths = jnp.where(zl_at == core, seq_lengths, lengths_other)[0]
    bias_other = lax.ppermute(variate_bias, "zl", [(0, 1), (1, 0)])
    bias_pair = jnp.where(zl_at == core, variate_bias, bias_other)

    all_gains = arrived[:, 0, span - WIDE :].reshape(16, 8, 2, 64)[:, 0]
    all_gains = all_gains.transpose(1, 0, 2).reshape(2, D).astype(F32)
    gain_one, gain_two = all_gains[0], all_gains[1]
    slots = arrived[:, :, 2 * D].reshape(2 * DEVICES)
    place = (jnp.arange(ROWS).astype(BF16)[:, None] == slots[None, :]).astype(BF16)
    placed = mm(place, arrived.reshape(2 * DEVICES, span))
    inputs = placed[:, :D]
    grad_rows = placed[:, D : 2 * D].astype(BF16)
    facts_here = placed[:, 2 * D : 2 * D + WIDE].astype(BF16)

    scale_one = root_stats(inputs)
    normed_one = inputs * scale_one
    attn_in = (normed_one * gain_one).astype(BF16)
    attn_all = gather_ring(jnp.concatenate([attn_in, facts_here], axis=1))
    attn_all = jnp.concatenate(attn_all, 0)
    grad_all = gather_ring(grad_rows)

    variates_own = attn_all[:, D + 1].astype(jnp.int32)
    variates = jnp.concatenate([variates_own, swap_core(variates_own)])
    blocks_y = (y_at + jnp.arange(RING)) % RING
    blocks = jnp.concatenate([core * RING + blocks_y, (1 - core) * RING + blocks_y])
    positions = (blocks[:, None] * ROWS + jnp.arange(ROWS)[None, :]).reshape(GROUP)
    segments = jnp.sum((positions[:, None] >= jnp.cumsum(lengths)[None, :]).astype(jnp.int32), 1)

    inverse = THETA ** (-2.0 * jnp.arange(HALF).astype(F32) / HEAD_DIM)
    freq = jnp.concatenate(
        [
            jnp.tile(inverse, 8)[None],
            jnp.tile(qk_gains, (1, 4)),
            jnp.zeros((5, 2 * WIDE), F32),
        ]
    )
    qkv_mine, qkv_send, raw = project(core_scalar, attn_all, attn_w, freq)
    qkv = jnp.concatenate([qkv_mine, swap_core(qkv_send)], axis=1)

    lane = jnp.arange(WIDE)[None, :]
    tail_lane = lane % HEAD_DIM
    bias_lane = tail_lane < 3 * VARIATES
    seg_lane = (tail_lane >= 3 * VARIATES) & (tail_lane < LOG_LANE)
    one_lane = (tail_lane >= LOG_LANE) & (tail_lane < LOG_LANE + 3)
    equal = bias_lane & (tail_lane % VARIATES == variates[:, None])
    inside = seg_lane & (tail_lane - 3 * VARIATES == segments[:, None])
    query_tail = (equal | inside).astype(BF16)
    bias_parts = jnp.stack(pieces(bias_pair * LOG2E, 3)).astype(F32)
    bias_rows = jnp.repeat(bias_parts, VARIATES, axis=0).transpose(1, 2, 0)
    bias_rows = jnp.pad(bias_rows, ((0, 0), (0, 0), (0, HEAD_DIM - 3 * VARIATES))).reshape(2, WIDE)
    key_tail = jnp.where(equal, bias_rows[0:1], bias_rows[1:2])
    key_tail = jnp.where(seg_lane, jnp.where(inside, 0.0, FAR), key_tail)
    key_tail = jnp.where(one_lane, 1.0, key_tail).astype(BF16)
    value_tail = jnp.broadcast_to((lane < 3).astype(BF16), (GROUP, WIDE))
    attended, att_low, query_back = attend(qkv, query_tail, key_tail, value_tail)
    att_plane = side_by_side(att_low[:PLANE], swap_core(att_low[PLANE:]))
    out_part = mm(att_plane, attn_w[3], NT).astype(BF16).reshape(RING, ROWS, D)
    hidden_one = inputs + reduce_ring([out_part[r] for r in range(RING)])

    scale_two = root_stats(hidden_one)
    normed_two = hidden_one * scale_two
    feed_in = (normed_two * gain_two).astype(BF16)
    feed_all = gather_ring(feed_in)
    fed = [feed(feed_all[r], grad_all[r], feed_w) for r in range(RING)]
    grad_normed_two = reduce_ring([f[1] for f in fed])
    mixed = (hidden_one + reduce_ring([f[0] for f in fed])).astype(BF16)

    feed_grad = grads_home(
        weight_grads(core_scalar, feed_all, grad_all, [f[2] for f in fed], 2)
    )

    gain_two_grad = jnp.sum(grad_normed_two * normed_two, axis=0)
    grad_one = grad_rows.astype(F32) + norm_back(grad_normed_two * gain_two, normed_two, scale_two)

    grad_one_all = jnp.concatenate(gather_ring(grad_one.astype(BF16)), 0)
    grad_att = mm(grad_one_all, attn_w[3]).astype(BF16)
    grad_left, grad_right = grad_att[:, :WIDE], grad_att[:, WIDE:]
    grad_send = jnp.where(low_core, grad_right, grad_left)
    grad_mine = jnp.where(low_core, grad_left, grad_right)
    grad_mine = jnp.concatenate([grad_mine, swap_core(grad_send)], 0)
    d_query, d_key, d_value, bias_sums = attend_back(
        qkv, query_back, key_tail, value_tail, query_tail, grad_mine, attended
    )
    first_part = (jnp.arange(HEAD_DIM) < VARIATES)[None, None]
    bias_sums = jnp.where(first_part, bias_sums[:2].reshape(2, 2, HEAD_DIM), 0.0)
    bias_sums = jnp.sum(bias_sums, axis=2)
    bias_part = jnp.stack([bias_sums[0], bias_sums[1] - bias_sums[0]])
    back_mixed = mm(place, mixed, TN).astype(BF16).reshape(DEVICES, 2, D)
    home_mixed = lax.all_to_all(back_mixed, ALL, 0, 0, tiled=True)
    d_mine = jnp.stack([d_query[:PLANE], d_key[:PLANE], d_value[:PLANE]])
    d_got = swap_core(jnp.stack([d_query[PLANE:], d_key[PLANE:], d_value[PLANE:]]))
    d_got, home_mixed = lax.optimization_barrier((d_got, home_mixed))
    grad_proj, in_part, qk_sums = unproject(
        core_scalar, d_mine, d_got, raw, attn_all, attn_w, freq
    )
    in_part = in_part.reshape(RING, ROWS, D)
    grad_normed_one = reduce_ring([in_part[r] for r in range(RING)])
    attn_grad = grads_home(
        weight_grads(
            core_scalar,
            [attn_all],
            [grad_one_all],
            [jnp.concatenate([grad_proj, att_plane[None]], 0)],
            3,
        )
    )
    qk_sums = jnp.sum(qk_sums[:2].reshape(2, 4, HEAD_DIM), axis=1)

    gain_one_grad = jnp.sum(grad_normed_one * normed_one, axis=0)
    input_grad = grad_one + norm_back(grad_normed_one * gain_one, normed_one, scale_one)

    new_tokens = mm(deal, home_mixed.reshape(ROWS, D), TN).astype(BF16)

    gain_sums = jnp.stack([gain_one_grad, gain_two_grad]).reshape(2, 16, 64).transpose(1, 0, 2)
    gain_sums = jnp.broadcast_to(gain_sums.reshape(16, 1, WIDE), (16, 8, WIDE))
    qk_row = qk_sums.reshape(WIDE)
    qk_row = jnp.broadcast_to(qk_row[None, None], (16, 8, WIDE))
    here = (jnp.arange(8) == y_at * 2 + core)[None, :, None]
    bias_row = jnp.where(here, bias_part.reshape(1, 1, 4), 0.0)
    bias_row = jnp.broadcast_to(bias_row, (16, 8, 4))
    smalls = jnp.concatenate([gain_sums, qk_row, bias_row, jnp.zeros((16, 8, WIDE - 4), F32)], axis=2)
    smalls = jnp.stack(pieces(smalls.reshape(DEVICES, 3 * WIDE), 2), axis=1)
    back_grads = mm(place, input_grad.astype(BF16), TN).astype(BF16).reshape(DEVICES, 2, D)
    home = lax.all_to_all(jnp.concatenate([back_grads, smalls], axis=2), ALL, 0, 0, tiled=True)
    token_grads = mm(deal, home[:, :, :D].reshape(ROWS, D), TN).astype(BF16)
    sums = jnp.sum(home[:, :, D:].astype(F32), axis=(0, 1))
    gains_grad = sums[:WIDE].reshape(2, 64)
    qk_grad = sums[WIDE : 2 * WIDE].reshape(2, 64)
    bias_grad = sums[2 * WIDE : 2 * WIDE + 4].reshape(2, 2)

    return (
        new_tokens,
        token_grads,
        attn_grad[:3],
        attn_grad[3].T,
        feed_grad[:2],
        feed_grad[2].T,
        gains_grad,
        qk_grad,
        bias_grad,
    )


def solution(mesh):
    fine = Mesh(mesh.devices.reshape(4, 2, 2, 4, 2), ALL)
    dp = ("x", "zh", "core")
    tensor = ("y", "zl")
    in_specs = (
        P(ALL, None),
        P(ALL, None),
        P(ALL),
        P(ALL),
        P(ALL),
        P(dp, None),
        P(None, dp, tensor),
        P(tensor, dp),
        P(None, dp, tensor),
        P(tensor, dp),
        P(None, dp),
        P(),
        P(None, tensor),
    )
    out_specs = (
        P(ALL, None),
        P(ALL, None),
        P(None, dp, tensor),
        P(tensor, dp),
        P(None, dp, tensor),
        P(tensor, dp),
        P(None, dp),
        P(),
        P(None, tensor),
    )
    return jax.shard_map(body, mesh=fine, in_specs=in_specs, out_specs=out_specs, check_vma=False)
```

time: 618 us -> 740 us (1.20)
  Pallas kernels: 68.6 us -> 357 us
  local copies, waits for them, and re-layouts: 198 us -> 70.4 us
  matrix products: 39.2 us -> 12.5 us
  other arithmetic: 61 us -> 40.6 us
    pallas_call x2 -> x8, Pallas kernels: 39.2 us -> 329 us  [the longest x2 257 us: assemble(): pl.pallas_call(functools.partial(assemble_kernel, depth=depth, width=widt...]
    concatenate x14 -> x4, local copies, waits for them, and re-layouts: 46 us -> 1.17 us  [the longest x2 0.99 us: gather_ring(): return [values, ahead, jnp.concatenate([far_top, far_low], 0), behind]]
    unnamed x179 -> x128, local copies, waits for them, and re-layouts: 41.3 us -> 22 us
    reshape x4 -> x3, local copies, waits for them, and re-layouts: 18.7 us -> 0.25 us  [the longest x1 0.09 us: body(): bias_rows = jnp.repeat(bias_parts, VARIATES, axis=0).transpose(1, 2, 0)]
    transpose x5 -> x0, local copies, waits for them, and re-layouts: 15.4 us -> none  [the longest x2 9.41 us: weights_of(): full.transpose(4, 1, 2, 0, 5, 3, 6).reshape(kinds, 16 * depth, 2 * width)]
    dot_general x4 -> x0, matrix products: 15.4 us -> none  [the longest x1 6.23 us: body(): jnp.einsum('gd,kgf->kdf', feed_rows, d_pair, preferred_element_type=F32)]
    all_to_all x2, waiting for transfers between devices: 1.94 us -> 13.7 us  [flat_gather(): mine = lax.all_to_all(many, FLAT, 0, 0, tiled=True)]
    transpose x5 -> x0, other arithmetic: 11.5 us -> none  [the longest x2 10.5 us: grads_home(): total = total.transpose(1, 2, 4, 0, 3, 5).reshape(16, kinds, depth, width)]
  transfers between devices with their start and end apart: 46 -> 46, of which waited for: 18 -> 22; matrix products, arithmetic and copies ran while one was open for 40% -> 13% of each run, Pallas kernels for 9% -> 22%
where the time goes in v2:
time: 740 us; the launch traced here: 727 us
  Pallas kernels  357 us (48%)
  waiting for transfers between devices  156 us (21%)
  starting transfers between devices  88.2 us (12%)
  local copies, waits for them, and re-layouts  70.4 us (10%)
  other arithmetic  40.6 us (5%)
  matrix products  12.5 us (2%)
    pallas_call x2, Pallas kernels, assemble(): pl.pallas_call(functools.partial(assemble_kernel, depth=depth, width=widt...  257 us
    ppermute x28, waiting for transfers between devices, ring(): lax.ppermute(values, 'y', [(i, (i + step) % RING) for i in range(RING)])  75.3 us
    ppermute x28, starting transfers between devices, ring(): lax.ppermute(values, 'y', [(i, (i + step) % RING) for i in range(RING)])  39.7 us
    all_to_all x2, waiting for transfers between devices, grads_home(): arrived = lax.all_to_all(total, FLAT, 0, 0, tiled=True)  36 us
    pallas_call x4, Pallas kernels, feed(): pl.pallas_call(feed_kernel, grid=(width // block,), in_specs=[whole, whol...  28.3 us
    pallas_call x1, Pallas kernels, attend_back(): pl.pallas_call(functools.partial(attend_back_kernel, chunks=4), grid=(row...  25.5 us
    unnamed x128, local copies, waits for them, and re-layouts  22 us
    pallas_call x2, Pallas kernels, weight_grads(): pl.pallas_call(functools.partial(weight_grad_kernel, parts=parts, switch=...  19.5 us
  transfers between devices with their start and end apart: 46, of which 22 were waited for; matrix products, arithmetic and copies ran while one was open for 13% of the time, Pallas kernels for 22%

profile of v2, /device:TPU:0, one launch (start us, length us, event | category | flops | bytes accessed | tf_op | source)
XLA Modules:
  0.0 727.3 jit_solution(8098650322691238836)
XLA Ops:
  4.1 2.3 concatenate.58
  8.3 11.1 %all-to-all-start = ((bf16[128,2,2304]{2,1,0:T(2,128)(2,1)}), bf16[128,2,2304]{2,1,0:T(2,128)(2,1)S(1)}, u32[]{:S(2)}, u32[]{:S(2)}) async-start(bf16[128,2,2304]{2,1,0:T(2,128)(2,1)} %reshape.376), calls=%async_computation | async-start | bytes 2359296 | tf_op jit(solution)/shard_map/all_to_all | solution.py:553
  25.2 14.9 %all-to-all-done = bf16[128,2,2304]{2,1,0:T(2,128)(2,1)S(1)} async-done(((bf16[128,2,2304]{2,1,0:T(2,128)(2,1)}), bf16[128,2,2304]{2,1,0:T(2,128)(2,1)S(1)}, u32[]{:S(2)}, u32[]{:S(2)}) %all-to-all-start) | async-done | bytes 1179680 | tf_op jit(solution)/shard_map/all_to_all | solution.py:553
  42.2 2.3 fusion.44
  48.6 3.7 all-to-all-start.1
  56.1 13.7 %all-to-all-done.1.mine_ref = bf16[16,4,64,128]{3,2,1,0:T(8,128)(2,1)S(1)} async-done(((bf16[16,4,64,128]{3,2,1,0:T(8,128)(2,1)}), bf16[16,4,64,128]{3,2,1,0:T(8,128)(2,1)S(1)}, u32[]{:S(2)}, u32[]{:S(2)}) %all-to-all-start.1) | async-done | bytes 1048608 | tf_op jit(solution)/shard_map/all_to_all | solution.py:86
  77.4 5.1 collective-permute-done.1
  87.0 4.5 all-to-all-start.2
  94.2 64.9 %shard_map.196.w_ref = bf16[4,1024,256]{2,1,0:T(8,128)(2,1)} custom-call(s32[1]{0:T(128)} %bitcast.core_ref, bf16[16,4,64,128]{3,2,1,0:T(8,128)(2,1)} %copy-done.37, bf16[16,4,64,128]{3,2,1,0:T(8,128)(2,1)} %collective-permute-done.4.other_ref), custom_call_target="tpu_custom_call" | custom-call | bytes 4194304 | tf_op jit(solution)/shard_map/pallas_call | solution.py:108
  160.7 7.1 shard_map.197
  171.1 11.6 %shard_map.198 = (f32[2048,128]{1,0:T(8,128)S(1)}, bf16[2048,128]{1,0:T(8,128)(2,1)S(1)}, bf16[2048,128]{1,0:T(8,128)(2,1)S(1)}) custom-call(bf16[3,2048,128]{2,1,0:T(8,128)(2,1)S(1)} %constant_dynamic-update-slice_fusion.5.qkv_ref.all_ref, bf16[3,2048,128]{2,1,0:T(8,128)(2,1)S(1)} %constant_dynamic-update-slice_fusion.5.qkv_ref.all_ref, ...), custom_call_target="tpu_custom_call" | custom-call | flops 8589934592 | bytes 6291456 | tf_op jit(solution)/shard_map/pallas_call | solution.py:358
  189.9 2.9 collective-permute-start.11
  196.6 19.9 %collective-permute-done.10 = bf16[256,1024]{1,0:T(8,128)(2,1)} collective-permute-done((bf16[256,1024]{1,0:T(8,128)(2,1)}, bf16[256,1024]{1,0:T(8,128)(2,1)}, u32[]{:S(2)}, u32[]{:S(2)}) %collective-permute-start.10) | collective-permute-done | bytes 524320 | tf_op jit(solution)/shard_map/ppermute | solution.py:59
  219.9 3.8 collective-permute-start.14
  223.8 4.1 collective-permute-done.15.g_ref.refs_5_
  229.4 3.6 collective-permute-start.22
  234.5 4.6 collective-permute-done.14.b_ref.refs_1_
  240.6 3.6 collective-permute-start.20
  246.3 2.8 collective-permute-done.23
  254.6 192.0 %shard_map.199.w_ref = bf16[3,1024,1024]{2,1,0:T(8,128)(2,1)} custom-call(s32[1]{0:T(128)} %bitcast.core_ref, bf16[16,3,64,512]{3,2,1,0:T(8,128)(2,1)} %all-to-all-done.2.mine_ref, bf16[16,3,64,512]{3,2,1,0:T(8,128)(2,1)} %collective-permute-done.13.other_ref), custom_call_target="tpu_custom_call" | custom-call | bytes 12582912 | tf_op jit(solution)/shard_map/pallas_call | solution.py:108
  448.6 7.0 shard_map.201
  457.1 7.2 shard_map.202
  465.4 3.1 collective-permute-start.19
  468.6 7.0 shard_map.203
  477.5 7.2 shard_map.200
  484.7 4.2 collective-permute-done.19
  490.1 2.7 constant_dynamic-update-slice_fusion.15
  492.8 3.1 collective-permute-start.25
  495.9 10.8 %shard_map.207 = bf16[2,8,2,3,64,512]{5,4,3,2,1,0:T(8,128)(2,1)} custom-call(s32[1]{0:T(128)} %bitcast.core_ref, bf16[256,1024]{1,0:T(8,128)(2,1)} %multiply_convert_fusion.b_ref.refs_0_, bf16[256,1024]{1,0:T(8,128)(2,1)S(1)} %copy-done.19, bf16[256,1024]{1,0:T(8,128)(2,1)S(1)} %copy-done.23, bf16[256,1024]{1,0:T(8,128)(2,1)} %collective-permute-done.17.b_ref.refs_3_, ...), custom_call_target="tpu_custom_call" | custom-call | flops 6442450944 | bytes 16777216 | tf_op jit(solution)/shard_map/pallas_call | solution.py:160
  506.7 3.3 collective-permute-start.26
  510.1 6.4 fusion.38
  516.5 3.3 collective-permute-start.32
  524.0 8.3 %collective-permute-done.31 = bf16[256,1024]{1,0:T(8,128)(2,1)S(1)} collective-permute-done((bf16[256,1024]{1,0:T(8,128)(2,1)S(1)}, bf16[256,1024]{1,0:T(8,128)(2,1)S(1)}, u32[]{:S(2)}, u32[]{:S(2)}) %collective-permute-start.31) | collective-permute-done | bytes 524320 | tf_op jit(solution)/shard_map/ppermute | solution.py:59
  532.3 10.5 %collective-permute-done.32 = bf16[256,1024]{1,0:T(8,128)(2,1)S(1)} collective-permute-done((bf16[256,1024]{1,0:T(8,128)(2,1)S(1)}, bf16[256,1024]{1,0:T(8,128)(2,1)S(1)}, u32[]{:S(2)}, u32[]{:S(2)}) %collective-permute-start.32) | collective-permute-done | bytes 524320 | tf_op jit(solution)/shard_map/ppermute | solution.py:59
  546.3 8.9 %all-to-all-start.3 = ((bf16[128,2,1024]{2,1,0:T(2,128)(2,1)}), bf16[128,2,1024]{2,1,0:T(2,128)(2,1)S(1)}, u32[]{:S(2)}, u32[]{:S(2)}) async-start(bf16[128,2,1024]{2,1,0:T(2,128)(2,1)} %reshape.381), calls=%async_computation.3 | async-start | bytes 1048576 | tf_op jit(solution)/shard_map/all_to_all | solution.py:653
  557.5 25.5 %shard_map.204 = (bf16[2048,128]{1,0:T(8,128)(2,1)S(1)}, bf16[2048,128]{1,0:T(8,128)(2,1)S(1)}, bf16[2048,128]{1,0:T(8,128)(2,1)S(1)}, f32[8,128]{1,0:T(8,128)S(1)}) custom-call(bf16[3,2048,128]{2,1,0:T(8,128)(2,1)} %copy-done.11, bf16[3,2048,128]{2,1,0:T(8,128)(2,1)} %copy-done.11, bf16[2048,128]{1,0:T(8,128)(2,1)S(1)} %copy-done.30, ...), custom_call_target="tpu_custom_call" | custom-call | flops 21474836480 | bytes 6291456 | tf_op jit(solution)/shard_map/pallas_call | solution.py:433
  588.8 8.6 %shard_map.205 = (bf16[3,1024,256]{2,1,0:T(8,128)(2,1)S(1)}, bf16[1024,1024]{1,0:T(8,128)(2,1)S(1)}, f32[8,256]{1,0:T(8,128)S(1)}) custom-call(s32[1]{0:T(128)} %bitcast.core_ref, bf16[3,1024,128]{2,1,0:T(8,128)(2,1)S(1)} %pad_maximum_fusion.2.mine_ref, bf16[3,1024,128]{2,1,0:T(8,128)(2,1)S(1)} %copy-done.6, f32[2,1024,256]{2,1,0:T(8,128)} %copy-done.4, ...), custom_call_target="tpu_custom_call" | custom-call | flops 2147483648 | bytes 8388608 | tf_op jit(solution)/shard_map/pallas_call | solution.py:285
  605.4 8.7 %shard_map.206 = bf16[2,8,2,4,64,128]{5,4,3,2,1,0:T(8,128)(2,1)S(1)} custom-call(s32[1]{0:T(128)} %bitcast.core_ref, bf16[1024,1152]{1,0:T(8,128)(2,1)} %copy-done.34, bf16[1024,1024]{1,0:T(8,128)(2,1)S(1)} %copy-done.3, bf16[4,1024,256]{2,1,0:T(8,128)(2,1)} %pad_maximum_fusion.refs_2_), custom_call_target="tpu_custom_call" | custom-call | flops 2147483648 | bytes 8388608 | tf_op jit(solution)/shard_map/pallas_call | solution.py:160
  615.8 8.7 %collective-permute-done.35 = bf16[256,1024]{1,0:T(8,128)(2,1)} collective-permute-done((bf16[256,1024]{1,0:T(8,128)(2,1)}, bf16[256,1024]{1,0:T(8,128)(2,1)}, u32[]{:S(2)}, u32[]{:S(2)}) %collective-permute-start.35) | collective-permute-done | bytes 524320 | tf_op jit(solution)/shard_map/ppermute | solution.py:59
  628.0 3.3 convolution_convert_fusion.3
  634.5 9.6 %all-to-all-start.4 = ((bf16[128,2,1408]{2,1,0:T(2,128)(2,1)}), bf16[128,2,1408]{2,1,0:T(2,128)(2,1)}, u32[]{:S(2)}, u32[]{:S(2)}) async-start(bf16[128,2,1408]{2,1,0:T(2,128)(2,1)} %pad_maximum_fusion.3), calls=%async_computation.4 | async-start | bytes 1441792 | tf_op jit(solution)/shard_map/all_to_all | solution.py:688
  644.2 3.1 fusion.1
  647.3 12.1 %all-to-all-done.4 = bf16[128,2,1408]{2,1,0:T(2,128)(2,1)} async-done(((bf16[128,2,1408]{2,1,0:T(2,128)(2,1)}), bf16[128,2,1408]{2,1,0:T(2,128)(2,1)}, u32[]{:S(2)}, u32[]{:S(2)}) %all-to-all-start.4) | async-done | bytes 720928 | tf_op jit(solution)/shard_map/all_to_all | solution.py:688
  659.4 4.5 all-to-all-start.5
  664.0 4.9 fusion
  669.0 12.4 %all-to-all-done.5 = bf16[16,4,64,128]{3,2,1,0:T(8,128)(2,1)} async-done(((bf16[16,4,64,128]{3,2,1,0:T(8,128)(2,1)}), bf16[16,4,64,128]{3,2,1,0:T(8,128)(2,1)}, u32[]{:S(2)}, u32[]{:S(2)}) %all-to-all-start.5) | async-done | bytes 1048608 | tf_op jit(solution)/shard_map/all_to_all | solution.py:122
  681.3 3.7 all-to-all-start.6
  701.5 23.7 %all-to-all-done.6 = bf16[16,3,64,512]{3,2,1,0:T(8,128)(2,1)S(1)} async-done(((bf16[16,3,64,512]{3,2,1,0:T(8,128)(2,1)}), bf16[16,3,64,512]{3,2,1,0:T(8,128)(2,1)S(1)}, u32[]{:S(2)}, u32[]{:S(2)}) %all-to-all-start.6) | async-done | bytes 3145760 | tf_op jit(solution)/shard_map/all_to_all | solution.py:122
  (341 shorter events, 125.0 us)
Async XLA Ops:
  8.3 31.7 %all-to-all-start = ((bf16[128,2,2304]{2,1,0:T(2,128)(2,1)}), bf16[128,2,2304]{2,1,0:T(2,128)(2,1)S(1)}, u32[]{:S(2)}, u32[]{:S(2)}) async-start(bf16[128,2,2304]{2,1,0:T(2,128)(2,1)} %reshape.376), calls=%async_computation | async-start | bytes 2359296 | tf_op jit(solution)/shard_map/all_to_all | solution.py:553
  19.5 34.9 %collective-permute-start.8 = (f32[2,2]{1,0:T(2,128)}, f32[2,2]{1,0:T(2,128)}, u32[]{:S(2)}, u32[]{:S(2)}) collective-permute-start(f32[2,2]{1,0:T(2,128)} %param.25), channel_id=1, source_target_pairs={{0,1},{1,0},{2,3},{3,2},{4,5},{5,4},{6,7},{7,6},{8,9},{9,8},{10,11... | collective-permute-start | bytes 56 | tf_op jit(solution)/shard_map/ppermute | solution.py:566
  20.6 49.2 %collective-permute-start.7 = (s32[1,4]{1,0:T(1,128)}, s32[1,4]{1,0:T(1,128)}, u32[]{:S(2)}, u32[]{:S(2)}) collective-permute-start(s32[1,4]{1,0:T(1,128)} %param.18), channel_id=1, source_target_pairs={{0,8},{8,0},{1,9},{9,1},{2,10},{10,2},{3,11},{11,3},{4,12},{12,4},... | collective-permute-start | bytes 56 | tf_op jit(solution)/shard_map/ppermute | solution.py:63
  48.6 21.2 %all-to-all-start.1 = ((bf16[16,4,64,128]{3,2,1,0:T(8,128)(2,1)}), bf16[16,4,64,128]{3,2,1,0:T(8,128)(2,1)S(1)}, u32[]{:S(2)}, u32[]{:S(2)}) async-start(bf16[16,4,64,128]{3,2,1,0:T(8,128)(2,1)} %broadcast_in_dim.167), calls=%async_computation.1 | async-start | bytes 2097152 | tf_op jit(solution)/shard_map/all_to_all | solution.py:86
  53.4 17.8 %collective-permute-start = (bf16[256,1152]{1,0:T(8,128)(2,1)}, bf16[256,1152]{1,0:T(8,128)(2,1)}, u32[]{:S(2)}, u32[]{:S(2)}) collective-permute-start(bf16[256,1152]{1,0:T(8,128)(2,1)} %get-tuple-element.94), channel_id=1, source_target_pairs={{0,6},{2,0},{4,2},{6,4},{1,7},{3,1},{5,3},{7,5},{8,14},{10,8},{12,... | collective-permute-start | bytes 1769480 | tf_op jit(solution)/shard_map/ppermute | solution.py:59
  55.1 18.6 %collective-permute-start.2 = (bf16[256,1152]{1,0:T(8,128)(2,1)}, bf16[256,1152]{1,0:T(8,128)(2,1)}, u32[]{:S(2)}, u32[]{:S(2)}) collective-permute-start(bf16[256,1152]{1,0:T(8,128)(2,1)} %get-tuple-element.94), channel_id=1, source_target_pairs={{0,2},{2,4},{4,6},{6,0},{1,3},{3,5},{5,7},{7,1},{8,10},{10,12},{12... | collective-permute-start | bytes 1769480 | tf_op jit(solution)/shard_map/ppermute | solution.py:59
  69.8 15.2 %collective-permute-start.4 = (bf16[16,4,64,128]{3,2,1,0:T(8,128)(2,1)S(1)}, bf16[16,4,64,128]{3,2,1,0:T(8,128)(2,1)}, u32[]{:S(2)}, u32[]{:S(2)}) collective-permute-start(bf16[16,4,64,128]{3,2,1,0:T(8,128)(2,1)S(1)} %all-to-all-done.1.mine_ref), channel_id=1, source_target_pairs={{0,8},{8,0},{1,9},{9,1},{2,10},{10,2},{3,11},{11,3},{4,12},{12,4},... | collective-permute-start | bytes 3145736 | tf_op jit(solution)/shard_map/ppermute | solution.py:63
  72.9 9.6 %collective-permute-start.1 = (bf16[128,1152]{1,0:T(8,128)(2,1)}, bf16[128,1152]{1,0:T(8,128)(2,1)}, u32[]{:S(2)}, u32[]{:S(2)}) collective-permute-start(bf16[128,1152]{1,0:T(8,128)(2,1)} %slice.268), channel_id=1, source_target_pairs={{0,6},{2,0},{4,2},{6,4},{1,7},{3,1},{5,3},{7,5},{8,14},{10,8},{12,... | collective-permute-start | bytes 884744 | tf_op jit(solution)/shard_map/ppermute | solution.py:59
  74.7 10.3 %collective-permute-start.3 = (bf16[128,1152]{1,0:T(8,128)(2,1)S(1)}, bf16[128,1152]{1,0:T(8,128)(2,1)S(1)}, u32[]{:S(2)}, u32[]{:S(2)}) collective-permute-start(bf16[128,1152]{1,0:T(8,128)(2,1)S(1)} %slice.269), channel_id=1, source_target_pairs={{0,2},{2,4},{4,6},{6,0},{1,3},{3,5},{5,7},{7,1},{8,10},{10,12},{12... | collective-permute-start | bytes 884744 | tf_op jit(solution)/shard_map/ppermute | solution.py:59
  87.0 98.1 %all-to-all-start.2 = ((bf16[16,3,64,512]{3,2,1,0:T(8,128)(2,1)}), bf16[16,3,64,512]{3,2,1,0:T(8,128)(2,1)}, u32[]{:S(2)}, u32[]{:S(2)}) async-start(bf16[16,3,64,512]{3,2,1,0:T(8,128)(2,1)} %broadcast_in_dim.180), calls=%async_computation.2 | async-start | bytes 6291456 | tf_op jit(solution)/shard_map/all_to_all | solution.py:86
  92.6 66.5 %copy-start.34 = (bf16[1024,1152]{1,0:T(8,128)(2,1)}, bf16[1024,1152]{1,0:T(8,128)(2,1)S(1)}, u32[]{:S(2)}) copy-start(bf16[1024,1152]{1,0:T(8,128)(2,1)S(1)} %constant_dynamic-update-slice_fusion.a_ref.facts_ref.refs_0_) | copy-start | bytes 7077892
  92.9 1.2 collective-permute-start.6
  167.8 3.0 collective-permute-start.5
  184.7 1.7 collective-permute-start.9
  185.1 69.5 %collective-permute-start.13 = (bf16[16,3,64,512]{3,2,1,0:T(8,128)(2,1)}, bf16[16,3,64,512]{3,2,1,0:T(8,128)(2,1)}, u32[]{:S(2)}, u32[]{:S(2)}) collective-permute-start(bf16[16,3,64,512]{3,2,1,0:T(8,128)(2,1)} %all-to-all-done.2.mine_ref), channel_id=1, source_target_pairs={{0,8},{8,0},{1,9},{9,1},{2,10},{10,2},{3,11},{11,3},{4,12},{12,4},... | collective-permute-start | bytes 9437192 | tf_op jit(solution)/shard_map/ppermute | solution.py:63
  189.5 26.9 %collective-permute-start.10 = (bf16[256,1024]{1,0:T(8,128)(2,1)}, bf16[256,1024]{1,0:T(8,128)(2,1)}, u32[]{:S(2)}, u32[]{:S(2)}) collective-permute-start(bf16[256,1024]{1,0:T(8,128)(2,1)} %get-tuple-element.89), channel_id=1, source_target_pairs={{0,2},{2,4},{4,6},{6,0},{1,3},{3,5},{5,7},{7,1},{8,10},{10,12},{12... | collective-permute-start | bytes 1572872 | tf_op jit(solution)/shard_map/ppermute | solution.py:59
  189.9 26.6 %collective-permute-start.11 = (bf16[256,1024]{1,0:T(8,128)(2,1)}, bf16[256,1024]{1,0:T(8,128)(2,1)}, u32[]{:S(2)}, u32[]{:S(2)}) collective-permute-start(bf16[256,1024]{1,0:T(8,128)(2,1)} %get-tuple-element.91), channel_id=1, source_target_pairs={{0,6},{2,0},{4,2},{6,4},{1,7},{3,1},{5,3},{7,5},{8,14},{10,8},{12,... | collective-permute-start | bytes 1572872 | tf_op jit(solution)/shard_map/ppermute | solution.py:59
  192.8 23.7 %collective-permute-start.12 = (bf16[256,1024]{1,0:T(8,128)(2,1)}, bf16[256,1024]{1,0:T(8,128)(2,1)}, u32[]{:S(2)}, u32[]{:S(2)}) collective-permute-start(bf16[256,1024]{1,0:T(8,128)(2,1)} %get-tuple-element.90), channel_id=1, source_target_pairs={{0,4},{2,6},{4,0},{6,2},{1,5},{3,7},{5,1},{7,3},{8,12},{10,14},{12... | collective-permute-start | bytes 1572872 | tf_op jit(solution)/shard_map/ppermute | solution.py:59
  194.8 33.1 %collective-permute-start.15 = (bf16[256,1024]{1,0:T(8,128)(2,1)}, bf16[256,1024]{1,0:T(8,128)(2,1)S(1)}, u32[]{:S(2)}, u32[]{:S(2)}) collective-permute-start(bf16[256,1024]{1,0:T(8,128)(2,1)} %slice.271.g_ref.refs_4_), channel_id=1, source_target_pairs={{0,6},{2,0},{4,2},{6,4},{1,7},{3,1},{5,3},{7,5},{8,14},{10,8},{12,... | collective-permute-start | bytes 1572872 | tf_op jit(solution)/shard_map/ppermute | solution.py:59
  216.5 16.5 %collective-permute-start.18 = (bf16[256,1024]{1,0:T(8,128)(2,1)}, bf16[256,1024]{1,0:T(8,128)(2,1)S(1)}, u32[]{:S(2)}, u32[]{:S(2)}) collective-permute-start(bf16[256,1024]{1,0:T(8,128)(2,1)} %slice.271.g_ref.refs_4_), channel_id=1, source_target_pairs={{0,2},{2,4},{4,6},{6,0},{1,3},{3,5},{5,7},{7,1},{8,10},{10,12},{12... | collective-permute-start | bytes 1572872 | tf_op jit(solution)/shard_map/ppermute | solution.py:59
  219.9 19.2 %collective-permute-start.14 = (bf16[256,1024]{1,0:T(8,128)(2,1)}, bf16[256,1024]{1,0:T(8,128)(2,1)S(1)}, u32[]{:S(2)}, u32[]{:S(2)}) collective-permute-start(bf16[256,1024]{1,0:T(8,128)(2,1)} %multiply_convert_fusion.b_ref.refs_0_), channel_id=1, source_target_pairs={{0,6},{2,0},{4,2},{6,4},{1,7},{3,1},{5,3},{7,5},{8,14},{10,8},{12,... | collective-permute-start | bytes 1572872 | tf_op jit(solution)/shard_map/ppermute | solution.py:59
  223.8 20.5 %collective-permute-start.17 = (bf16[256,1024]{1,0:T(8,128)(2,1)}, bf16[256,1024]{1,0:T(8,128)(2,1)}, u32[]{:S(2)}, u32[]{:S(2)}) collective-permute-start(bf16[256,1024]{1,0:T(8,128)(2,1)} %multiply_convert_fusion.b_ref.refs_0_), channel_id=1, source_target_pairs={{0,2},{2,4},{4,6},{6,0},{1,3},{3,5},{5,7},{7,1},{8,10},{10,12},{12... | collective-permute-start | bytes 1572872 | tf_op jit(solution)/shard_map/ppermute | solution.py:59
  229.4 16.0 %collective-permute-start.22 = (bf16[128,1024]{1,0:T(8,128)(2,1)}, bf16[128,1024]{1,0:T(8,128)(2,1)}, u32[]{:S(2)}, u32[]{:S(2)}) collective-permute-start(bf16[128,1024]{1,0:T(8,128)(2,1)} %slice.280), channel_id=1, source_target_pairs={{0,6},{2,0},{4,2},{6,4},{1,7},{3,1},{5,3},{7,5},{8,14},{10,8},{12,... | collective-permute-start | bytes 786440 | tf_op jit(solution)/shard_map/ppermute | solution.py:59
  234.5 14.6 %collective-permute-start.23 = (bf16[128,1024]{1,0:T(8,128)(2,1)}, bf16[128,1024]{1,0:T(8,128)(2,1)}, u32[]{:S(2)}, u32[]{:S(2)}) collective-permute-start(bf16[128,1024]{1,0:T(8,128)(2,1)} %slice.281), channel_id=1, source_target_pairs={{0,2},{2,4},{4,6},{6,0},{1,3},{3,5},{5,7},{7,1},{8,10},{10,12},{12... | collective-permute-start | bytes 786440 | tf_op jit(solution)/shard_map/ppermute | solution.py:59
  240.6 10.3 %collective-permute-start.20 = (bf16[128,1024]{1,0:T(8,128)(2,1)}, bf16[128,1024]{1,0:T(8,128)(2,1)}, u32[]{:S(2)}, u32[]{:S(2)}) collective-permute-start(bf16[128,1024]{1,0:T(8,128)(2,1)} %slice.278), channel_id=1, source_target_pairs={{0,6},{2,0},{4,2},{6,4},{1,7},{3,1},{5,3},{7,5},{8,14},{10,8},{12,... | collective-permute-start | bytes 786440 | tf_op jit(solution)/shard_map/ppermute | solution.py:59
  245.3 8.5 %collective-permute-start.21 = (bf16[128,1024]{1,0:T(8,128)(2,1)S(1)}, bf16[128,1024]{1,0:T(8,128)(2,1)S(1)}, u32[]{:S(2)}, u32[]{:S(2)}) collective-permute-start(bf16[128,1024]{1,0:T(8,128)(2,1)S(1)} %slice.279), channel_id=1, source_target_pairs={{0,2},{2,4},{4,6},{6,0},{1,3},{3,5},{5,7},{7,1},{8,10},{10,12},{12... | collective-permute-start | bytes 786440 | tf_op jit(solution)/shard_map/ppermute | solution.py:59
  456.9 27.8 %collective-permute-start.16 = (bf16[256,1024]{1,0:T(8,128)(2,1)S(1)}, bf16[256,1024]{1,0:T(8,128)(2,1)S(1)}, u32[]{:S(2)}, u32[]{:S(2)}) collective-permute-start(bf16[256,1024]{1,0:T(8,128)(2,1)S(1)} %get-tuple-element.47), channel_id=1, source_target_pairs={{0,2},{2,4},{4,6},{6,0},{1,3},{3,5},{5,7},{7,1},{8,10},{10,12},{12... | collective-permute-start | bytes 1572872 | tf_op jit(solution)/shard_map/ppermute | solution.py:59
  465.4 23.5 %collective-permute-start.19 = (bf16[256,1024]{1,0:T(8,128)(2,1)S(1)}, bf16[256,1024]{1,0:T(8,128)(2,1)S(1)}, u32[]{:S(2)}, u32[]{:S(2)}) collective-permute-start(bf16[256,1024]{1,0:T(8,128)(2,1)S(1)} %get-tuple-element.48), channel_id=1, source_target_pairs={{0,6},{2,0},{4,2},{6,4},{1,7},{3,1},{5,3},{7,5},{8,14},{10,8},{12,... | collective-permute-start | bytes 1572872 | tf_op jit(solution)/shard_map/ppermute | solution.py:59
  476.7 12.9 %collective-permute-start.24 = (bf16[256,1024]{1,0:T(8,128)(2,1)S(1)}, bf16[256,1024]{1,0:T(8,128)(2,1)S(1)}, u32[]{:S(2)}, u32[]{:S(2)}) collective-permute-start(bf16[256,1024]{1,0:T(8,128)(2,1)S(1)} %get-tuple-element.49), channel_id=1, source_target_pairs={{0,4},{2,6},{4,0},{6,2},{1,5},{3,7},{5,1},{7,3},{8,12},{10,14},{12... | collective-permute-start | bytes 1572872 | tf_op jit(solution)/shard_map/ppermute | solution.py:59
  492.8 13.9 %collective-permute-start.25 = (bf16[256,1024]{1,0:T(8,128)(2,1)S(1)}, bf16[256,1024]{1,0:T(8,128)(2,1)S(1)}, u32[]{:S(2)}, u32[]{:S(2)}) collective-permute-start(bf16[256,1024]{1,0:T(8,128)(2,1)S(1)} %get-tuple-element.76), channel_id=1, source_target_pairs={{0,6},{2,0},{4,2},{6,4},{1,7},{3,1},{5,3},{7,5},{8,14},{10,8},{12,... | collective-permute-start | bytes 1572872 | tf_op jit(solution)/shard_map/ppermute | solution.py:59
  495.9 14.1 %collective-permute-start.27 = (bf16[256,1024]{1,0:T(8,128)(2,1)S(1)}, bf16[256,1024]{1,0:T(8,128)(2,1)S(1)}, u32[]{:S(2)}, u32[]{:S(2)}) collective-permute-start(bf16[256,1024]{1,0:T(8,128)(2,1)S(1)} %get-tuple-element.76), channel_id=1, source_target_pairs={{0,2},{2,4},{4,6},{6,0},{1,3},{3,5},{5,7},{7,1},{8,10},{10,12},{12... | collective-permute-start | bytes 1572872 | tf_op jit(solution)/shard_map/ppermute | solution.py:59
  506.7 13.1 %collective-permute-start.26 = (bf16[128,1024]{1,0:T(8,128)(2,1)S(1)}, bf16[128,1024]{1,0:T(8,128)(2,1)S(1)}, u32[]{:S(2)}, u32[]{:S(2)}) collective-permute-start(bf16[128,1024]{1,0:T(8,128)(2,1)S(1)} %slice.282), channel_id=1, source_target_pairs={{0,6},{2,0},{4,2},{6,4},{1,7},{3,1},{5,3},{7,5},{8,14},{10,8},{12,... | collective-permute-start | bytes 786440 | tf_op jit(solution)/shard_map/ppermute | solution.py:59
  510.0 11.7 %collective-permute-start.28 = (bf16[128,1024]{1,0:T(8,128)(2,1)S(1)}, bf16[128,1024]{1,0:T(8,128)(2,1)S(1)}, u32[]{:S(2)}, u32[]{:S(2)}) collective-permute-start(bf16[128,1024]{1,0:T(8,128)(2,1)S(1)} %slice.283), channel_id=1, source_target_pairs={{0,2},{2,4},{4,6},{6,0},{1,3},{3,5},{5,7},{7,1},{8,10},{10,12},{12... | collective-permute-start | bytes 786440 | tf_op jit(solution)/shard_map/ppermute | solution.py:59
  516.5 147.5 %collective-permute-start.38 = (bf16[16,3,64,512]{3,2,1,0:T(8,128)(2,1)}, bf16[16,3,64,512]{3,2,1,0:T(8,128)(2,1)}, u32[]{:S(2)}, u32[]{:S(2)}) collective-permute-start(bf16[16,3,64,512]{3,2,1,0:T(8,128)(2,1)} %bitcast.29), channel_id=1, source_target_pairs={{0,8},{8,0},{1,9},{9,1},{2,10},{10,2},{3,11},{11,3},{4,12},{12,4},... | collective-permute-start | bytes 9437192 | tf_op jit(solution)/shard_map/ppermute | solution.py:63
  516.5 15.8 %collective-permute-start.31 = (bf16[256,1024]{1,0:T(8,128)(2,1)S(1)}, bf16[256,1024]{1,0:T(8,128)(2,1)S(1)}, u32[]{:S(2)}, u32[]{:S(2)}) collective-permute-start(bf16[256,1024]{1,0:T(8,128)(2,1)S(1)} %get-tuple-element.55), channel_id=1, source_target_pairs={{0,2},{2,4},{4,6},{6,0},{1,3},{3,5},{5,7},{7,1},{8,10},{10,12},{12... | collective-permute-start | bytes 1572872 | tf_op jit(solution)/shard_map/ppermute | solution.py:59
  516.5 26.3 %collective-permute-start.32 = (bf16[256,1024]{1,0:T(8,128)(2,1)S(1)}, bf16[256,1024]{1,0:T(8,128)(2,1)S(1)}, u32[]{:S(2)}, u32[]{:S(2)}) collective-permute-start(bf16[256,1024]{1,0:T(8,128)(2,1)S(1)} %get-tuple-element.56), channel_id=1, source_target_pairs={{0,6},{2,0},{4,2},{6,4},{1,7},{3,1},{5,3},{7,5},{8,14},{10,8},{12,... | collective-permute-start | bytes 1572872 | tf_op jit(solution)/shard_map/ppermute | solution.py:59
  519.8 24.9 %collective-permute-start.33 = (bf16[256,1024]{1,0:T(8,128)(2,1)S(1)}, bf16[256,1024]{1,0:T(8,128)(2,1)S(1)}, u32[]{:S(2)}, u32[]{:S(2)}) collective-permute-start(bf16[256,1024]{1,0:T(8,128)(2,1)S(1)} %get-tuple-element.57), channel_id=1, source_target_pairs={{0,4},{2,6},{4,0},{6,2},{1,5},{3,7},{5,1},{7,3},{8,12},{10,14},{12... | collective-permute-start | bytes 1572872 | tf_op jit(solution)/shard_map/ppermute | solution.py:59
  521.8 22.9 %copy-start.50 = (bf16[256]{0:T(256)(128)(2,1)S(1)}, bf16[256]{0:T(256)(128)(2,1)}, u32[]{:S(2)}) copy-start(bf16[256]{0:T(256)(128)(2,1)} %eq.86) | copy-start | bytes 1540
  524.0 31.4 %collective-permute-start.29 = (bf16[1024,128]{1,0:T(8,128)(2,1)}, bf16[1024,128]{1,0:T(8,128)(2,1)}, u32[]{:S(2)}, u32[]{:S(2)}) collective-permute-start(bf16[1024,128]{1,0:T(8,128)(2,1)} %get-tuple-element.103), channel_id=1, source_target_pairs={{0,8},{8,0},{1,9},{9,1},{2,10},{10,2},{3,11},{11,3},{4,12},{12,4},... | collective-permute-start | bytes 786440 | tf_op jit(solution)/shard_map/ppermute | solution.py:63
  546.3 38.4 %all-to-all-start.3 = ((bf16[128,2,1024]{2,1,0:T(2,128)(2,1)}), bf16[128,2,1024]{2,1,0:T(2,128)(2,1)S(1)}, u32[]{:S(2)}, u32[]{:S(2)}) async-start(bf16[128,2,1024]{2,1,0:T(2,128)(2,1)} %reshape.381), calls=%async_computation.3 | async-start | bytes 1048576 | tf_op jit(solution)/shard_map/all_to_all | solution.py:653
  584.1 2.6 collective-permute-start.30
  598.5 17.3 %collective-permute-start.34 = (bf16[256,1024]{1,0:T(8,128)(2,1)}, bf16[256,1024]{1,0:T(8,128)(2,1)}, u32[]{:S(2)}, u32[]{:S(2)}) collective-permute-start(bf16[256,1024]{1,0:T(8,128)(2,1)} %get-tuple-element.86), channel_id=1, source_target_pairs={{0,2},{2,4},{4,6},{6,0},{1,3},{3,5},{5,7},{7,1},{8,10},{10,12},{12... | collective-permute-start | bytes 1572872 | tf_op jit(solution)/shard_map/ppermute | solution.py:59
  599.5 25.1 %collective-permute-start.35 = (bf16[256,1024]{1,0:T(8,128)(2,1)}, bf16[256,1024]{1,0:T(8,128)(2,1)}, u32[]{:S(2)}, u32[]{:S(2)}) collective-permute-start(bf16[256,1024]{1,0:T(8,128)(2,1)} %get-tuple-element.88), channel_id=1, source_target_pairs={{0,6},{2,0},{4,2},{6,4},{1,7},{3,1},{5,3},{7,5},{8,14},{10,8},{12,... | collective-permute-start | bytes 1572872 | tf_op jit(solution)/shard_map/ppermute | solution.py:59
  601.8 24.0 %collective-permute-start.36 = (bf16[256,1024]{1,0:T(8,128)(2,1)}, bf16[256,1024]{1,0:T(8,128)(2,1)}, u32[]{:S(2)}, u32[]{:S(2)}) collective-permute-start(bf16[256,1024]{1,0:T(8,128)(2,1)} %get-tuple-element.87), channel_id=1, source_target_pairs={{0,4},{2,6},{4,0},{6,2},{1,5},{3,7},{5,1},{7,3},{8,12},{10,14},{12... | collective-permute-start | bytes 1572872 | tf_op jit(solution)/shard_map/ppermute | solution.py:59
  615.6 28.5 %collective-permute-start.37 = (bf16[16,4,64,128]{3,2,1,0:T(8,128)(2,1)}, bf16[16,4,64,128]{3,2,1,0:T(8,128)(2,1)}, u32[]{:S(2)}, u32[]{:S(2)}) collective-permute-start(bf16[16,4,64,128]{3,2,1,0:T(8,128)(2,1)} %bitcast.25), channel_id=1, source_target_pairs={{0,8},{8,0},{1,9},{9,1},{2,10},{10,2},{3,11},{11,3},{4,12},{12,4},... | collective-permute-start | bytes 3145736 | tf_op jit(solution)/shard_map/ppermute | solution.py:63
  634.5 24.9 %all-to-all-start.4 = ((bf16[128,2,1408]{2,1,0:T(2,128)(2,1)}), bf16[128,2,1408]{2,1,0:T(2,128)(2,1)}, u32[]{:S(2)}, u32[]{:S(2)}) async-start(bf16[128,2,1408]{2,1,0:T(2,128)(2,1)} %pad_maximum_fusion.3), calls=%async_computation.4 | async-start | bytes 1441792 | tf_op jit(solution)/shard_map/all_to_all | solution.py:688
  659.4 21.9 %all-to-all-start.5 = ((bf16[16,4,64,128]{3,2,1,0:T(8,128)(2,1)}), bf16[16,4,64,128]{3,2,1,0:T(8,128)(2,1)}, u32[]{:S(2)}, u32[]{:S(2)}) async-start(bf16[16,4,64,128]{3,2,1,0:T(8,128)(2,1)} %fusion.1), calls=%async_computation.5 | async-start | bytes 2097152 | tf_op jit(solution)/shard_map/all_to_all | solution.py:122
  681.3 43.8 %all-to-all-start.6 = ((bf16[16,3,64,512]{3,2,1,0:T(8,128)(2,1)}), bf16[16,3,64,512]{3,2,1,0:T(8,128)(2,1)S(1)}, u32[]{:S(2)}, u32[]{:S(2)}) async-start(bf16[16,3,64,512]{3,2,1,0:T(8,128)(2,1)} %fusion), calls=%async_computation.6 | async-start | bytes 6291456 | tf_op jit(solution)/shard_map/all_to_all | solution.py:122
  (57 other events, 445.9 us)

commit v3 on v2

--- a/solution.py
+++ b/solution.py
@@ -83,34 +83,27 @@
 
 def flat_gather(shard):
     many = jnp.broadcast_to(shard[None], (16,) + shard.shape)
-    mine = lax.all_to_all(many, FLAT, 0, 0, tiled=True)
-    return mine, swap_core(mine)
-
-
-def assemble_kernel(core_ref, mine_ref, other_ref, out_ref, sems, *, depth, width):
+    return lax.all_to_all(many, FLAT, 0, 0, tiled=True)
+
+
+def assemble_kernel(core_ref, mine_ref, other_ref, out_ref):
     core = core_ref[0]
-    copies = []
-    for side, ref in enumerate((mine_ref, other_ref)):
-        at = core if side == 0 else 1 - core
-        for i in range(16):
-            rows = pl.multiple_of((i // 2) * 2 * depth + at * depth, depth)
-            target = out_ref.at[:, pl.ds(rows, depth), pl.ds((i % 2) * width, width)]
-            copies.append(pltpu.make_async_copy(ref.at[i], target, sems.at[side, i]))
-    for copy in copies:
-        copy.start()
-    for copy in copies:
-        copy.wait()
+    _, _, depth, width = mine_ref.shape
+    for ref, at in ((mine_ref, core), (other_ref, 1 - core)):
+        rows = pl.ds(pl.multiple_of(at * depth, depth), depth)
+        for z in range(2):
+            out_ref[:, rows, z * width : (z + 1) * width] = ref[z]
 
 
 def assemble(core, mine, other):
     _, kinds, depth, width = mine.shape
-    anywhere = pl.BlockSpec(memory_space=pl.ANY)
+    pair = pl.BlockSpec((2, kinds, depth, width), lambda p: (p, 0, 0, 0))
     return pl.pallas_call(
-        functools.partial(assemble_kernel, depth=depth, width=width),
-        in_specs=[pl.BlockSpec(memory_space=pltpu.SMEM), anywhere, anywhere],
-        out_specs=anywhere,
+        assemble_kernel,
+        grid=(8,),
+        in_specs=[pl.BlockSpec(memory_space=pltpu.SMEM), pair, pair],
+        out_specs=pl.BlockSpec((kinds, 2 * depth, 2 * width), lambda p: (0, p, 0)),
         out_shape=jax.ShapeDtypeStruct((kinds, 16 * depth, 2 * width), BF16),
-        scratch_shapes=[pltpu.SemaphoreType.DMA((2, 16))],
         cost_estimate=pl.CostEstimate(
             flops=0, bytes_accessed=kinds * 128 * depth * width, transcendentals=0
         ),
@@ -537,6 +530,10 @@
             [jnp.where(low_core, mine, other), jnp.where(low_core, other, mine)], axis=-1
         )
 
+    attn_shard = jnp.concatenate([qkv_weight, out_weight.T[None]], 0)
+    feed_shard = jnp.concatenate([gate_up_weight, down_weight.T[None]], 0)
+    attn_mine = flat_gather(attn_shard)
+
     slot = destination % ROWS
     group_at = destination // GROUP
     block_at = (destination % GROUP) // ROWS
@@ -550,16 +547,13 @@
     outgoing = jnp.concatenate([tokens, cotangent, facts, gains_row], axis=1)
     span = outgoing.shape[1]
     outgoing = mm(deal, outgoing).astype(BF16).reshape(DEVICES, 2, span)
+    outgoing, attn_mine = lax.optimization_barrier((outgoing, attn_mine))
     arrived = lax.all_to_all(outgoing, ALL, 0, 0, tiled=True)
 
-    attn_shard = jnp.concatenate([qkv_weight, out_weight.T[None]], 0)
-    feed_shard = jnp.concatenate([gate_up_weight, down_weight.T[None]], 0)
-    attn_shard, arrived = lax.optimization_barrier((attn_shard, arrived))
-    attn_mine, attn_other = flat_gather(attn_shard)
-    attn_w = assemble(core_scalar, attn_mine, attn_other)
-    feed_shard, attn_other = lax.optimization_barrier((feed_shard, attn_other))
-    feed_mine, feed_other = flat_gather(feed_shard)
-    feed_w = assemble(core_scalar, feed_mine, feed_other)
+    attn_w = assemble(core_scalar, attn_mine, swap_core(attn_mine))
+    feed_shard, arrived = lax.optimization_barrier((feed_shard, arrived))
+    feed_mine = flat_gather(feed_shard)
+    feed_w = assemble(core_scalar, feed_mine, swap_core(feed_mine))
 
     lengths_other = swap_core(seq_lengths)
     lengths = jnp.where(zl_at == core, seq_lengths, lengths_other)[0]
@@ -617,6 +611,7 @@
     key_tail = jnp.where(one_lane, 1.0, key_tail).astype(BF16)
     value_tail = jnp.broadcast_to((lane < 3).astype(BF16), (GROUP, WIDE))
     attended, att_low, query_back = attend(qkv, query_tail, key_tail, value_tail)
+    att_low, grad_all = lax.optimization_barrier((att_low, grad_all))
     att_plane = side_by_side(att_low[:PLANE], swap_core(att_low[PLANE:]))
     out_part = mm(att_plane, attn_w[3], NT).astype(BF16).reshape(RING, ROWS, D)
     hidden_one = inputs + reduce_ring([out_part[r] for r in range(RING)])
@@ -627,7 +622,6 @@
     feed_all = gather_ring(feed_in)
     fed = [feed(feed_all[r], grad_all[r], feed_w) for r in range(RING)]
     grad_normed_two = reduce_ring([f[1] for f in fed])
-    mixed = (hidden_one + reduce_ring([f[0] for f in fed])).astype(BF16)
 
     feed_grad = grads_home(
         weight_grads(core_scalar, feed_all, grad_all, [f[2] for f in fed], 2)
@@ -637,6 +631,8 @@
     grad_one = grad_rows.astype(F32) + norm_back(grad_normed_two * gain_two, normed_two, scale_two)
 
     grad_one_all = jnp.concatenate(gather_ring(grad_one.astype(BF16)), 0)
+    y_parts, grad_one_all = lax.optimization_barrier(([f[0] for f in fed], grad_one_all))
+    mixed = (hidden_one + reduce_ring(y_parts)).astype(BF16)
     grad_att = mm(grad_one_all, attn_w[3]).astype(BF16)
     grad_left, grad_right = grad_att[:, :WIDE], grad_att[:, WIDE:]
     grad_send = jnp.where(low_core, grad_right, grad_left)
@@ -649,6 +645,7 @@
     bias_sums = jnp.where(first_part, bias_sums[:2].reshape(2, 2, HEAD_DIM), 0.0)
     bias_sums = jnp.sum(bias_sums, axis=2)
     bias_part = jnp.stack([bias_sums[0], bias_sums[1] - bias_sums[0]])
+    mixed, feed_grad = lax.optimization_barrier((mixed, feed_grad))
     back_mixed = mm(place, mixed, TN).astype(BF16).reshape(DEVICES, 2, D)
     home_mixed = lax.all_to_all(back_mixed, ALL, 0, 0, tiled=True)
     d_mine = jnp.stack([d_query[:PLANE], d_key[:PLANE], d_value[:PLANE]])
@@ -685,7 +682,11 @@
     smalls = jnp.concatenate([gain_sums, qk_row, bias_row, jnp.zeros((16, 8, WIDE - 4), F32)], axis=2)
     smalls = jnp.stack(pieces(smalls.reshape(DEVICES, 3 * WIDE), 2), axis=1)
     back_grads = mm(place, input_grad.astype(BF16), TN).astype(BF16).reshape(DEVICES, 2, D)
-    home = lax.all_to_all(jnp.concatenate([back_grads, smalls], axis=2), ALL, 0, 0, tiled=True)
+    last = jnp.concatenate([back_grads, smalls], axis=2)
+    last, new_tokens, attn_grad, feed_grad = lax.optimization_barrier(
+        (last, new_tokens, attn_grad, feed_grad)
+    )
+    home = lax.all_to_all(last, ALL, 0, 0, tiled=True)
     token_grads = mm(deal, home[:, :, :D].reshape(ROWS, D), TN).astype(BF16)
     sums = jnp.sum(home[:, :, D:].astype(F32), axis=(0, 1))
     gains_grad = sums[:WIDE].reshape(2, 64)

time: 740 us -> 500 us (0.68)
  Pallas kernels: 357 us -> 114 us
  waiting for transfers between devices: 156 us -> 180 us
  local copies, waits for them, and re-layouts: 70.4 us -> 59.9 us
    pallas_call x2, Pallas kernels: 257 us -> 13.8 us  [assemble(): pl.pallas_call(assemble_kernel, grid=(8,), in_specs=[pl.BlockSpec(memory_...]
    ppermute x28, waiting for transfers between devices: 75.3 us -> 108 us  [ring(): lax.ppermute(values, 'y', [(i, (i + step) % RING) for i in range(RING)])]
    all_to_all x2, waiting for transfers between devices: 36 us -> 20.8 us  [grads_home(): arrived = lax.all_to_all(total, FLAT, 0, 0, tiled=True)]
    all_to_all x1, waiting for transfers between devices: 0.01 us -> 10.4 us  [body(): home_mixed = lax.all_to_all(back_mixed, ALL, 0, 0, tiled=True)]
    unnamed x128 -> x147, local copies, waits for them, and re-layouts: 22 us -> 21.8 us
  transfers between devices with their start and end apart: 46 -> 46, of which waited for: 22 -> 20; matrix products, arithmetic and copies ran while one was open for 13% -> 17% of each run, Pallas kernels for 22% -> 15%
where the time goes in v3:
time: 500 us; the launch traced here: 491 us
  waiting for transfers between devices  180 us (36%)
  Pallas kernels  114 us (23%)
  starting transfers between devices  82.1 us (16%)
  local copies, waits for them, and re-layouts  59.9 us (12%)
  other arithmetic  42 us (8%)
  matrix products  11 us (2%)
    ppermute x28, waiting for transfers between devices, ring(): lax.ppermute(values, 'y', [(i, (i + step) % RING) for i in range(RING)])  108 us
    ppermute x28, starting transfers between devices, ring(): lax.ppermute(values, 'y', [(i, (i + step) % RING) for i in range(RING)])  34.1 us
    pallas_call x4, Pallas kernels, feed(): pl.pallas_call(feed_kernel, grid=(width // block,), in_specs=[whole, whol...  28.1 us
    pallas_call x1, Pallas kernels, attend_back(): pl.pallas_call(functools.partial(attend_back_kernel, chunks=4), grid=(row...  25.4 us
    unnamed x147, local copies, waits for them, and re-layouts  21.8 us
    all_to_all x2, waiting for transfers between devices, grads_home(): arrived = lax.all_to_all(total, FLAT, 0, 0, tiled=True)  20.8 us
    pallas_call x2, Pallas kernels, weight_grads(): pl.pallas_call(functools.partial(weight_grad_kernel, parts=parts, switch=...  19.2 us
    all_to_all x1, waiting for transfers between devices, body(): arrived = lax.all_to_all(outgoing, ALL, 0, 0, tiled=True)  16.7 us
  transfers between devices with their start and end apart: 46, of which 20 were waited for; matrix products, arithmetic and copies ran while one was open for 17% of the time, Pallas kernels for 15%

profile of v3, /device:TPU:0, one launch (start us, length us, event | category | flops | bytes accessed | tf_op | source)
XLA Modules:
  0.0 490.6 jit_solution(4424565512090613266)
XLA Ops:
  2.9 8.0 %all-to-all-start = ((bf16[16,4,64,128]{3,2,1,0:T(8,128)(2,1)}), bf16[16,4,64,128]{3,2,1,0:T(8,128)(2,1)S(1)}, u32[]{:S(2)}, u32[]{:S(2)}) async-start(bf16[16,4,64,128]{3,2,1,0:T(8,128)(2,1)} %broadcast_in_dim.168), calls=%async_computation | async-start | bytes 2097152 | tf_op jit(solution)/shard_map/all_to_all | solution.py:86
  19.2 9.4 %all-to-all-done.mine_ref = bf16[16,4,64,128]{3,2,1,0:T(8,128)(2,1)S(1)} async-done(((bf16[16,4,64,128]{3,2,1,0:T(8,128)(2,1)}), bf16[16,4,64,128]{3,2,1,0:T(8,128)(2,1)S(1)}, u32[]{:S(2)}, u32[]{:S(2)}) %all-to-all-start) | async-done | bytes 1048608 | tf_op jit(solution)/shard_map/all_to_all | solution.py:86
  28.5 6.5 %all-to-all-start.1 = ((bf16[128,2,2304]{2,1,0:T(2,128)(2,1)}), bf16[128,2,2304]{2,1,0:T(2,128)(2,1)S(1)}, u32[]{:S(2)}, u32[]{:S(2)}) async-start(bf16[128,2,2304]{2,1,0:T(2,128)(2,1)} %reshape.375), calls=%async_computation.1 | async-start | bytes 2359296 | tf_op jit(solution)/shard_map/all_to_all | solution.py:551
  38.8 16.7 %all-to-all-done.1 = bf16[128,2,2304]{2,1,0:T(2,128)(2,1)S(1)} async-done(((bf16[128,2,2304]{2,1,0:T(2,128)(2,1)}), bf16[128,2,2304]{2,1,0:T(2,128)(2,1)S(1)}, u32[]{:S(2)}, u32[]{:S(2)}) %all-to-all-start.1) | async-done | bytes 1179680 | tf_op jit(solution)/shard_map/all_to_all | solution.py:551
  57.4 2.8 fusion.44
  69.6 19.3 %collective-permute-done.9.g_ref.refs_5_ = bf16[256,1024]{1,0:T(8,128)(2,1)S(1)} collective-permute-done((bf16[256,1024]{1,0:T(8,128)(2,1)S(1)}, bf16[256,1024]{1,0:T(8,128)(2,1)S(1)}, u32[]{:S(2)}, u32[]{:S(2)}) %collective-permute-start.9) | collective-permute-done | bytes 524320 | tf_op jit(solution)/shard_map/ppermute | solution.py:59
  91.9 5.9 %shard_map.196.w_ref = bf16[4,1024,256]{2,1,0:T(8,128)(2,1)} custom-call(s32[1]{0:T(128)} %bitcast.4.core_ref, bf16[16,4,64,128]{3,2,1,0:T(8,128)(2,1)} %copy-done.43, bf16[16,4,64,128]{3,2,1,0:T(8,128)(2,1)} %collective-permute-done.4.other_ref), custom_call_target="tpu_custom_call" | custom-call | bytes 4194304 | tf_op jit(solution)/shard_map/pallas_call | solution.py:101
  99.9 4.5 all-to-all-start.2
  104.5 3.2 collective-permute-start.1
  113.3 2.8 collective-permute-done.3
  120.3 7.0 %shard_map.197 = (bf16[3,1024,128]{2,1,0:T(8,128)(2,1)S(1)}, bf16[3,1024,128]{2,1,0:T(8,128)(2,1)S(1)}, f32[2,1024,256]{2,1,0:T(8,128)S(1)}) custom-call(s32[1]{0:T(128)} %bitcast.4.core_ref, bf16[1024,1152]{1,0:T(8,128)(2,1)} %constant_dynamic-update-slice_fusion.a_ref.facts_ref.refs_0_, bf16[4,1024,256]{2,1,0:T(8,128)(2,1)S(1)} %copy-done, ...), custom_call_target="tpu_custom_call" | custom-call | flops 2147483648 | bytes 8388608 | tf_op jit(solution)/shard_map/pallas_call | solution.py:225
  130.8 11.6 %shard_map.198 = (f32[2048,128]{1,0:T(8,128)S(1)}, bf16[2048,128]{1,0:T(8,128)(2,1)S(1)}, bf16[2048,128]{1,0:T(8,128)(2,1)S(1)}) custom-call(bf16[3,2048,128]{2,1,0:T(8,128)(2,1)S(1)} %constant_dynamic-update-slice_fusion.5.qkv_ref.all_ref, bf16[3,2048,128]{2,1,0:T(8,128)(2,1)S(1)} %constant_dynamic-update-slice_fusion.5.qkv_ref.all_ref, ...), custom_call_target="tpu_custom_call" | custom-call | flops 8589934592 | bytes 6291456 | tf_op jit(solution)/shard_map/pallas_call | solution.py:351
  155.4 11.1 %collective-permute-done.14 = bf16[256,1024]{1,0:T(8,128)(2,1)S(1)} collective-permute-done((bf16[256,1024]{1,0:T(8,128)(2,1)}, bf16[256,1024]{1,0:T(8,128)(2,1)S(1)}, u32[]{:S(2)}, u32[]{:S(2)}) %collective-permute-start.14) | collective-permute-done | bytes 524320 | tf_op jit(solution)/shard_map/ppermute | solution.py:59
  166.5 10.6 %collective-permute-done.15 = bf16[256,1024]{1,0:T(8,128)(2,1)} collective-permute-done((bf16[256,1024]{1,0:T(8,128)(2,1)}, bf16[256,1024]{1,0:T(8,128)(2,1)}, u32[]{:S(2)}, u32[]{:S(2)}) %collective-permute-start.15) | collective-permute-done | bytes 524320 | tf_op jit(solution)/shard_map/ppermute | solution.py:59
  184.0 10.7 %collective-permute-done.18.b_ref.refs_1_ = bf16[256,1024]{1,0:T(8,128)(2,1)S(1)} collective-permute-done((bf16[256,1024]{1,0:T(8,128)(2,1)S(1)}, bf16[256,1024]{1,0:T(8,128)(2,1)S(1)}, u32[]{:S(2)}, u32[]{:S(2)}) %collective-permute-start.18) | collective-permute-done | bytes 524320 | tf_op jit(solution)/shard_map/ppermute | solution.py:59
  198.0 3.9 collective-permute-done.22
  201.9 3.7 collective-permute-done.23
  206.4 7.8 %shard_map.199.w_ref = bf16[3,1024,1024]{2,1,0:T(8,128)(2,1)} custom-call(s32[1]{0:T(128)} %bitcast.4.core_ref, bf16[16,3,64,512]{3,2,1,0:T(8,128)(2,1)} %all-to-all-done.2.mine_ref, bf16[16,3,64,512]{3,2,1,0:T(8,128)(2,1)} %collective-permute-done.17.other_ref), custom_call_target="tpu_custom_call" | custom-call | bytes 12582912 | tf_op jit(solution)/shard_map/pallas_call | solution.py:101
  216.3 7.0 %shard_map.200 = (bf16[256,1024]{1,0:T(8,128)(2,1)S(1)}, bf16[256,1024]{1,0:T(8,128)(2,1)S(1)}, bf16[3,256,1024]{2,1,0:T(8,128)(2,1)S(1)}) custom-call(bf16[256,1024]{1,0:T(8,128)(2,1)S(1)} %copy-done.15, bf16[256,1024]{1,0:T(8,128)(2,1)S(1)} %copy-done.11, bf16[3,1024,1024]{2,1,0:T(8,128)(2,1)} %shard_map.199.w_ref), custom_call_target="tpu_custom_call" | custom-call | flops 3221225472 | bytes 9961472 | tf_op jit(solution)/shard_map/pallas_call | solution.py:491
  223.3 7.0 %shard_map.202 = (bf16[256,1024]{1,0:T(8,128)(2,1)S(1)}, bf16[256,1024]{1,0:T(8,128)(2,1)S(1)}, bf16[3,256,1024]{2,1,0:T(8,128)(2,1)S(1)}) custom-call(bf16[256,1024]{1,0:T(8,128)(2,1)S(1)} %copy-done.25, bf16[256,1024]{1,0:T(8,128)(2,1)S(1)} %copy-done.21, bf16[3,1024,1024]{2,1,0:T(8,128)(2,1)} %shard_map.199.w_ref), custom_call_target="tpu_custom_call" | custom-call | flops 3221225472 | bytes 9961472 | tf_op jit(solution)/shard_map/pallas_call | solution.py:491
  231.6 7.2 %shard_map.203 = (bf16[256,1024]{1,0:T(8,128)(2,1)S(1)}, bf16[256,1024]{1,0:T(8,128)(2,1)S(1)}, bf16[3,256,1024]{2,1,0:T(8,128)(2,1)S(1)}) custom-call(bf16[256,1024]{1,0:T(8,128)(2,1)S(1)} %copy-done.27, bf16[256,1024]{1,0:T(8,128)(2,1)S(1)} %copy-done.13, bf16[3,1024,1024]{2,1,0:T(8,128)(2,1)} %shard_map.199.w_ref), custom_call_target="tpu_custom_call" | custom-call | flops 3221225472 | bytes 9961472 | tf_op jit(solution)/shard_map/pallas_call | solution.py:491
  241.6 6.9 %shard_map.201 = (bf16[256,1024]{1,0:T(8,128)(2,1)S(1)}, bf16[256,1024]{1,0:T(8,128)(2,1)S(1)}, bf16[3,256,1024]{2,1,0:T(8,128)(2,1)S(1)}) custom-call(bf16[256,1024]{1,0:T(8,128)(2,1)S(1)} %copy-done.23, bf16[256,1024]{1,0:T(8,128)(2,1)S(1)} %copy-done.19, bf16[3,1024,1024]{2,1,0:T(8,128)(2,1)} %shard_map.199.w_ref), custom_call_target="tpu_custom_call" | custom-call | flops 3221225472 | bytes 9961472 | tf_op jit(solution)/shard_map/pallas_call | solution.py:491
  250.7 10.5 %shard_map.205 = bf16[2,8,2,3,64,512]{5,4,3,2,1,0:T(8,128)(2,1)} custom-call(s32[1]{0:T(128)} %bitcast.4.core_ref, bf16[256,1024]{1,0:T(8,128)(2,1)S(1)} %copy-done.16, bf16[256,1024]{1,0:T(8,128)(2,1)S(1)} %copy-done.23, bf16[256,1024]{1,0:T(8,128)(2,1)S(1)} %copy-done.27, bf16[256,1024]{1,0:T(8,128)(2,1)S(1)} %copy-done.25, ...), custom_call_target="tpu_custom_call" | custom-call | flops 6442450944 | bytes 16777216 | tf_op jit(solution)/shard_map/pallas_call | solution.py:153
  261.2 6.5 %fusion.38 = (bf16[1,8,2,3,64,512]{5,4,3,2,1,0:T(8,128)(2,1)}, bf16[1,8,2,3,64,512]{5,4,3,2,1,0:T(8,128)(2,1)}) fusion(bf16[2,8,2,3,64,512]{5,4,3,2,1,0:T(8,128)(2,1)} %shard_map.205), kind=kLoop, calls=%fused_computation.188 | loop fusion | bytes 12582912 | tf_op jit(solution)/shard_map/slice | solution.py:114
  268.3 2.6 constant_dynamic-update-slice_fusion.13
  270.8 2.7 collective-permute-start.25
  273.6 11.8 %collective-permute-done.25 = bf16[256,1024]{1,0:T(8,128)(2,1)S(1)} collective-permute-done((bf16[256,1024]{1,0:T(8,128)(2,1)S(1)}, bf16[256,1024]{1,0:T(8,128)(2,1)S(1)}, u32[]{:S(2)}, u32[]{:S(2)}) %collective-permute-start.25) | collective-permute-done | bytes 524320 | tf_op jit(solution)/shard_map/ppermute | solution.py:59
  285.4 3.8 collective-permute-start.26
  289.7 4.9 collective-permute-done.26
  294.7 3.9 collective-permute-done.28
  300.2 3.2 collective-permute-start.32
  303.5 5.9 %fusion = bf16[16,3,64,512]{3,2,1,0:T(8,128)(2,1)} fusion(bf16[16,3,64,512]{3,2,1,0:T(8,128)(2,1)} %collective-permute-done.34, bf16[1,8,2,3,64,512]{5,4,3,2,1,0:T(8,128)(2,1)} %get-tuple-element.116), kind=kLoop, calls=%fused_computation.1 | loop fusion | flops 6291456 | bytes 9437184 | tf_op jit(solution)/shard_map/convert_element_type | solution.py:114
  309.4 6.5 %all-to-all-start.3 = ((bf16[16,3,64,512]{3,2,1,0:T(8,128)(2,1)}), bf16[16,3,64,512]{3,2,1,0:T(8,128)(2,1)}, u32[]{:S(2)}, u32[]{:S(2)}) async-start(bf16[16,3,64,512]{3,2,1,0:T(8,128)(2,1)} %fusion), calls=%async_computation.3 | async-start | bytes 6291456 | tf_op jit(solution)/shard_map/all_to_all | solution.py:115
  318.2 25.4 %shard_map.204 = (bf16[2048,128]{1,0:T(8,128)(2,1)S(1)}, bf16[2048,128]{1,0:T(8,128)(2,1)S(1)}, bf16[2048,128]{1,0:T(8,128)(2,1)S(1)}, f32[8,128]{1,0:T(8,128)S(1)}) custom-call(bf16[3,2048,128]{2,1,0:T(8,128)(2,1)} %copy-done.17, bf16[3,2048,128]{2,1,0:T(8,128)(2,1)} %copy-done.17, bf16[2048,128]{1,0:T(8,128)(2,1)S(1)} %copy-done.37, ...), custom_call_target="tpu_custom_call" | custom-call | flops 21474836480 | bytes 6291456 | tf_op jit(solution)/shard_map/pallas_call | solution.py:426
  348.8 9.7 %all-to-all-done.3 = bf16[16,3,64,512]{3,2,1,0:T(8,128)(2,1)} async-done(((bf16[16,3,64,512]{3,2,1,0:T(8,128)(2,1)}), bf16[16,3,64,512]{3,2,1,0:T(8,128)(2,1)}, u32[]{:S(2)}, u32[]{:S(2)}) %all-to-all-start.3) | async-done | bytes 3145760 | tf_op jit(solution)/shard_map/all_to_all | solution.py:115
  358.5 3.2 convert_reduce_fusion
  363.1 10.0 %all-to-all-start.4 = ((bf16[128,2,1024]{2,1,0:T(2,128)(2,1)}), bf16[128,2,1024]{2,1,0:T(2,128)(2,1)S(1)}, u32[]{:S(2)}, u32[]{:S(2)}) async-start(bf16[128,2,1024]{2,1,0:T(2,128)(2,1)} %reshape.381), calls=%async_computation.4 | async-start | bytes 1048576 | tf_op jit(solution)/shard_map/all_to_all | solution.py:650
  376.2 10.4 %all-to-all-done.4 = bf16[128,2,1024]{2,1,0:T(2,128)(2,1)S(1)} async-done(((bf16[128,2,1024]{2,1,0:T(2,128)(2,1)}), bf16[128,2,1024]{2,1,0:T(2,128)(2,1)S(1)}, u32[]{:S(2)}, u32[]{:S(2)}) %all-to-all-start.4) | async-done | bytes 524320 | tf_op jit(solution)/shard_map/all_to_all | solution.py:650
  388.5 8.6 %shard_map.206 = (bf16[3,1024,256]{2,1,0:T(8,128)(2,1)S(1)}, bf16[1024,1024]{1,0:T(8,128)(2,1)S(1)}, f32[8,256]{1,0:T(8,128)S(1)}) custom-call(s32[1]{0:T(128)} %bitcast.4.core_ref, bf16[3,1024,128]{2,1,0:T(8,128)(2,1)S(1)} %pad_maximum_fusion.1.mine_ref, bf16[3,1024,128]{2,1,0:T(8,128)(2,1)S(1)} %copy-done.5, f32[2,1024,256]{2,1,0:T(8,128)} %copy-done.3, ...), custom_call_target="tpu_custom_call" | custom-call | flops 2147483648 | bytes 8388608 | tf_op jit(solution)/shard_map/pallas_call | solution.py:278
  399.5 8.7 %shard_map.207 = bf16[2,8,2,4,64,128]{5,4,3,2,1,0:T(8,128)(2,1)S(1)} custom-call(s32[1]{0:T(128)} %bitcast.4.core_ref, bf16[1024,1152]{1,0:T(8,128)(2,1)} %constant_dynamic-update-slice_fusion.a_ref.facts_ref.refs_0_, bf16[1024,1024]{1,0:T(8,128)(2,1)S(1)} %copy-done.2, bf16[4,1024,256]{2,1,0:T(8,128)(2,1)} %pad_maximum_fusion.refs_2_), custom_call_target="tpu_custom_call" | custom-call | flops 2147483648 | bytes 8388608 | tf_op jit(solution)/shard_map/pallas_call | solution.py:153
  411.2 3.2 collective-permute-start.36
  416.1 22.1 %collective-permute-done.35 = bf16[256,1024]{1,0:T(8,128)(2,1)} collective-permute-done((bf16[256,1024]{1,0:T(8,128)(2,1)}, bf16[256,1024]{1,0:T(8,128)(2,1)}, u32[]{:S(2)}, u32[]{:S(2)}) %collective-permute-start.35) | collective-permute-done | bytes 524320 | tf_op jit(solution)/shard_map/ppermute | solution.py:59
  440.5 2.7 fusion.1
  443.2 3.9 all-to-all-start.5
  447.0 3.5 convolution_convert_fusion.4
  453.8 11.1 %all-to-all-done.5 = bf16[16,4,64,128]{3,2,1,0:T(8,128)(2,1)S(1)} async-done(((bf16[16,4,64,128]{3,2,1,0:T(8,128)(2,1)}), bf16[16,4,64,128]{3,2,1,0:T(8,128)(2,1)S(1)}, u32[]{:S(2)}, u32[]{:S(2)}) %all-to-all-start.5) | async-done | bytes 1048608 | tf_op jit(solution)/shard_map/all_to_all | solution.py:115
  465.1 5.7 %all-to-all-start.6 = ((bf16[128,2,1408]{2,1,0:T(2,128)(2,1)}), bf16[128,2,1408]{2,1,0:T(2,128)(2,1)S(1)}, u32[]{:S(2)}, u32[]{:S(2)}) async-start(bf16[128,2,1408]{2,1,0:T(2,128)(2,1)} %pad_maximum_fusion.3), calls=%async_computation.6 | async-start | bytes 1441792 | tf_op jit(solution)/shard_map/all_to_all | solution.py:689
  473.5 13.0 %all-to-all-done.6 = bf16[128,2,1408]{2,1,0:T(2,128)(2,1)S(1)} async-done(((bf16[128,2,1408]{2,1,0:T(2,128)(2,1)}), bf16[128,2,1408]{2,1,0:T(2,128)(2,1)S(1)}, u32[]{:S(2)}, u32[]{:S(2)}) %all-to-all-start.6) | async-done | bytes 720928 | tf_op jit(solution)/shard_map/all_to_all | solution.py:689
  (361 shorter events, 111.7 us)
Async XLA Ops:
  2.9 25.7 %all-to-all-start = ((bf16[16,4,64,128]{3,2,1,0:T(8,128)(2,1)}), bf16[16,4,64,128]{3,2,1,0:T(8,128)(2,1)S(1)}, u32[]{:S(2)}, u32[]{:S(2)}) async-start(bf16[16,4,64,128]{3,2,1,0:T(8,128)(2,1)} %broadcast_in_dim.168), calls=%async_computation | async-start | bytes 2097152 | tf_op jit(solution)/shard_map/all_to_all | solution.py:86
  10.8 27.3 %collective-permute-start.8 = (f32[2,2]{1,0:T(2,128)}, f32[2,2]{1,0:T(2,128)}, u32[]{:S(2)}, u32[]{:S(2)}) collective-permute-start(f32[2,2]{1,0:T(2,128)} %param.25), channel_id=1, source_target_pairs={{0,1},{1,0},{2,3},{3,2},{4,5},{5,4},{6,7},{7,6},{8,9},{9,8},{10,11... | collective-permute-start | bytes 56 | tf_op jit(solution)/shard_map/ppermute | solution.py:560
  12.7 54.7 %collective-permute-start.7 = (s32[1,4]{1,0:T(1,128)}, s32[1,4]{1,0:T(1,128)}, u32[]{:S(2)}, u32[]{:S(2)}) collective-permute-start(s32[1,4]{1,0:T(1,128)} %param.18), channel_id=1, source_target_pairs={{0,8},{8,0},{1,9},{9,1},{2,10},{10,2},{3,11},{11,3},{4,12},{12,4},... | collective-permute-start | bytes 56 | tf_op jit(solution)/shard_map/ppermute | solution.py:63
  28.5 27.0 %all-to-all-start.1 = ((bf16[128,2,2304]{2,1,0:T(2,128)(2,1)}), bf16[128,2,2304]{2,1,0:T(2,128)(2,1)S(1)}, u32[]{:S(2)}, u32[]{:S(2)}) async-start(bf16[128,2,2304]{2,1,0:T(2,128)(2,1)} %reshape.375), calls=%async_computation.1 | async-start | bytes 2359296 | tf_op jit(solution)/shard_map/all_to_all | solution.py:551
  38.8 53.1 %collective-permute-start.4 = (bf16[16,4,64,128]{3,2,1,0:T(8,128)(2,1)}, bf16[16,4,64,128]{3,2,1,0:T(8,128)(2,1)}, u32[]{:S(2)}, u32[]{:S(2)}) collective-permute-start(bf16[16,4,64,128]{3,2,1,0:T(8,128)(2,1)} %copy-done.43), channel_id=1, source_target_pairs={{0,8},{8,0},{1,9},{9,1},{2,10},{10,2},{3,11},{11,3},{4,12},{12,4},... | collective-permute-start | bytes 3145736 | tf_op jit(solution)/shard_map/ppermute | solution.py:63
  62.8 41.6 %collective-permute-start = (bf16[256,1152]{1,0:T(8,128)(2,1)}, bf16[256,1152]{1,0:T(8,128)(2,1)S(1)}, u32[]{:S(2)}, u32[]{:S(2)}) collective-permute-start(bf16[256,1152]{1,0:T(8,128)(2,1)} %get-tuple-element.128), channel_id=1, source_target_pairs={{0,6},{2,0},{4,2},{6,4},{1,7},{3,1},{5,3},{7,5},{8,14},{10,8},{12,... | collective-permute-start | bytes 1769480 | tf_op jit(solution)/shard_map/ppermute | solution.py:59
  63.0 44.7 %collective-permute-start.2 = (bf16[256,1152]{1,0:T(8,128)(2,1)}, bf16[256,1152]{1,0:T(8,128)(2,1)S(1)}, u32[]{:S(2)}, u32[]{:S(2)}) collective-permute-start(bf16[256,1152]{1,0:T(8,128)(2,1)} %get-tuple-element.128), channel_id=1, source_target_pairs={{0,2},{2,4},{4,6},{6,0},{1,3},{3,5},{5,7},{7,1},{8,10},{10,12},{12... | collective-permute-start | bytes 1769480 | tf_op jit(solution)/shard_map/ppermute | solution.py:59
  65.9 31.9 %copy-start.10 = (bf16[256,1024]{1,0:T(8,128)(2,1)}, bf16[256,1024]{1,0:T(8,128)(2,1)S(1)}, u32[]{:S(2)}) copy-start(bf16[256,1024]{1,0:T(8,128)(2,1)S(1)} %slice.264.g_ref.refs_4_) | copy-start | bytes 1572868
  65.9 22.9 %collective-permute-start.9 = (bf16[256,1024]{1,0:T(8,128)(2,1)S(1)}, bf16[256,1024]{1,0:T(8,128)(2,1)S(1)}, u32[]{:S(2)}, u32[]{:S(2)}) collective-permute-start(bf16[256,1024]{1,0:T(8,128)(2,1)S(1)} %slice.264.g_ref.refs_4_), channel_id=1, source_target_pairs={{0,6},{2,0},{4,2},{6,4},{1,7},{3,1},{5,3},{7,5},{8,14},{10,8},{12,... | collective-permute-start | bytes 1572872 | tf_op jit(solution)/shard_map/ppermute | solution.py:59
  67.4 23.5 %collective-permute-start.11 = (bf16[256,1024]{1,0:T(8,128)(2,1)S(1)}, bf16[256,1024]{1,0:T(8,128)(2,1)S(1)}, u32[]{:S(2)}, u32[]{:S(2)}) collective-permute-start(bf16[256,1024]{1,0:T(8,128)(2,1)S(1)} %slice.264.g_ref.refs_4_), channel_id=1, source_target_pairs={{0,2},{2,4},{4,6},{6,0},{1,3},{3,5},{5,7},{7,1},{8,10},{10,12},{12... | collective-permute-start | bytes 1572872 | tf_op jit(solution)/shard_map/ppermute | solution.py:59
  88.9 20.5 %collective-permute-start.10 = (bf16[128,1024]{1,0:T(8,128)(2,1)S(1)}, bf16[128,1024]{1,0:T(8,128)(2,1)}, u32[]{:S(2)}, u32[]{:S(2)}) collective-permute-start(bf16[128,1024]{1,0:T(8,128)(2,1)S(1)} %slice.272), channel_id=1, source_target_pairs={{0,6},{2,0},{4,2},{6,4},{1,7},{3,1},{5,3},{7,5},{8,14},{10,8},{12,... | collective-permute-start | bytes 786440 | tf_op jit(solution)/shard_map/ppermute | solution.py:59
  91.6 17.8 %collective-permute-start.12 = (bf16[128,1024]{1,0:T(8,128)(2,1)}, bf16[128,1024]{1,0:T(8,128)(2,1)}, u32[]{:S(2)}, u32[]{:S(2)}) collective-permute-start(bf16[128,1024]{1,0:T(8,128)(2,1)} %slice.273), channel_id=1, source_target_pairs={{0,2},{2,4},{4,6},{6,0},{1,3},{3,5},{5,7},{7,1},{8,10},{10,12},{12... | collective-permute-start | bytes 786440 | tf_op jit(solution)/shard_map/ppermute | solution.py:59
  99.9 46.4 %all-to-all-start.2 = ((bf16[16,3,64,512]{3,2,1,0:T(8,128)(2,1)}), bf16[16,3,64,512]{3,2,1,0:T(8,128)(2,1)}, u32[]{:S(2)}, u32[]{:S(2)}) async-start(bf16[16,3,64,512]{3,2,1,0:T(8,128)(2,1)} %broadcast_in_dim.180), calls=%async_computation.2 | async-start | bytes 6291456 | tf_op jit(solution)/shard_map/all_to_all | solution.py:86
  104.5 8.1 %collective-permute-start.1 = (bf16[128,1152]{1,0:T(8,128)(2,1)S(1)}, bf16[128,1152]{1,0:T(8,128)(2,1)S(1)}, u32[]{:S(2)}, u32[]{:S(2)}) collective-permute-start(bf16[128,1152]{1,0:T(8,128)(2,1)S(1)} %slice.269), channel_id=1, source_target_pairs={{0,6},{2,0},{4,2},{6,4},{1,7},{3,1},{5,3},{7,5},{8,14},{10,8},{12,... | collective-permute-start | bytes 884744 | tf_op jit(solution)/shard_map/ppermute | solution.py:59
  107.7 8.4 %collective-permute-start.3 = (bf16[128,1152]{1,0:T(8,128)(2,1)S(1)}, bf16[128,1152]{1,0:T(8,128)(2,1)S(1)}, u32[]{:S(2)}, u32[]{:S(2)}) collective-permute-start(bf16[128,1152]{1,0:T(8,128)(2,1)S(1)} %slice.270), channel_id=1, source_target_pairs={{0,2},{2,4},{4,6},{6,0},{1,3},{3,5},{5,7},{7,1},{8,10},{10,12},{12... | collective-permute-start | bytes 884744 | tf_op jit(solution)/shard_map/ppermute | solution.py:59
  120.0 8.0 %collective-permute-start.6 = (s32[1024]{0:T(1024)S(1)}, s32[1024]{0:T(1024)S(1)}, u32[]{:S(2)}, u32[]{:S(2)}) collective-permute-start(s32[1024]{0:T(1024)S(1)} %convert_reduce_fusion.2), channel_id=1, source_target_pairs={{0,8},{8,0},{1,9},{9,1},{2,10},{10,2},{3,11},{11,3},{4,12},{12,4},... | collective-permute-start | bytes 12296 | tf_op jit(solution)/shard_map/ppermute | solution.py:63
  127.4 3.1 collective-permute-start.5
  144.2 2.1 collective-permute-start.13
  146.4 60.0 %collective-permute-start.17 = (bf16[16,3,64,512]{3,2,1,0:T(8,128)(2,1)}, bf16[16,3,64,512]{3,2,1,0:T(8,128)(2,1)}, u32[]{:S(2)}, u32[]{:S(2)}) collective-permute-start(bf16[16,3,64,512]{3,2,1,0:T(8,128)(2,1)} %all-to-all-done.2.mine_ref), channel_id=1, source_target_pairs={{0,8},{8,0},{1,9},{9,1},{2,10},{10,2},{3,11},{11,3},{4,12},{12,4},... | collective-permute-start | bytes 9437192 | tf_op jit(solution)/shard_map/ppermute | solution.py:63
  150.7 15.8 %collective-permute-start.14 = (bf16[256,1024]{1,0:T(8,128)(2,1)}, bf16[256,1024]{1,0:T(8,128)(2,1)S(1)}, u32[]{:S(2)}, u32[]{:S(2)}) collective-permute-start(bf16[256,1024]{1,0:T(8,128)(2,1)} %get-tuple-element.123), channel_id=1, source_target_pairs={{0,2},{2,4},{4,6},{6,0},{1,3},{3,5},{5,7},{7,1},{8,10},{10,12},{12... | collective-permute-start | bytes 1572872 | tf_op jit(solution)/shard_map/ppermute | solution.py:59
  151.7 25.4 %collective-permute-start.15 = (bf16[256,1024]{1,0:T(8,128)(2,1)}, bf16[256,1024]{1,0:T(8,128)(2,1)}, u32[]{:S(2)}, u32[]{:S(2)}) collective-permute-start(bf16[256,1024]{1,0:T(8,128)(2,1)} %get-tuple-element.125), channel_id=1, source_target_pairs={{0,6},{2,0},{4,2},{6,4},{1,7},{3,1},{5,3},{7,5},{8,14},{10,8},{12,... | collective-permute-start | bytes 1572872 | tf_op jit(solution)/shard_map/ppermute | solution.py:59
  153.9 24.8 %collective-permute-start.16 = (bf16[256,1024]{1,0:T(8,128)(2,1)}, bf16[256,1024]{1,0:T(8,128)(2,1)}, u32[]{:S(2)}, u32[]{:S(2)}) collective-permute-start(bf16[256,1024]{1,0:T(8,128)(2,1)} %get-tuple-element.124), channel_id=1, source_target_pairs={{0,4},{2,6},{4,0},{6,2},{1,5},{3,7},{5,1},{7,3},{8,12},{10,14},{12... | collective-permute-start | bytes 1572872 | tf_op jit(solution)/shard_map/ppermute | solution.py:59
  181.1 13.6 %collective-permute-start.18 = (bf16[256,1024]{1,0:T(8,128)(2,1)S(1)}, bf16[256,1024]{1,0:T(8,128)(2,1)S(1)}, u32[]{:S(2)}, u32[]{:S(2)}) collective-permute-start(bf16[256,1024]{1,0:T(8,128)(2,1)S(1)} %multiply_convert_fusion.b_ref.refs_0_), channel_id=1, source_target_pairs={{0,6},{2,0},{4,2},{6,4},{1,7},{3,1},{5,3},{7,5},{8,14},{10,8},{12,... | collective-permute-start | bytes 1572872 | tf_op jit(solution)/shard_map/ppermute | solution.py:59
  183.1 13.8 %collective-permute-start.20 = (bf16[256,1024]{1,0:T(8,128)(2,1)S(1)}, bf16[256,1024]{1,0:T(8,128)(2,1)S(1)}, u32[]{:S(2)}, u32[]{:S(2)}) collective-permute-start(bf16[256,1024]{1,0:T(8,128)(2,1)S(1)} %multiply_convert_fusion.b_ref.refs_0_), channel_id=1, source_target_pairs={{0,2},{2,4},{4,6},{6,0},{1,3},{3,5},{5,7},{7,1},{8,10},{10,12},{12... | collective-permute-start | bytes 1572872 | tf_op jit(solution)/shard_map/ppermute | solution.py:59
  194.7 7.1 %collective-permute-start.22 = (bf16[128,1024]{1,0:T(8,128)(2,1)S(1)}, bf16[128,1024]{1,0:T(8,128)(2,1)S(1)}, u32[]{:S(2)}, u32[]{:S(2)}) collective-permute-start(bf16[128,1024]{1,0:T(8,128)(2,1)S(1)} %slice.280), channel_id=1, source_target_pairs={{0,6},{2,0},{4,2},{6,4},{1,7},{3,1},{5,3},{7,5},{8,14},{10,8},{12,... | collective-permute-start | bytes 786440 | tf_op jit(solution)/shard_map/ppermute | solution.py:59
  197.7 7.8 %collective-permute-start.23 = (bf16[128,1024]{1,0:T(8,128)(2,1)S(1)}, bf16[128,1024]{1,0:T(8,128)(2,1)S(1)}, u32[]{:S(2)}, u32[]{:S(2)}) collective-permute-start(bf16[128,1024]{1,0:T(8,128)(2,1)S(1)} %slice.281), channel_id=1, source_target_pairs={{0,2},{2,4},{4,6},{6,0},{1,3},{3,5},{5,7},{7,1},{8,10},{10,12},{12... | collective-permute-start | bytes 786440 | tf_op jit(solution)/shard_map/ppermute | solution.py:59
  231.5 36.1 %collective-permute-start.21 = (bf16[256,1024]{1,0:T(8,128)(2,1)S(1)}, bf16[256,1024]{1,0:T(8,128)(2,1)S(1)}, u32[]{:S(2)}, u32[]{:S(2)}) collective-permute-start(bf16[256,1024]{1,0:T(8,128)(2,1)S(1)} %get-tuple-element.69), channel_id=1, source_target_pairs={{0,6},{2,0},{4,2},{6,4},{1,7},{3,1},{5,3},{7,5},{8,14},{10,8},{12,... | collective-permute-start | bytes 1572872 | tf_op jit(solution)/shard_map/ppermute | solution.py:59
  240.7 26.9 %collective-permute-start.24 = (bf16[256,1024]{1,0:T(8,128)(2,1)S(1)}, bf16[256,1024]{1,0:T(8,128)(2,1)S(1)}, u32[]{:S(2)}, u32[]{:S(2)}) collective-permute-start(bf16[256,1024]{1,0:T(8,128)(2,1)S(1)} %get-tuple-element.71), channel_id=1, source_target_pairs={{0,4},{2,6},{4,0},{6,2},{1,5},{3,7},{5,1},{7,3},{8,12},{10,14},{12... | collective-permute-start | bytes 1572872 | tf_op jit(solution)/shard_map/ppermute | solution.py:59
  249.7 18.0 %collective-permute-start.19 = (bf16[256,1024]{1,0:T(8,128)(2,1)S(1)}, bf16[256,1024]{1,0:T(8,128)(2,1)S(1)}, u32[]{:S(2)}, u32[]{:S(2)}) collective-permute-start(bf16[256,1024]{1,0:T(8,128)(2,1)S(1)} %get-tuple-element.67), channel_id=1, source_target_pairs={{0,2},{2,4},{4,6},{6,0},{1,3},{3,5},{5,7},{7,1},{8,10},{10,12},{12... | collective-permute-start | bytes 1572872 | tf_op jit(solution)/shard_map/ppermute | solution.py:59
  267.7 35.9 %collective-permute-start.34 = (bf16[16,3,64,512]{3,2,1,0:T(8,128)(2,1)}, bf16[16,3,64,512]{3,2,1,0:T(8,128)(2,1)}, u32[]{:S(2)}, u32[]{:S(2)}) collective-permute-start(bf16[16,3,64,512]{3,2,1,0:T(8,128)(2,1)} %bitcast.22), channel_id=1, source_target_pairs={{0,8},{8,0},{1,9},{9,1},{2,10},{10,2},{3,11},{11,3},{4,12},{12,4},... | collective-permute-start | bytes 9437192 | tf_op jit(solution)/shard_map/ppermute | solution.py:63
  270.8 14.6 %collective-permute-start.25 = (bf16[256,1024]{1,0:T(8,128)(2,1)S(1)}, bf16[256,1024]{1,0:T(8,128)(2,1)S(1)}, u32[]{:S(2)}, u32[]{:S(2)}) collective-permute-start(bf16[256,1024]{1,0:T(8,128)(2,1)S(1)} %get-tuple-element.110), channel_id=1, source_target_pairs={{0,6},{2,0},{4,2},{6,4},{1,7},{3,1},{5,3},{7,5},{8,14},{10,8},{12,... | collective-permute-start | bytes 1572872 | tf_op jit(solution)/shard_map/ppermute | solution.py:59
  273.6 15.6 %collective-permute-start.27 = (bf16[256,1024]{1,0:T(8,128)(2,1)S(1)}, bf16[256,1024]{1,0:T(8,128)(2,1)S(1)}, u32[]{:S(2)}, u32[]{:S(2)}) collective-permute-start(bf16[256,1024]{1,0:T(8,128)(2,1)S(1)} %get-tuple-element.110), channel_id=1, source_target_pairs={{0,2},{2,4},{4,6},{6,0},{1,3},{3,5},{5,7},{7,1},{8,10},{10,12},{12... | collective-permute-start | bytes 1572872 | tf_op jit(solution)/shard_map/ppermute | solution.py:59
  285.4 9.2 %collective-permute-start.26 = (bf16[128,1024]{1,0:T(8,128)(2,1)S(1)}, bf16[128,1024]{1,0:T(8,128)(2,1)S(1)}, u32[]{:S(2)}, u32[]{:S(2)}) collective-permute-start(bf16[128,1024]{1,0:T(8,128)(2,1)S(1)} %slice.282), channel_id=1, source_target_pairs={{0,6},{2,0},{4,2},{6,4},{1,7},{3,1},{5,3},{7,5},{8,14},{10,8},{12,... | collective-permute-start | bytes 786440 | tf_op jit(solution)/shard_map/ppermute | solution.py:59
  289.2 9.3 %collective-permute-start.28 = (bf16[128,1024]{1,0:T(8,128)(2,1)S(1)}, bf16[128,1024]{1,0:T(8,128)(2,1)S(1)}, u32[]{:S(2)}, u32[]{:S(2)}) collective-permute-start(bf16[128,1024]{1,0:T(8,128)(2,1)S(1)} %slice.283), channel_id=1, source_target_pairs={{0,2},{2,4},{4,6},{6,0},{1,3},{3,5},{5,7},{7,1},{8,10},{10,12},{12... | collective-permute-start | bytes 786440 | tf_op jit(solution)/shard_map/ppermute | solution.py:59
  300.0 3.5 collective-permute-start.29
  300.2 46.8 %collective-permute-start.31 = (bf16[256,1024]{1,0:T(8,128)(2,1)}, bf16[256,1024]{1,0:T(8,128)(2,1)}, u32[]{:S(2)}, u32[]{:S(2)}) collective-permute-start(bf16[256,1024]{1,0:T(8,128)(2,1)} %copy-done.30), channel_id=1, source_target_pairs={{0,2},{2,4},{4,6},{6,0},{1,3},{3,5},{5,7},{7,1},{8,10},{10,12},{12... | collective-permute-start | bytes 1572872 | tf_op jit(solution)/shard_map/ppermute | solution.py:59
  300.2 46.8 %collective-permute-start.32 = (bf16[256,1024]{1,0:T(8,128)(2,1)}, bf16[256,1024]{1,0:T(8,128)(2,1)}, u32[]{:S(2)}, u32[]{:S(2)}) collective-permute-start(bf16[256,1024]{1,0:T(8,128)(2,1)} %copy-done.28), channel_id=1, source_target_pairs={{0,6},{2,0},{4,2},{6,4},{1,7},{3,1},{5,3},{7,5},{8,14},{10,8},{12,... | collective-permute-start | bytes 1572872 | tf_op jit(solution)/shard_map/ppermute | solution.py:59
  303.5 43.5 %collective-permute-start.33 = (bf16[256,1024]{1,0:T(8,128)(2,1)}, bf16[256,1024]{1,0:T(8,128)(2,1)}, u32[]{:S(2)}, u32[]{:S(2)}) collective-permute-start(bf16[256,1024]{1,0:T(8,128)(2,1)} %copy-done.29), channel_id=1, source_target_pairs={{0,4},{2,6},{4,0},{6,2},{1,5},{3,7},{5,1},{7,3},{8,12},{10,14},{12... | collective-permute-start | bytes 1572872 | tf_op jit(solution)/shard_map/ppermute | solution.py:59
  309.4 49.1 %all-to-all-start.3 = ((bf16[16,3,64,512]{3,2,1,0:T(8,128)(2,1)}), bf16[16,3,64,512]{3,2,1,0:T(8,128)(2,1)}, u32[]{:S(2)}, u32[]{:S(2)}) async-start(bf16[16,3,64,512]{3,2,1,0:T(8,128)(2,1)} %fusion), calls=%async_computation.3 | async-start | bytes 6291456 | tf_op jit(solution)/shard_map/all_to_all | solution.py:115
  346.8 28.5 %collective-permute-start.30 = (bf16[3,1024,128]{2,1,0:T(8,128)(2,1)}, bf16[3,1024,128]{2,1,0:T(8,128)(2,1)S(1)}, u32[]{:S(2)}, u32[]{:S(2)}) collective-permute-start(bf16[3,1024,128]{2,1,0:T(8,128)(2,1)} %pad_maximum_fusion.2), channel_id=1, source_target_pairs={{0,8},{8,0},{1,9},{9,1},{2,10},{10,2},{3,11},{11,3},{4,12},{12,4},... | collective-permute-start | bytes 2359304 | tf_op jit(solution)/shard_map/ppermute | solution.py:63
  363.1 23.5 %all-to-all-start.4 = ((bf16[128,2,1024]{2,1,0:T(2,128)(2,1)}), bf16[128,2,1024]{2,1,0:T(2,128)(2,1)S(1)}, u32[]{:S(2)}, u32[]{:S(2)}) async-start(bf16[128,2,1024]{2,1,0:T(2,128)(2,1)} %reshape.381), calls=%async_computation.4 | async-start | bytes 1048576 | tf_op jit(solution)/shard_map/all_to_all | solution.py:650
  409.9 30.6 %collective-permute-start.38 = (bf16[16,4,64,128]{3,2,1,0:T(8,128)(2,1)}, bf16[16,4,64,128]{3,2,1,0:T(8,128)(2,1)}, u32[]{:S(2)}, u32[]{:S(2)}) collective-permute-start(bf16[16,4,64,128]{3,2,1,0:T(8,128)(2,1)} %bitcast.27), channel_id=1, source_target_pairs={{0,8},{8,0},{1,9},{9,1},{2,10},{10,2},{3,11},{11,3},{4,12},{12,4},... | collective-permute-start | bytes 3145736 | tf_op jit(solution)/shard_map/ppermute | solution.py:63
  411.2 27.1 %collective-permute-start.35 = (bf16[256,1024]{1,0:T(8,128)(2,1)}, bf16[256,1024]{1,0:T(8,128)(2,1)}, u32[]{:S(2)}, u32[]{:S(2)}) collective-permute-start(bf16[256,1024]{1,0:T(8,128)(2,1)} %get-tuple-element.120), channel_id=1, source_target_pairs={{0,2},{2,4},{4,6},{6,0},{1,3},{3,5},{5,7},{7,1},{8,10},{10,12},{12... | collective-permute-start | bytes 1572872 | tf_op jit(solution)/shard_map/ppermute | solution.py:59
  411.2 27.1 %collective-permute-start.36 = (bf16[256,1024]{1,0:T(8,128)(2,1)}, bf16[256,1024]{1,0:T(8,128)(2,1)}, u32[]{:S(2)}, u32[]{:S(2)}) collective-permute-start(bf16[256,1024]{1,0:T(8,128)(2,1)} %get-tuple-element.122), channel_id=1, source_target_pairs={{0,6},{2,0},{4,2},{6,4},{1,7},{3,1},{5,3},{7,5},{8,14},{10,8},{12,... | collective-permute-start | bytes 1572872 | tf_op jit(solution)/shard_map/ppermute | solution.py:59
  414.4 23.9 %collective-permute-start.37 = (bf16[256,1024]{1,0:T(8,128)(2,1)}, bf16[256,1024]{1,0:T(8,128)(2,1)}, u32[]{:S(2)}, u32[]{:S(2)}) collective-permute-start(bf16[256,1024]{1,0:T(8,128)(2,1)} %get-tuple-element.121), channel_id=1, source_target_pairs={{0,4},{2,6},{4,0},{6,2},{1,5},{3,7},{5,1},{7,3},{8,12},{10,14},{12... | collective-permute-start | bytes 1572872 | tf_op jit(solution)/shard_map/ppermute | solution.py:59
  415.0 25.5 %copy-start.44 = (bf16[1,8,2,4,64,128]{5,4,3,2,1,0:T(8,128)(2,1)S(1)}, bf16[1,8,2,4,64,128]{5,4,3,2,1,0:T(8,128)(2,1)}, u32[]{:S(2)}) copy-start(bf16[1,8,2,4,64,128]{5,4,3,2,1,0:T(8,128)(2,1)} %get-tuple-element.118) | copy-start | bytes 3145732
  443.2 21.8 %all-to-all-start.5 = ((bf16[16,4,64,128]{3,2,1,0:T(8,128)(2,1)}), bf16[16,4,64,128]{3,2,1,0:T(8,128)(2,1)S(1)}, u32[]{:S(2)}, u32[]{:S(2)}) async-start(bf16[16,4,64,128]{3,2,1,0:T(8,128)(2,1)} %fusion.1), calls=%async_computation.5 | async-start | bytes 2097152 | tf_op jit(solution)/shard_map/all_to_all | solution.py:115
  465.1 21.3 %all-to-all-start.6 = ((bf16[128,2,1408]{2,1,0:T(2,128)(2,1)}), bf16[128,2,1408]{2,1,0:T(2,128)(2,1)S(1)}, u32[]{:S(2)}, u32[]{:S(2)}) async-start(bf16[128,2,1408]{2,1,0:T(2,128)(2,1)} %pad_maximum_fusion.3), calls=%async_computation.6 | async-start | bytes 1441792 | tf_op jit(solution)/shard_map/all_to_all | solution.py:689
  (67 other events, 473.2 us)
